TPU v7x, 32 devices: a whole 2x2x4 slice. The times are simulated.
32 devices in a mesh: dp: 2 (over x), tensor: 4 (over z), section: 4 (over y, core).
Axes of the slice: x: 2, y: 2, z: 4, core: 2. Of those that a mesh axis runs over, the one named last changes fastest.
Arguments:
- grad_parts: bfloat16 [4, 2, 4, 1024, 1024], P('section', 'dp', None, None, 'tensor'), may hold values from -1.5 to 1.5
- first_moment: float32 [4, 4, 1024, 1024], P('section', 'tensor', 'dp'), may hold values from -3 to 3
- second_moment: float32 [4, 4, 1024, 1024], P('section', 'tensor', 'dp'), may hold values from 0.1 to 4
- left_stat: float32 [4, 4, 1024, 1024], P('section', 'tensor', 'dp'), may hold values from -12288 to 184320
- right_stat: float32 [4, 4, 1024, 1024], P('section', 'tensor', 'dp'), may hold values from -12288 to 184320
- left_basis: float32 [4, 4, 1024, 1024], P('section', 'tensor', 'dp'), may hold values from -0.1875 to 0.1875
- right_basis: float32 [4, 4, 1024, 1024], P('section', 'tensor', 'dp'), may hold values from -0.1875 to 0.1875
- gain_grads: float32 [4, 2, 4, 2, 1024], P('section', 'dp', 'tensor'), may hold values from -1.2 to 1.2
- gain_first: float32 [4, 2, 1024], P('section'), may hold values from -3 to 3
- gain_second: float32 [4, 2, 1024], P('section'), may hold values from 0.1 to 4
- table_grads: float32 [4, 2, 32, 16], P('section', 'dp', None, 'tensor'), may hold values from -1.2 to 1.2
- table_first: float32 [32, 16], P(None, 'tensor'), may hold values from -3 to 3
- table_second: float32 [32, 16], P(None, 'tensor'), may hold values from 0.1 to 4
Outputs:
- update: float32 [4, 4, 1024, 1024], P('section', 'tensor', 'dp')
- first_next: float32 [4, 4, 1024, 1024], P('section', 'tensor', 'dp')
- second_next: float32 [4, 4, 1024, 1024], P('section', 'tensor', 'dp')
- left_next: float32 [4, 4, 1024, 1024], P('section', 'tensor', 'dp')
- right_next: float32 [4, 4, 1024, 1024], P('section', 'tensor', 'dp')
- left_rotation: float32 [4, 4, 1024, 1024], P('section', 'tensor', 'dp')
- right_rotation: float32 [4, 4, 1024, 1024], P('section', 'tensor', 'dp')
- gain_update: float32 [4, 2, 1024], P('section')
- gain_moment: float32 [4, 2, 1024], P('section')
- gain_squares: float32 [4, 2, 1024], P('section')
- table_update: float32 [32, 16], P(None, 'tensor')
- table_moment: float32 [32, 16], P(None, 'tensor')
- table_squares: float32 [32, 16], P(None, 'tensor')
All inputs are finite; a program needn't handle non-finite values.
Results may differ from a plain program's by a relative error of at most 0.014.
Values may be sent and summed in bfloat16 or wider, within the bound.
No kernel may reach another device: no remote copies, remote signals or barrier semaphores. Data moves between devices by JAX's collectives and lax.ppermute only.
A program may use at most 128 MiB of HBM per device.

v0:
```python
import jax
import jax.numpy as jnp
from jax import lax
from jax.sharding import PartitionSpec as P

NS_ITERS = 3


beta_first = 0.9
beta_second = 0.95
beta_stat = 0.95
adam_eps = 1e-08
norm_eps = 1e-06
step_count = 10.0


def to_half(value):
    return value.astype(jnp.bfloat16)


def batched(pattern, left, right):
    return jnp.einsum(pattern, left, right, preferred_element_type=jnp.float32)


def adam_direction(first, second):
    first_hat = first / (1.0 - beta_first**step_count)
    second_hat = second / (1.0 - beta_second**step_count)
    return first_hat / (jnp.sqrt(second_hat) + adam_eps)


def local(
    grad_parts,
    first_moment,
    second_moment,
    left_stat,
    right_stat,
    left_basis,
    right_basis,
    gain_grads,
    gain_first,
    gain_second,
    table_grads,
    table_first,
    table_second,
):
    partial_value = grad_parts[0, 0]
    columns = lax.all_to_all(partial_value, "tensor", split_axis=0, concat_axis=2, tiled=True)
    summed = lax.psum_scatter(
        columns.astype(jnp.float32).astype(jnp.bfloat16), "dp", scatter_dimension=1, tiled=True
    ).astype(jnp.float32)
    grad_rows = to_half(summed)
    row_count = grad_rows.shape[1]
    offset = lax.axis_index("dp") * row_count
    left_local = to_half(left_basis[0])
    right_local = to_half(right_basis[0])
    left_full, right_full = (
        lax.all_gather(left_local, "dp", axis=1, tiled=True),
        lax.all_gather(right_local, "dp", axis=1, tiled=True),
    )
    grad_full = lax.all_gather(grad_rows, "dp", axis=1, tiled=True)
    rotated_half = to_half(batched("mik,mkj->mij", grad_rows, right_full))
    block = left_local
    rotated = jnp.swapaxes(
        lax.psum_scatter(
            batched("mkc,mkj->cmj", block, rotated_half), "dp", scatter_dimension=0, tiled=True
        ),
        0,
        1,
    )
    first_new = beta_first * first_moment[0] + (1.0 - beta_first) * rotated
    second_new = beta_second * second_moment[0] + (1.0 - beta_second) * rotated * rotated
    direction = to_half(adam_direction(first_new, second_new))
    block = left_local
    back_half = to_half(
        batched("mik,mkj->mij", block, lax.all_gather(direction, "dp", axis=1, tiled=True))
    )
    update = batched("mik,mjk->mij", back_half, right_full)
    grad_columns = lax.dynamic_slice_in_dim(grad_full, offset, row_count, 2)
    left_new = beta_stat * left_stat[0] + batched("mik,mjk->mij", grad_rows, grad_full)
    right_new = beta_stat * right_stat[0] + batched("mki,mkj->mij", grad_columns, grad_full)
    power_left = batched("mik,mkj->mij", to_half(left_new), left_full)
    power_right = batched("mik,mkj->mij", to_half(right_new), right_full)
    power = jnp.concatenate([power_left, power_right], axis=0)
    squares = lax.psum(jnp.sum(power * power, axis=(1, 2)), "dp")
    iterate = power / jnp.sqrt(squares + norm_eps)[:, None, None]
    for sweep in range(NS_ITERS):
        iterate_half = to_half(iterate)
        iterate_full = lax.all_gather(iterate_half, "dp", axis=1, tiled=True)
        gram = to_half(batched("mik,mjk->mij", iterate_half, iterate_full))
        iterate = 1.5 * iterate - 0.5 * batched("mik,mkj->mij", gram, iterate_full)
    local_mats = power_left.shape[0]
    left_rotation = iterate[:local_mats]
    right_rotation = iterate[local_mats:]
    gain_sum = lax.psum(gain_grads[0, 0, 0], ("dp", "tensor"))
    gain_moment = beta_first * gain_first[0] + (1.0 - beta_first) * gain_sum
    gain_squares = beta_second * gain_second[0] + (1.0 - beta_second) * gain_sum * gain_sum
    gain_update = adam_direction(gain_moment, gain_squares)
    table_sum = lax.psum(table_grads[0, 0], ("dp", "section"))
    table_moment = beta_first * table_first + (1.0 - beta_first) * table_sum
    table_squares = beta_second * table_second + (1.0 - beta_second) * table_sum * table_sum
    table_update = adam_direction(table_moment, table_squares)
    return (
        update[None],
        first_new[None],
        second_new[None],
        left_new[None],
        right_new[None],
        left_rotation[None],
        right_rotation[None],
        gain_update[None],
        gain_moment[None],
        gain_squares[None],
        table_update,
        table_moment,
        table_squares,
    )


def solution(mesh):
    return jax.shard_map(
        local,
        mesh=mesh,
        in_specs=(
            P("section", "dp", None, None, "tensor"),
            P("section", "tensor", "dp", None),
            P("section", "tensor", "dp", None),
            P("section", "tensor", "dp", None),
            P("section", "tensor", "dp", None),
            P("section", "tensor", "dp", None),
            P("section", "tensor", "dp", None),
            P("section", "dp", "tensor", None, None),
            P("section", None, None),
            P("section", None, None),
            P("section", "dp", None, "tensor"),
            P(None, "tensor"),
            P(None, "tensor"),
        ),
        out_specs=(
            P("section", "tensor", "dp", None),
            P("section", "tensor", "dp", None),
            P("section", "tensor", "dp", None),
            P("section", "tensor", "dp", None),
            P("section", "tensor", "dp", None),
            P("section", "tensor", "dp", None),
            P("section", "tensor", "dp", None),
            P("section", None, None),
            P("section", None, None),
            P("section", None, None),
            P(None, "tensor"),
            P(None, "tensor"),
            P(None, "tensor"),
        ),
        check_vma=False,
    )
```

profile of v0, /device:TPU:0, one launch (start us, length us, event | category | flops | bytes accessed | tf_op | source)
XLA Modules:
  0.0 504.2 jit_solution(17281424494151594363)
XLA Ops:
  10.2 54.4 %all_to_all.18 = bf16[4,1024,256]{1,2,0:T(8,128)(2,1)} all-to-all(bf16[4,1024,256]{1,2,0:T(8,128)(2,1)S(1)} %bitcast.134), channel_id=1, replica_groups=mesh['dp'=2,'tensor'=4,'section'=4] {'tensor'}, dimensions={0} | all-to-all | bytes 4194304 | tf_op jit(solution)/shard_map/all_to_all | solution.py:47
  64.7 31.1 %reduce-scatter.3.cloned.1.call-done = bf16[1,512,1024]{1,2,0:T(8,128)(2,1)} async-done(((bf16[1,1024,1024]{1,2,0:T(8,128)(2,1)}), bf16[1,512,1024]{1,2,0:T(8,128)(2,1)}) %reduce-scatter.3.cloned.1.call-update) | async-done | bytes 1048592 | tf_op jit(solution)/shard_map/reduce_scatter | solution.py:48
  105.1 25.6 %all-gather.12.cloned.1.call-done = bf16[1,1024,1024]{1,2,0:T(8,128)(2,1)} async-done(((bf16[1,512,1024]{1,2,0:T(8,128)(2,1)}), bf16[1,1024,1024]{1,2,0:T(8,128)(2,1)}) %all-gather.12.cloned.1.call-update) | async-done | bytes 2097168 | tf_op jit(solution)/shard_map/all_gather | solution.py:60
  130.6 4.5 bitcast_add_fusion
  135.2 30.8 %all-gather.20.cloned.1.call-done = bf16[1,1,1024,1024]{3,2,1,0:T(8,128)(2,1)} async-done(((bf16[1,1,512,1024]{3,2,1,0:T(8,128)(2,1)}), bf16[1,1,1024,1024]{3,2,1,0:T(8,128)(2,1)}) %all-gather.20.cloned.1.call-update) | async-done | bytes 2097168 | tf_op jit(solution)/shard_map/all_gather | solution.py:58
  166.0 3.6 fusion.31
  172.3 28.9 %all-gather.22.cloned.1.call-done = bf16[1,1,1024,1024]{3,2,1,0:T(8,128)(2,1)} async-done(((bf16[1,1,512,1024]{3,2,1,0:T(8,128)(2,1)}), bf16[1,1,1024,1024]{3,2,1,0:T(8,128)(2,1)}) %all-gather.22.cloned.1.call-update) | async-done | bytes 2097168 | tf_op jit(solution)/shard_map/all_gather | solution.py:57
  201.2 3.5 fusion.34
  206.7 4.9 psum.21
  211.6 3.5 fusion.75
  216.3 6.3 %convolution_bitcast_fusion = f32[1024,1,1024]{0,2,1:T(8,128)} fusion(bf16[1,1,512,1024]{3,2,1,0:T(8,128)(2,1)S(1)} %copy-done.2, bf16[1,1,1024,1024]{3,2,1,0:T(8,128)(2,1)} %all-gather.20.cloned.1.call-done, bf16[1,512,1024]{1,2,0:T(8,128)(2,1)} %reduce-scatter.3.cloned.1.call-done), kind=kOutput, calls=%fused_computation.8 | convolution fusion | flops 2148007936 | bytes 8388608 | tf_op jit(solution)/shard_map/mkc,mkj->cmj/dot_general | solution.py:22
  222.9 49.2 %all-gather.14.cloned.1.call-done = bf16[2,1024,1024]{2,1,0:T(8,128)(2,1)} async-done(((bf16[2,512,1024]{2,1,0:T(8,128)(2,1)}), bf16[2,1024,1024]{2,1,0:T(8,128)(2,1)}) %all-gather.14.cloned.1.call-update) | async-done | bytes 4194320 | tf_op jit(solution)/shard_map/all_gather | solution.py:88
  272.0 12.0 %fusion.79 = (bf16[2,512,1024]{2,1,0:T(8,128)(2,1)}, f32[2,512,1024]{2,1,0:T(8,128)}) fusion(bf16[2,1024,1024]{2,1,0:T(8,128)(2,1)} %all-gather.14.cloned.1.call-done, f32[2]{0:T(128)S(1)} %add_sqrt_fusion, f32[1,512,1024]{2,1,0:T(8,128)S(1)} %fusion.31, f32[1,512,1024]{2,1,0:T(8,128)} %copy-done), kind=kOutput, calls=%fused_computation.72 | convolution fusion | flops 4305453056 | bytes 14680072 | tf_op jit(solution)/shard_map/mik,mkj->mij/dot_general | solution.py:22
  289.0 39.7 %reduce-scatter.5.cloned.1.call-done = f32[512,1,1024]{0,2,1:T(8,128)} async-done(((f32[1024,1,1024]{0,2,1:T(8,128)}), f32[512,1,1024]{0,2,1:T(8,128)}) %reduce-scatter.5.cloned.1.call-update) | async-done | bytes 2097168 | tf_op jit(solution)/shard_map/reduce_scatter | solution.py:64
  328.6 4.6 fusion.27
  333.3 54.2 %all-gather.16.cloned.1.call-done = bf16[2,1024,1024]{2,1,0:T(8,128)(2,1)} async-done(((bf16[2,512,1024]{2,1,0:T(8,128)(2,1)}), bf16[2,1024,1024]{2,1,0:T(8,128)(2,1)}) %all-gather.16.cloned.1.call-update) | async-done | bytes 4194320 | tf_op jit(solution)/shard_map/all_gather | solution.py:88
  387.5 12.6 %fusion.82 = (bf16[2,512,1024]{2,1,0:T(8,128)(2,1)}, f32[2,512,1024]{2,1,0:T(8,128)}) fusion(bf16[2,1024,1024]{2,1,0:T(8,128)(2,1)} %all-gather.16.cloned.1.call-done, bf16[2,512,1024]{2,1,0:T(8,128)(2,1)} %get-tuple-element.49, f32[2,512,1024]{2,1,0:T(8,128)} %get-tuple-element.50), kind=kOutput, calls=%fused_computation.73 | convolution fusion | flops 4300210176 | bytes 16777216 | tf_op jit(solution)/shard_map/mik,mkj->mij/dot_general | solution.py:22
  400.8 12.9 %psum.23 = f32[32,4]{0,1:T(4,128)S(1)} all-reduce(f32[32,4]{0,1:T(4,128)S(1)} %bitcast.136), channel_id=1, replica_groups=mesh['dp'=2,'tensor'=4,'section'=4] {'dp','section'}, use_global_device_ids=true, to_apply=%region_5.0 | all-reduce | flops 128 | bytes 1024 | tf_op jit(solution)/shard_map/psum | solution.py:98
  413.7 22.1 %psum.22 = f32[2,1024]{1,0:T(2,128)S(1)} all-reduce(f32[2,1024]{1,0:T(2,128)S(1)} %bitcast.135), channel_id=1, replica_groups=mesh['dp'=2,'tensor'=4,'section'=4] {'dp','tensor'}, use_global_device_ids=true, to_apply=%region_4.0 | all-reduce | flops 2048 | bytes 16384 | tf_op jit(solution)/shard_map/psum | solution.py:94
  442.9 5.0 fusion.6
  452.8 6.1 %fusion.28 = f32[1,1,512,1024]{3,2,1,0:T(8,128)} fusion(bf16[1,1,1024,1024]{3,2,1,0:T(8,128)(2,1)} %all-gather.20.cloned.1.call-done, bf16[1,1024,1024]{1,2,0:T(8,128)(2,1)} %all-gather.10.cloned.1.call-done, bf16[1,1,512,1024]{3,2,1,0:T(8,128)(2,1)S(1)} %copy-done.2), kind=kOutput, calls=%fused_computation.42 | convolution fusion | flops 2148007936 | bytes 7340032 | tf_op jit(solution)/shard_map/mik,mjk->mij/dot_general | solution.py:22
  458.9 22.8 %all-gather.18.cloned.1.call-done = bf16[2,1024,1024]{2,1,0:T(8,128)(2,1)} async-done(((bf16[2,512,1024]{2,1,0:T(8,128)(2,1)}), bf16[2,1024,1024]{2,1,0:T(8,128)(2,1)}) %all-gather.18.cloned.1.call-update) | async-done | bytes 4194320 | tf_op jit(solution)/shard_map/all_gather | solution.py:88
  481.7 11.2 %multiply_subtract_fusion = f32[2,512,1024]{2,1,0:T(8,128)} fusion(f32[2,512,1024]{2,1,0:T(8,128)} %get-tuple-element.52, bf16[2,1024,1024]{2,1,0:T(8,128)(2,1)} %all-gather.18.cloned.1.call-done, bf16[2,512,1024]{2,1,0:T(8,128)(2,1)S(1)} %copy-done.5), kind=kOutput, calls=%fused_computation.1 | convolution fusion | flops 4299161600 | bytes 14680064 | tf_op jit(solution)/shard_map/mik,mkj->mij/dot_general | solution.py:22
  492.9 4.8 slice_bitcast_fusion
  (67 shorter events, 35.8 us)
Async XLA Ops:
  7.2 88.7 %reduce-scatter.3.cloned.1.call-start = ((), (), s32[]{:S(2)}) async-start(), calls=%async_computation.3 | async-start | bytes 3145728 | tf_op jit(solution)/shard_map/reduce_scatter | solution.py:48
  64.7 31.3 %copy-start.3 = (f32[1,1,512,1024]{3,2,1,0:T(8,128)S(1)}, f32[1,1,512,1024]{3,2,1,0:T(8,128)}, u32[]{:S(2)}) copy-start(f32[1,1,512,1024]{3,2,1,0:T(8,128)} %param.19) | copy-start | bytes 6291460
  64.7 66.0 %all-gather.12.cloned.1.call-start = ((), (), s32[]{:S(2)}) async-start(), calls=%async_computation.6 | async-start | bytes 3145728 | tf_op jit(solution)/shard_map/all_gather | solution.py:60
  95.9 70.1 %all-gather.20.cloned.1.call-start = ((), (), s32[]{:S(2)}) async-start(), calls=%async_computation.10 | async-start | bytes 3145728 | tf_op jit(solution)/shard_map/all_gather | solution.py:58
  97.1 3.0 copy-start.4
  97.1 104.1 %all-gather.22.cloned.1.call-start = ((), (), s32[]{:S(2)}) async-start(), calls=%async_computation.11 | async-start | bytes 3145728 | tf_op jit(solution)/shard_map/all_gather | solution.py:57
  100.1 172.0 %all-gather.14.cloned.1.call-start = ((), (), s32[]{:S(2)}) async-start(), calls=%async_computation.7 | async-start | bytes 6291456 | tf_op jit(solution)/shard_map/all_gather | solution.py:88
  101.9 28.7 %copy-start.7 = (f32[1,1,512,1024]{2,3,1,0:T(8,128)S(1)}, f32[1,1,512,1024]{2,3,1,0:T(8,128)}, u32[]{:S(2)}) copy-start(f32[1,1,512,1024]{2,3,1,0:T(8,128)} %copy.41) | copy-start | bytes 6291460
  135.2 34.5 %copy-start.8 = (bf16[1,512,1024]{1,2,0:T(8,128)(2,1)S(1)}, bf16[1,512,1024]{1,2,0:T(8,128)(2,1)}, u32[]{:S(2)}) copy-start(bf16[1,512,1024]{1,2,0:T(8,128)(2,1)} %reduce-scatter.3.cloned.1.call-done) | copy-start | bytes 3145732
  166.0 3.7 copy-start.6
  166.0 3.7 copy-start.15
  204.7 1.3 copy-start
  215.1 1.2 copy-start.2
  215.1 113.5 %reduce-scatter.5.cloned.1.call-start = ((), (), s32[]{:S(2)}) async-start(), calls=%async_computation.4 | async-start | bytes 6291456 | tf_op jit(solution)/shard_map/reduce_scatter | solution.py:64
  222.6 164.9 %all-gather.16.cloned.1.call-start = ((), (), s32[]{:S(2)}) async-start(), calls=%async_computation.8 | async-start | bytes 6291456 | tf_op jit(solution)/shard_map/all_gather | solution.py:88
  284.1 168.7 %all-gather.10.cloned.1.call-start = ((), (), s32[]{:S(2)}) async-start(), calls=%async_computation.5 | async-start | bytes 3145728 | tf_op jit(solution)/shard_map/all_gather | solution.py:75
  333.3 148.4 %all-gather.18.cloned.1.call-start = ((), (), s32[]{:S(2)}) async-start(), calls=%async_computation.9 | async-start | bytes 6291456 | tf_op jit(solution)/shard_map/all_gather | solution.py:88
  400.1 13.6 %copy-start.9 = (f32[1,1,1,2,1024]{4,3,2,1,0:T(2,128)S(1)}, f32[1,1,1,2,1024]{4,3,2,1,0:T(2,128)}, u32[]{:S(2)}) copy-start(f32[1,1,1,2,1024]{4,3,2,1,0:T(2,128)} %param.20) | copy-start | bytes 24580
  400.1 35.7 %copy-start.13 = (f32[32,4]{0,1:T(4,128)S(1)}, f32[32,4]{0,1:T(4,128)}, u32[]{:S(2)}) copy-start(f32[32,4]{0,1:T(4,128)} %param.24) | copy-start | bytes 1540
  400.1 35.7 %copy-start.14 = (f32[32,4]{0,1:T(4,128)S(1)}, f32[32,4]{0,1:T(4,128)}, u32[]{:S(2)}) copy-start(f32[32,4]{0,1:T(4,128)} %param.25) | copy-start | bytes 1540
  400.1 36.3 %copy-start.10 = (f32[1,2,1024]{2,1,0:T(2,128)S(1)}, f32[1,2,1024]{2,1,0:T(2,128)}, u32[]{:S(2)}) copy-start(f32[1,2,1024]{2,1,0:T(2,128)} %param.22) | copy-start | bytes 24580
  400.1 36.3 %copy-start.11 = (f32[1,2,1024]{2,1,0:T(2,128)S(1)}, f32[1,2,1024]{2,1,0:T(2,128)}, u32[]{:S(2)}) copy-start(f32[1,2,1024]{2,1,0:T(2,128)} %param.21) | copy-start | bytes 24580
  447.9 3.0 copy-start.1
  452.8 28.9 %copy-start.5 = (bf16[2,512,1024]{2,1,0:T(8,128)(2,1)S(1)}, bf16[2,512,1024]{2,1,0:T(8,128)(2,1)}, u32[]{:S(2)}) copy-start(bf16[2,512,1024]{2,1,0:T(8,128)(2,1)} %get-tuple-element.51) | copy-start | bytes 6291460
  (1 other events, 0.7 us)
Sparse Core Ops, SparseCore 0:
  64.8 31.0 reduce-scatter.2
  97.5 33.1 all-gather.11
  132.8 33.1 all-gather.19
  168.0 33.1 all-gather.21
  215.2 56.7 all-gather.13
  274.3 54.3 reduce-scatter.4
  330.7 56.7 all-gather.15
  389.6 33.4 all-gather.9
  424.7 56.9 all-gather.17
where the time goes:
time: 505 us; the launch traced here: 504 us
  waiting for transfers between devices  282 us (56%)
  blocking collectives  94.3 us (19%)
  matrix products  62.5 us (12%)
  local copies, waits for them, and re-layouts  31.4 us (6%)
  other arithmetic  19.1 us (4%)
  between operations  14 us (3%)
    all_gather x3, waiting for transfers between devices, local(): iterate_full = lax.all_gather(iterate_half, 'dp', axis=1, tiled=True)  126 us
    dot_general x9, matrix products, batched(): return jnp.einsum(pattern, left, right, preferred_element_type=jnp.float32)  62.5 us
    all_to_all x1, blocking collectives, local(): lax.all_to_all(partial_value, 'tensor', split_axis=0, concat_axis=2, tile...  54.4 us
    reduce_scatter x1, waiting for transfers between devices, local(): lax.psum_scatter(batched('mkc,mkj->cmj', block, rotated_half), 'dp', scat...  39.7 us
    reduce_scatter x1, waiting for transfers between devices, local(): lax.psum_scatter(columns.astype(jnp.float32).astype(jnp.bfloat16), 'dp',...  31.1 us
    all_gather x1, waiting for transfers between devices, local(): lax.all_gather(right_local, 'dp', axis=1, tiled=True)  30.8 us
    all_gather x1, waiting for transfers between devices, local(): lax.all_gather(left_local, 'dp', axis=1, tiled=True)  28.9 us
    unnamed x41, local copies, waits for them, and re-layouts  26.6 us
  transfers between devices with their start and end apart: 9, of which 8 were waited for; matrix products, arithmetic and copies ran while one was open for 16% of the time, Pallas kernels for 0%

commit v1 on v0

v1 whole, which is shorter than its diff:
```python
import functools

import jax
import jax.numpy as jnp
from jax import lax
from jax.experimental import pallas as pl
from jax.experimental.pallas import tpu as pltpu
from jax.sharding import PartitionSpec as P

NS_ITERS = 3

beta_first = 0.9
beta_second = 0.95
beta_stat = 0.95
adam_eps = 1e-08
norm_eps = 1e-06
step_count = 10.0

f32 = jnp.float32
bf16 = jnp.bfloat16
MIB = 1024 * 1024

NN = (((1,), (0,)), ((), ()))
NT = (((1,), (1,)), ((), ()))
TN = (((0,), (0,)), ((), ()))


def product(left, right, dims=NN):
    return lax.dot_general(left, right, dims, preferred_element_type=f32)


def adam_direction(first, second):
    first_hat = first / (1.0 - beta_first**step_count)
    second_hat = second / (1.0 - beta_second**step_count)
    return first_hat / (jnp.sqrt(second_hat) + adam_eps)


def tiles(extent, most=256):
    size = min(extent, most)
    return [slice(start, start + size) for start in range(0, extent, size)]


def join(whole, offsets, pieces):
    for place, piece in enumerate(pieces):
        count = piece.shape[0]
        whole[pl.ds(pl.multiple_of(offsets[place], count), count), :] = piece[...]


def call(kernel, outs, scratch, flops, nbytes, *operands):
    return pl.pallas_call(
        kernel,
        out_shape=outs,
        in_specs=[pl.BlockSpec(memory_space=pltpu.SMEM)]
        + [pl.BlockSpec(memory_space=pltpu.VMEM)] * (len(operands) - 1),
        out_specs=[pl.BlockSpec(memory_space=pltpu.VMEM)] * len(outs),
        scratch_shapes=scratch,
        compiler_params=pltpu.CompilerParams(vmem_limit_bytes=40 * MIB),
    )(*operands)


def shape(rows, columns, dtype):
    return jax.ShapeDtypeStruct((rows, columns), dtype)


def assemble_kernel(width, places, *refs):
    *blocks, out = refs
    for place, block in enumerate(blocks):
        out[:, pl.ds(pl.multiple_of(places[place], width), width)] = block[...]


def stats_kernel(n, offsets, *refs):
    pieces, column_pieces = refs[:n], refs[n : 2 * n]
    rows_ref, left_stat, right_stat = refs[2 * n : 2 * n + 3]
    left_next, left_half, right_next, right_half, grad, columns = refs[2 * n + 3 :]
    join(grad, offsets, pieces)
    join(columns, offsets, column_pieces)
    for at in tiles(rows_ref.shape[0]):
        value = beta_stat * left_stat[at] + product(rows_ref[at], grad[...], NT)
        left_next[at] = value
        left_half[at] = value.astype(bf16)
    for at in tiles(rows_ref.shape[0]):
        value = beta_stat * right_stat[at] + product(columns[:, at], grad[...], TN)
        right_next[at] = value
        right_half[at] = value.astype(bf16)


def moments_kernel(n, nr, offsets, *refs):
    pieces, column_pieces, right_pieces = refs[:n], refs[n : 2 * n], refs[2 * n : 2 * n + nr]
    first, second = refs[2 * n + nr : 2 * n + nr + 2]
    first_next, second_next, direction, grad, columns, right, rotated_half = refs[2 * n + nr + 2 :]
    join(grad, [offsets[i] for i in range(n)], pieces)
    join(columns, [offsets[i] for i in range(n)], column_pieces)
    join(right, [offsets[n + i] for i in range(nr)], right_pieces)
    for at in tiles(grad.shape[0]):
        rotated_half[at] = product(grad[at], right[...]).astype(bf16)
    for at in tiles(first.shape[0]):
        rotated = product(columns[:, at], rotated_half[...], TN)
        first_new = beta_first * first[at] + (1.0 - beta_first) * rotated
        second_new = beta_second * second[at] + (1.0 - beta_second) * rotated * rotated
        first_next[at] = first_new
        second_next[at] = second_new
        direction[at] = adam_direction(first_new, second_new).astype(bf16)


def update_kernel(n, nr, offsets, *refs):
    pieces, right_pieces, rows_ref = refs[:n], refs[n : n + nr], refs[n + nr]
    update, direction, right = refs[n + nr + 1 :]
    join(direction, [offsets[i] for i in range(n)], pieces)
    join(right, [offsets[n + i] for i in range(nr)], right_pieces)
    for at in tiles(rows_ref.shape[0]):
        back_half = product(rows_ref[at], direction[...]).astype(bf16)
        update[at] = product(back_half, right[...], NT)


def rotation_kernel(ns, nb, offsets, *refs):
    stat_pieces, basis_pieces = refs[:ns], refs[ns : ns + nb]
    out, stat, basis, iterate, half_a, half_b = refs[ns + nb :]
    rows = out.shape[0]
    extent = stat.shape[0]
    join(stat, [offsets[i] for i in range(ns)], stat_pieces)
    join(basis, [offsets[ns + i] for i in range(nb)], basis_pieces)
    size = min(extent, 256)

    def at(step, base=0):
        return pl.ds(pl.multiple_of(base + step * size, size), size)

    def power_tile(step, total):
        power = product(stat[at(step), :], basis[...])
        iterate[at(step), :] = power
        return total + jnp.sum(power * power)

    squares = lax.fori_loop(0, extent // size, power_tile, jnp.zeros((), f32))
    scale = 1.0 / jnp.sqrt(squares + norm_eps)

    def scale_tile(step, carry):
        value = iterate[at(step), :] * scale
        iterate[at(step), :] = value
        half_a[at(step), :] = value.astype(bf16)
        return carry

    lax.fori_loop(0, extent // size, scale_tile, 0)
    halves = (half_a, half_b)
    for sweep in range(NS_ITERS):
        source, target = halves[sweep % 2], halves[(sweep + 1) % 2]
        if sweep < NS_ITERS - 1:

            def sweep_tile(step, carry, source=source, target=target):
                gram = product(source[at(step), :], source[...], NT).astype(bf16)
                value = 1.5 * iterate[at(step), :] - 0.5 * product(gram, source[...])
                iterate[at(step), :] = value
                target[at(step), :] = value.astype(bf16)
                return carry

            lax.fori_loop(0, extent // size, sweep_tile, 0)
        else:
            own = min(rows, size)
            base = offsets[ns + nb]

            def last_tile(step, carry, source=source):
                here = pl.ds(pl.multiple_of(base + step * own, own), own)
                gram = product(source[here, :], source[...], NT).astype(bf16)
                value = 1.5 * iterate[here, :] - 0.5 * product(gram, source[...])
                out[pl.ds(pl.multiple_of(step * own, own), own), :] = value
                return carry

            lax.fori_loop(0, rows // own, last_tile, 0)


def build(mesh):
    n_dp, n_tensor, n_section = mesh.shape["dp"], mesh.shape["tensor"], mesh.shape["section"]
    pair = n_dp == 2

    def swap(value):
        return lax.ppermute(value, "dp", [(0, 1), (1, 0)])

    def total(value, axis, count):
        if count & (count - 1):
            return lax.psum(value, axis)
        step = 1
        while step < count:
            value = value + lax.ppermute(value, axis, [(i, i ^ step) for i in range(count)])
            step *= 2
        return value

    def after(value, *others):
        return lax.optimization_barrier((value,) + others)[0]

    def local(
        grad_parts,
        first_moment,
        second_moment,
        left_stat,
        right_stat,
        left_basis,
        right_basis,
        gain_grads,
        gain_first,
        gain_second,
        table_grads,
        table_first,
        table_second,
    ):
        partial_value = grad_parts[0, 0]
        mats, extent, width = partial_value.shape
        rows = left_basis.shape[2]
        dp = lax.axis_index("dp")
        rank = lax.axis_index("tensor")
        own = dp * rows
        other = (n_dp - 1 - dp) * rows

        def rows_of(value, start):
            return lax.dynamic_slice_in_dim(value, start, rows, 1)

        gain_part = gain_grads[0, 0, 0]
        table_part = table_grads[0, 0]
        both = jnp.concatenate([gain_part.reshape(-1), table_part.reshape(-1)])
        both = total(both, "dp", n_dp)

        if pair:
            received = swap(rows_of(partial_value, other))
            received, both = lax.optimization_barrier((received, both))
            left_local = left_basis[0, 0].astype(bf16)
            right_local = right_basis[0, 0].astype(bf16)
            left_other = swap(after(left_local, both))
            summed = (
                rows_of(partial_value, own).astype(f32) + received.astype(f32)
            ).astype(bf16)
            middle = rows // 4
            right_other_a = swap(after(right_local[:middle], summed))
            blocks = []
            places = []
            for step in range(n_tensor):
                block = lax.dynamic_index_in_dim(summed, rank ^ step, 0, keepdims=False)
                if step:
                    block = lax.ppermute(
                        block, "tensor", [(i, i ^ step) for i in range(n_tensor)]
                    )
                blocks.append(block)
                places.append((rank ^ step) * width)
            *blocks, left_other, right_other_a = lax.optimization_barrier(
                (*blocks, left_other, right_other_a)
            )
            (grad_rows,) = call(
                functools.partial(assemble_kernel, width),
                [shape(rows, extent, bf16)],
                [],
                0,
                4 * rows * extent,
                jnp.stack(places),
                *blocks,
            )
            grad_other = swap(grad_rows)
            right_other_b = swap(after(right_local[middle:], grad_rows))
            grad_pieces = [grad_rows, grad_other]
            left_pieces = [left_local, left_other]
            right_pieces = [right_local, right_other_a, right_other_b]
            offsets = jnp.stack([own, other])
            right_offsets = jnp.stack([own, other, other + middle])
        else:
            columns = lax.all_to_all(partial_value, "tensor", split_axis=0, concat_axis=2, tiled=True)
            summed = lax.psum_scatter(columns, "dp", scatter_dimension=1, tiled=True)
            grad_rows = summed[0]
            left_local = left_basis[0, 0].astype(bf16)
            right_local = right_basis[0, 0].astype(bf16)

            def gather(value):
                return [lax.all_gather(value, "dp", axis=0, tiled=True)]

            grad_pieces, left_pieces, right_pieces = (
                gather(grad_rows),
                gather(left_local),
                gather(right_local),
            )
            offsets = right_offsets = jnp.zeros((1,), jnp.int32)
        gain_sum = total(both[: gain_part.size].reshape(gain_part.shape), "tensor", n_tensor)
        table_sum = total(both[gain_part.size :].reshape(table_part.shape), "section", n_section)
        n, nr = len(grad_pieces), len(right_pieces)
        cube = 2 * extent**3

        def columns_of(pieces):
            return [lax.dynamic_slice_in_dim(piece, own, rows, 1) for piece in pieces]

        left_new, left_new_half, right_new, right_new_half = call(
            functools.partial(stats_kernel, n),
            [shape(rows, extent, f32), shape(rows, extent, bf16)] * 2,
            [pltpu.VMEM((extent, extent), bf16), pltpu.VMEM((extent, rows), bf16)],
            cube,
            12 * MIB,
            offsets,
            *grad_pieces,
            *columns_of(grad_pieces),
            grad_rows,
            left_stat[0, 0],
            right_stat[0, 0],
        )
        if pair:
            left_new_pieces = [left_new_half, swap(left_new_half)]
            right_new_pieces = [right_new_half, swap(right_new_half)]
        else:
            left_new_pieces, right_new_pieces = gather(left_new_half), gather(right_new_half)
        first_new, second_new, direction = call(
            functools.partial(moments_kernel, n, nr),
            [shape(rows, extent, f32)] * 2 + [shape(rows, extent, bf16)],
            [
                pltpu.VMEM((extent, extent), bf16),
                pltpu.VMEM((extent, rows), bf16),
                pltpu.VMEM((extent, extent), bf16),
                pltpu.VMEM((extent, extent), bf16),
            ],
            cube * 3 // 2,
            12 * MIB,
            jnp.concatenate([offsets, right_offsets]),
            *grad_pieces,
            *columns_of(left_pieces),
            *right_pieces,
            first_moment[0, 0],
            second_moment[0, 0],
        )
        direction_pieces = [direction, swap(direction)] if pair else gather(direction)

        def rotation(stat_pieces, basis_pieces, basis_offsets):
            return call(
                functools.partial(rotation_kernel, len(stat_pieces), len(basis_pieces)),
                [shape(rows, extent, f32)],
                [
                    pltpu.VMEM((extent, extent), bf16),
                    pltpu.VMEM((extent, extent), bf16),
                    pltpu.VMEM((extent, extent), f32),
                    pltpu.VMEM((extent, extent), bf16),
                    pltpu.VMEM((extent, extent), bf16),
                ],
                cube * 6,
                6 * MIB,
                jnp.concatenate([offsets, basis_offsets, jnp.stack([own])]),
                *stat_pieces,
                *basis_pieces,
            )[0]

        left_new_pieces[-1] = after(left_new_pieces[-1], direction)
        left_rotation = rotation(left_new_pieces, left_pieces, offsets)
        right_new_pieces[-1] = after(right_new_pieces[-1], left_rotation)
        right_rotation = rotation(right_new_pieces, right_pieces, right_offsets)
        direction_pieces[-1] = after(direction_pieces[-1], right_rotation)
        (update,) = call(
            functools.partial(update_kernel, n, nr),
            [shape(rows, extent, f32)],
            [pltpu.VMEM((extent, extent), bf16), pltpu.VMEM((extent, extent), bf16)],
            cube,
            7 * MIB,
            jnp.concatenate([offsets, right_offsets]),
            *direction_pieces,
            *right_pieces,
            left_local,
        )

        gain_moment = beta_first * gain_first[0] + (1.0 - beta_first) * gain_sum
        gain_squares = beta_second * gain_second[0] + (1.0 - beta_second) * gain_sum * gain_sum
        gain_update = adam_direction(gain_moment, gain_squares)
        table_moment = beta_first * table_first + (1.0 - beta_first) * table_sum
        table_squares = beta_second * table_second + (1.0 - beta_second) * table_sum * table_sum
        table_update = adam_direction(table_moment, table_squares)
        return (
            update[None, None],
            first_new[None, None],
            second_new[None, None],
            left_new[None, None],
            right_new[None, None],
            left_rotation[None, None],
            right_rotation[None, None],
            gain_update[None],
            gain_moment[None],
            gain_squares[None],
            table_update,
            table_moment,
            table_squares,
        )

    return local


def solution(mesh):
    state = P("section", "tensor", "dp", None)
    gains = P("section", None, None)
    table = P(None, "tensor")
    return jax.shard_map(
        build(mesh),
        mesh=mesh,
        in_specs=(P("section", "dp", None, None, "tensor"),)
        + (state,) * 6
        + (P("section", "dp", "tensor", None, None), gains, gains)
        + (P("section", "dp", None, "tensor"), table, table),
        out_specs=(state,) * 7 + (gains,) * 3 + (table,) * 3,
        check_vma=False,
    )
```

time: 505 us -> 176 us (0.35)
  waiting for transfers between devices: 282 us -> 77.6 us
  blocking collectives: 94.3 us -> 0 us
  matrix products: 62.5 us -> 0 us
  Pallas kernels: 0 us -> 60.1 us
  local copies, waits for them, and re-layouts: 31.4 us -> 7.5 us
  starting transfers between devices: 0.55 us -> 21 us
  between operations: 14 us -> 0.96 us
  other arithmetic: 19.1 us -> 7.96 us
    all_gather x7 -> x0, waiting for transfers between devices: 211 us -> none  [the longest x3 126 us: local(): iterate_full = lax.all_gather(iterate_half, 'dp', axis=1, tiled=True)]
    ppermute x0 -> x16, waiting for transfers between devices: none -> 77.6 us  [the longest x8 35.2 us: swap(): return lax.ppermute(value, 'dp', [(0, 1), (1, 0)])]
    reduce_scatter x2 -> x0, waiting for transfers between devices: 70.8 us -> none  [the longest x1 39.7 us: local(): lax.psum_scatter(batched('mkc,mkj->cmj', block, rotated_half), 'dp', scat...]
    dot_general x9 -> x0, matrix products: 62.5 us -> none  [batched(): return jnp.einsum(pattern, left, right, preferred_element_type=jnp.float32)]
    pallas_call x0 -> x6, Pallas kernels: none -> 60.1 us  [call(): pl.pallas_call(kernel, out_shape=outs, in_specs=[pl.BlockSpec(memory_spac...]
    all_to_all x1 -> x0, blocking collectives: 54.4 us -> none  [local(): lax.all_to_all(partial_value, 'tensor', split_axis=0, concat_axis=2, tile...]
    psum x3 -> x0, blocking collectives: 39.9 us -> none  [the longest x1 22.1 us: local(): gain_sum = lax.psum(gain_grads[0, 0, 0], ('dp', 'tensor'))]
    unnamed x41 -> x38, local copies, waits for them, and re-layouts: 26.6 us -> 2.62 us
  transfers between devices with their start and end apart: 9 -> 16, of which waited for: 8 -> 10; matrix products, arithmetic and copies ran while one was open for 16% -> 6% of each run, Pallas kernels for 0% -> 31%
where the time goes in v1:
time: 176 us; the launch traced here: 175 us
  waiting for transfers between devices  77.6 us (44%)
  Pallas kernels  60.1 us (34%)
  starting transfers between devices  21 us (12%)
  other arithmetic  7.96 us (5%)
  local copies, waits for them, and re-layouts  7.5 us (4%)
    pallas_call x6, Pallas kernels, call(): pl.pallas_call(kernel, out_shape=outs, in_specs=[pl.BlockSpec(memory_spac...  60.1 us
    ppermute x8, waiting for transfers between devices, swap(): return lax.ppermute(value, 'dp', [(0, 1), (1, 0)])  35.2 us
    ppermute x5, waiting for transfers between devices, total(): lax.ppermute(value, axis, [(i, i ^ step) for i in range(count)])  26.8 us
    ppermute x3, waiting for transfers between devices, local(): lax.ppermute(block, 'tensor', [(i, i ^ step) for i in range(n_tensor)])  15.6 us
    ppermute x8, starting transfers between devices, swap(): return lax.ppermute(value, 'dp', [(0, 1), (1, 0)])  10.2 us
    ppermute x5, starting transfers between devices, total(): lax.ppermute(value, axis, [(i, i ^ step) for i in range(count)])  6.42 us
    ppermute x3, starting transfers between devices, local(): lax.ppermute(block, 'tensor', [(i, i ^ step) for i in range(n_tensor)])  4.39 us
  transfers between devices with their start and end apart: 16, of which 10 were waited for; matrix products, arithmetic and copies ran while one was open for 6% of the time, Pallas kernels for 31%

profile of v1, /device:TPU:0, one launch (start us, length us, event | category | flops | bytes accessed | tf_op | source)
XLA Modules:
  0.0 175.1 jit_solution(1408278693527613397)
XLA Ops:
  0.7 2.4 %dynamic-slice_bitcast_fusion = bf16[4,512,256]{2,1,0:T(8,128)(2,1)} fusion(bf16[1,1,4,1024,256]{4,3,2,1,0:T(8,128)(2,1)} %param.13, s32[]{:T(128)S(6)} %select_n.24), kind=kLoop, calls=%fused_computation.2 | loop fusion | bytes 2097156 | tf_op jit(solution)/shard_map/dynamic_slice | solution.py:212
  3.1 2.9 %collective-permute-start = (bf16[4,512,256]{2,1,0:T(8,128)(2,1)}, bf16[4,512,256]{2,1,0:T(8,128)(2,1)}, u32[]{:S(2)}, u32[]{:S(2)}) collective-permute-start(bf16[4,512,256]{2,1,0:T(8,128)(2,1)} %dynamic-slice_bitcast_fusion), channel_id=1, source_target_pairs={{0,16},{16,0},{1,17},{17,1},{2,18},{18,2},{3,19},{19,3},{4,20},{20... | collective-permute-start | bytes 3145736 | tf_op jit(solution)/shard_map/ppermute | solution.py:174
  6.5 23.1 %collective-permute-done.1 = f32[2176]{0:T(1024)S(1)} collective-permute-done((f32[2176]{0:T(1024)S(1)}, f32[2176]{0:T(1024)S(1)}, u32[]{:S(2)}, u32[]{:S(2)}) %collective-permute-start.1) | collective-permute-done | bytes 8736 | tf_op jit(solution)/shard_map/ppermute | solution.py:181
  29.7 1.7 collective-permute-start.5
  31.4 1.7 convert_element_type.28
  34.2 1.8 %fusion = bf16[4,512,256]{2,1,0:T(8,128)(2,1)S(1)} fusion(bf16[4,512,256]{2,1,0:T(8,128)(2,1)} %collective-permute-done, bf16[1,1,4,1024,256]{4,3,2,1,0:T(8,128)(2,1)} %param.13, s32[]{:T(128)S(6)} %select_n.23), kind=kLoop, calls=%fused_computation.1 | loop fusion | flops 2097152 | bytes 3145732 | tf_op jit(solution)/shard_map/convert_element_type | solution.py:227
  36.9 1.6 collective-permute-start.2
  38.5 2.6 %collective-permute-start.3 = (bf16[512,256]{1,0:T(8,128)(2,1)}, bf16[512,256]{1,0:T(8,128)(2,1)S(1)}, u32[]{:S(2)}, u32[]{:S(2)}) collective-permute-start(bf16[512,256]{1,0:T(8,128)(2,1)} %get-tuple-element.87), channel_id=1, source_target_pairs={{0,8},{4,12},{8,0},{12,4},{1,9},{5,13},{9,1},{13,5},{2,10},{6,14},... | collective-permute-start | bytes 786440 | tf_op jit(solution)/shard_map/ppermute | solution.py:235
  41.6 2.7 %convert_element_type.26 = bf16[1,1,512,1024]{3,2,1,0:T(8,128)(2,1)} convert(f32[1,1,512,1024]{3,2,1,0:T(8,128)} %param.18) | non-fusion elementwise | flops 524288 | bytes 3145728 | tf_op jit(solution)/shard_map/convert_element_type | solution.py:222
  44.5 3.9 %collective-permute-done.2.refs_1_ = bf16[512,256]{1,0:T(8,128)(2,1)S(1)} collective-permute-done((bf16[512,256]{1,0:T(8,128)(2,1)}, bf16[512,256]{1,0:T(8,128)(2,1)S(1)}, u32[]{:S(2)}, u32[]{:S(2)}) %collective-permute-start.2) | collective-permute-done | bytes 262176 | tf_op jit(solution)/shard_map/ppermute | solution.py:235
  48.4 11.7 %collective-permute-done.3.refs_2_ = bf16[512,256]{1,0:T(8,128)(2,1)S(1)} collective-permute-done((bf16[512,256]{1,0:T(8,128)(2,1)}, bf16[512,256]{1,0:T(8,128)(2,1)S(1)}, u32[]{:S(2)}, u32[]{:S(2)}) %collective-permute-start.3) | collective-permute-done | bytes 262176 | tf_op jit(solution)/shard_map/ppermute | solution.py:235
  64.4 22.5 %collective-permute-done.7.refs_1_ = bf16[512,1024]{1,0:T(8,128)(2,1)S(1)} collective-permute-done((bf16[512,1024]{1,0:T(8,128)(2,1)S(1)}, bf16[512,1024]{1,0:T(8,128)(2,1)S(1)}, u32[]{:S(2)}, u32[]{:S(2)}) %collective-permute-start.7) | collective-permute-done | bytes 1048608 | tf_op jit(solution)/shard_map/ppermute | solution.py:174
  87.1 4.9 %shard_map.230 = (f32[512,1024]{1,0:T(8,128)}, bf16[512,1024]{1,0:T(8,128)(2,1)}, f32[512,1024]{1,0:T(8,128)}, bf16[512,1024]{1,0:T(8,128)(2,1)}) custom-call(s32[2]{0:T(128)S(1)} %pad_add_fusion.1.offsets, bf16[512,1024]{1,0:T(8,128)(2,1)S(1)} %shard_map.228.refs_0_.refs_4_, bf16[512,1024]{1,0:T(8,128)(2,1)S(1)} %collective-permute-done.7.refs_1_, ...), custom_call_target="tpu_custom_call" | custom-call | tf_op jit(solution)/shard_map/pallas_call | solution.py:50
  93.9 9.9 %collective-permute-done.8.refs_6_.refs_4_ = bf16[384,1024]{1,0:T(8,128)(2,1)S(1)} collective-permute-done((bf16[384,1024]{1,0:T(8,128)(2,1)S(1)}, bf16[384,1024]{1,0:T(8,128)(2,1)S(1)}, u32[]{:S(2)}, u32[]{:S(2)}) %collective-permute-start.8) | collective-permute-done | bytes 786464 | tf_op jit(solution)/shard_map/ppermute | solution.py:174
  103.9 7.4 %shard_map.229 = (f32[512,1024]{1,0:T(8,128)}, f32[512,1024]{1,0:T(8,128)}, bf16[512,1024]{1,0:T(8,128)(2,1)}) custom-call(s32[5]{0:T(128)S(1)} %concatenate.17.offsets, bf16[512,1024]{1,0:T(8,128)(2,1)S(1)} %shard_map.228.refs_0_.refs_4_, bf16[512,1024]{1,0:T(8,128)(2,1)S(1)} %collective-permute-done.7.refs_1_, ...), custom_call_target="tpu_custom_call" | custom-call | tf_op jit(solution)/shard_map/pallas_call | solution.py:50
  112.3 3.2 %collective-permute-start.12 = (f32[2,1024]{1,0:T(2,128)S(1)}, f32[2,1024]{1,0:T(2,128)S(1)}, u32[]{:S(2)}, u32[]{:S(2)}) collective-permute-start(f32[2,1024]{1,0:T(2,128)S(1)} %reshape.53), channel_id=1, source_target_pairs={{0,4},{4,0},{8,12},{12,8},{1,5},{5,1},{9,13},{13,9},{2,6},{6,2},{1... | collective-permute-start | bytes 24584 | tf_op jit(solution)/shard_map/ppermute | solution.py:181
  116.9 1.5 collective-permute-start.15
  118.6 1.6 collective-permute-start.13
  121.1 2.2 %collective-permute-done.13 = f32[2,1024]{1,0:T(2,128)S(1)} collective-permute-done((f32[2,1024]{1,0:T(2,128)S(1)}, f32[2,1024]{1,0:T(2,128)S(1)}, u32[]{:S(2)}, u32[]{:S(2)}) %collective-permute-start.13) | collective-permute-done | bytes 8224 | tf_op jit(solution)/shard_map/ppermute | solution.py:181
  123.9 2.5 %collective-permute-done.11.refs_1_ = bf16[512,1024]{1,0:T(8,128)(2,1)} collective-permute-done((bf16[512,1024]{1,0:T(8,128)(2,1)}, bf16[512,1024]{1,0:T(8,128)(2,1)}, u32[]{:S(2)}, u32[]{:S(2)}) %collective-permute-start.11) | collective-permute-done | bytes 1048608 | tf_op jit(solution)/shard_map/ppermute | solution.py:174
  126.4 1.2 copy-done.2
  127.6 21.0 %shard_map.231 = f32[512,1024]{1,0:T(8,128)} custom-call(s32[5]{0:T(128)S(1)} %concatenate.20.offsets, bf16[512,1024]{1,0:T(8,128)(2,1)} %get-tuple-element.47.refs_0_, bf16[512,1024]{1,0:T(8,128)(2,1)} %collective-permute-done.11.refs_1_, bf16[512,1024]{1,0:T(8,128)(2,1)S(1)} %convert_bitcast_fusion.1.refs_2_.refs_5_, bf16[512,1024]{1,0:T(8,128)(2,1)S(1)} %copy-done.2), custom_call_target="tpu_custom_call" | custom-call | tf_op jit(solution)/shard_map/pallas_call | solution.py:50
  148.9 20.8 %shard_map.232 = f32[512,1024]{1,0:T(8,128)} custom-call(s32[6]{0:T(128)S(1)} %concatenate.19.offsets, bf16[512,1024]{1,0:T(8,128)(2,1)} %get-tuple-element.46.refs_0_, bf16[512,1024]{1,0:T(8,128)(2,1)} %collective-permute-done.10.refs_1_, bf16[512,1024]{1,0:T(8,128)(2,1)S(1)} %convert_bitcast_fusion.refs_4_.refs_2_, ...), custom_call_target="tpu_custom_call" | custom-call | tf_op jit(solution)/shard_map/pallas_call | solution.py:50
  169.7 5.5 %shard_map.233 = f32[512,1024]{1,0:T(8,128)} custom-call(s32[5]{0:T(128)S(1)} %concatenate.17.offsets, bf16[512,1024]{1,0:T(8,128)(2,1)} %get-tuple-element.45.refs_0_, bf16[512,1024]{1,0:T(8,128)(2,1)} %collective-permute-done.9.refs_1_, bf16[512,1024]{1,0:T(8,128)(2,1)S(1)} %convert_bitcast_fusion.refs_4_.refs_2_, ...), custom_call_target="tpu_custom_call" | custom-call | tf_op jit(solution)/shard_map/pallas_call | solution.py:50
  (82 shorter events, 13.8 us)
Async XLA Ops:
  3.1 26.6 %collective-permute-start = (bf16[4,512,256]{2,1,0:T(8,128)(2,1)}, bf16[4,512,256]{2,1,0:T(8,128)(2,1)}, u32[]{:S(2)}, u32[]{:S(2)}) collective-permute-start(bf16[4,512,256]{2,1,0:T(8,128)(2,1)} %dynamic-slice_bitcast_fusion), channel_id=1, source_target_pairs={{0,16},{16,0},{1,17},{17,1},{2,18},{18,2},{3,19},{19,3},{4,20},{20... | collective-permute-start | bytes 3145736 | tf_op jit(solution)/shard_map/ppermute | solution.py:174
  6.3 23.4 %collective-permute-start.1 = (f32[2176]{0:T(1024)S(1)}, f32[2176]{0:T(1024)S(1)}, u32[]{:S(2)}, u32[]{:S(2)}) collective-permute-start(f32[2176]{0:T(1024)S(1)} %constant_dynamic-update-slice_fusion), channel_id=1, source_target_pairs={{0,16},{16,0},{1,17},{17,1},{2,18},{18,2},{3,19},{19,3},{4,20},{20... | collective-permute-start | bytes 26120 | tf_op jit(solution)/shard_map/ppermute | solution.py:181
  29.7 30.4 %collective-permute-start.5 = (bf16[512,1024]{1,0:T(8,128)(2,1)S(1)}, bf16[512,1024]{1,0:T(8,128)(2,1)S(1)}, u32[]{:S(2)}, u32[]{:S(2)}) collective-permute-start(bf16[512,1024]{1,0:T(8,128)(2,1)S(1)} %convert_bitcast_fusion.1.refs_2_.refs_5_), channel_id=1, source_target_pairs={{0,16},{16,0},{1,17},{17,1},{2,18},{18,2},{3,19},{19,3},{4,20},{20... | collective-permute-start | bytes 3145736 | tf_op jit(solution)/shard_map/ppermute | solution.py:174
  36.9 11.5 %collective-permute-start.2 = (bf16[512,256]{1,0:T(8,128)(2,1)}, bf16[512,256]{1,0:T(8,128)(2,1)S(1)}, u32[]{:S(2)}, u32[]{:S(2)}) collective-permute-start(bf16[512,256]{1,0:T(8,128)(2,1)} %get-tuple-element.88), channel_id=1, source_target_pairs={{0,4},{4,0},{8,12},{12,8},{1,5},{5,1},{9,13},{13,9},{2,6},{6,2},{1... | collective-permute-start | bytes 786440 | tf_op jit(solution)/shard_map/ppermute | solution.py:235
  38.5 21.6 %collective-permute-start.3 = (bf16[512,256]{1,0:T(8,128)(2,1)}, bf16[512,256]{1,0:T(8,128)(2,1)S(1)}, u32[]{:S(2)}, u32[]{:S(2)}) collective-permute-start(bf16[512,256]{1,0:T(8,128)(2,1)} %get-tuple-element.87), channel_id=1, source_target_pairs={{0,8},{4,12},{8,0},{12,4},{1,9},{5,13},{9,1},{13,5},{2,10},{6,14},... | collective-permute-start | bytes 786440 | tf_op jit(solution)/shard_map/ppermute | solution.py:235
  41.1 19.0 %collective-permute-start.4 = (bf16[512,256]{1,0:T(8,128)(2,1)}, bf16[512,256]{1,0:T(8,128)(2,1)S(1)}, u32[]{:S(2)}, u32[]{:S(2)}) collective-permute-start(bf16[512,256]{1,0:T(8,128)(2,1)} %get-tuple-element.86), channel_id=1, source_target_pairs={{0,12},{4,8},{8,4},{12,0},{1,13},{5,9},{9,5},{13,1},{2,14},{6,10},... | collective-permute-start | bytes 786440 | tf_op jit(solution)/shard_map/ppermute | solution.py:235
  41.3 18.8 %collective-permute-start.6 = (bf16[128,1024]{1,0:T(8,128)(2,1)}, bf16[128,1024]{1,0:T(8,128)(2,1)S(1)}, u32[]{:S(2)}, u32[]{:S(2)}) collective-permute-start(bf16[128,1024]{1,0:T(8,128)(2,1)} %slice_bitcast_fusion.1), channel_id=1, source_target_pairs={{0,16},{16,0},{1,17},{17,1},{2,18},{18,2},{3,19},{19,3},{4,20},{20... | collective-permute-start | bytes 786440 | tf_op jit(solution)/shard_map/ppermute | solution.py:174
  44.4 17.5 %copy-start.11 = (bf16[1,1,512,1024]{3,2,1,0:T(8,128)(2,1)S(1)}, bf16[1,1,512,1024]{3,2,1,0:T(8,128)(2,1)}, u32[]{:S(2)}) copy-start(bf16[1,1,512,1024]{3,2,1,0:T(8,128)(2,1)} %convert_element_type.26) | copy-start | bytes 3145732
  44.4 17.5 %copy-start.10 = (bf16[1,1,512,1024]{3,2,1,0:T(8,128)(2,1)S(1)}, bf16[1,1,512,1024]{3,2,1,0:T(8,128)(2,1)}, u32[]{:S(2)}) copy-start(bf16[1,1,512,1024]{3,2,1,0:T(8,128)(2,1)} %copy-done.9) | copy-start | bytes 3145732
  60.8 26.2 %collective-permute-start.7 = (bf16[512,1024]{1,0:T(8,128)(2,1)S(1)}, bf16[512,1024]{1,0:T(8,128)(2,1)S(1)}, u32[]{:S(2)}, u32[]{:S(2)}) collective-permute-start(bf16[512,1024]{1,0:T(8,128)(2,1)S(1)} %shard_map.228.refs_0_.refs_4_), channel_id=1, source_target_pairs={{0,16},{16,0},{1,17},{17,1},{2,18},{18,2},{3,19},{19,3},{4,20},{20... | collective-permute-start | bytes 3145736 | tf_op jit(solution)/shard_map/ppermute | solution.py:174
  62.0 41.8 %collective-permute-start.8 = (bf16[384,1024]{1,0:T(8,128)(2,1)S(1)}, bf16[384,1024]{1,0:T(8,128)(2,1)S(1)}, u32[]{:S(2)}, u32[]{:S(2)}) collective-permute-start(bf16[384,1024]{1,0:T(8,128)(2,1)S(1)} %slice_bitcast_fusion), channel_id=1, source_target_pairs={{0,16},{16,0},{1,17},{17,1},{2,18},{18,2},{3,19},{19,3},{4,20},{20... | collective-permute-start | bytes 2359304 | tf_op jit(solution)/shard_map/ppermute | solution.py:174
  63.2 23.8 %copy-start.6 = (f32[1,1,512,1024]{3,2,1,0:T(8,128)S(1)}, f32[1,1,512,1024]{3,2,1,0:T(8,128)}, u32[]{:S(2)}) copy-start(f32[1,1,512,1024]{3,2,1,0:T(8,128)} %param.17) | copy-start | bytes 6291460
  63.3 23.7 %copy-start.5 = (f32[1,1,512,1024]{3,2,1,0:T(8,128)S(1)}, f32[1,1,512,1024]{3,2,1,0:T(8,128)}, u32[]{:S(2)}) copy-start(f32[1,1,512,1024]{3,2,1,0:T(8,128)} %param.16) | copy-start | bytes 6291460
  87.0 16.8 %copy-start.3 = (f32[1,1,512,1024]{3,2,1,0:T(8,128)S(1)}, f32[1,1,512,1024]{3,2,1,0:T(8,128)}, u32[]{:S(2)}) copy-start(f32[1,1,512,1024]{3,2,1,0:T(8,128)} %param.14) | copy-start | bytes 6291460
  87.0 16.8 %copy-start.4 = (f32[1,1,512,1024]{3,2,1,0:T(8,128)S(1)}, f32[1,1,512,1024]{3,2,1,0:T(8,128)}, u32[]{:S(2)}) copy-start(f32[1,1,512,1024]{3,2,1,0:T(8,128)} %param.15) | copy-start | bytes 6291460
  91.9 34.5 %collective-permute-start.11 = (bf16[512,1024]{1,0:T(8,128)(2,1)}, bf16[512,1024]{1,0:T(8,128)(2,1)}, u32[]{:S(2)}, u32[]{:S(2)}) collective-permute-start(bf16[512,1024]{1,0:T(8,128)(2,1)} %get-tuple-element.47.refs_0_), channel_id=1, source_target_pairs={{0,16},{16,0},{1,17},{17,1},{2,18},{18,2},{3,19},{19,3},{4,20},{20... | collective-permute-start | bytes 3145736 | tf_op jit(solution)/shard_map/ppermute | solution.py:174
  93.0 55.9 %collective-permute-start.10 = (bf16[512,1024]{1,0:T(8,128)(2,1)}, bf16[512,1024]{1,0:T(8,128)(2,1)}, u32[]{:S(2)}, u32[]{:S(2)}) collective-permute-start(bf16[512,1024]{1,0:T(8,128)(2,1)} %get-tuple-element.46.refs_0_), channel_id=1, source_target_pairs={{0,16},{16,0},{1,17},{17,1},{2,18},{18,2},{3,19},{19,3},{4,20},{20... | collective-permute-start | bytes 3145736 | tf_op jit(solution)/shard_map/ppermute | solution.py:174
  103.8 19.4 %copy-start.12 = (f32[1,2,1024]{2,1,0:T(2,128)S(1)}, f32[1,2,1024]{2,1,0:T(2,128)}, u32[]{:S(2)}) copy-start(f32[1,2,1024]{2,1,0:T(2,128)} %param.21) | copy-start | bytes 24580
  103.8 19.4 %copy-start.13 = (f32[1,2,1024]{2,1,0:T(2,128)S(1)}, f32[1,2,1024]{2,1,0:T(2,128)}, u32[]{:S(2)}) copy-start(f32[1,2,1024]{2,1,0:T(2,128)} %param.22) | copy-start | bytes 24580
  111.2 58.4 %collective-permute-start.9 = (bf16[512,1024]{1,0:T(8,128)(2,1)}, bf16[512,1024]{1,0:T(8,128)(2,1)}, u32[]{:S(2)}, u32[]{:S(2)}) collective-permute-start(bf16[512,1024]{1,0:T(8,128)(2,1)} %get-tuple-element.45.refs_0_), channel_id=1, source_target_pairs={{0,16},{16,0},{1,17},{17,1},{2,18},{18,2},{3,19},{19,3},{4,20},{20... | collective-permute-start | bytes 3145736 | tf_op jit(solution)/shard_map/ppermute | solution.py:174
  112.3 6.3 %collective-permute-start.12 = (f32[2,1024]{1,0:T(2,128)S(1)}, f32[2,1024]{1,0:T(2,128)S(1)}, u32[]{:S(2)}, u32[]{:S(2)}) collective-permute-start(f32[2,1024]{1,0:T(2,128)S(1)} %reshape.53), channel_id=1, source_target_pairs={{0,4},{4,0},{8,12},{12,8},{1,5},{5,1},{9,13},{13,9},{2,6},{6,2},{1... | collective-permute-start | bytes 24584 | tf_op jit(solution)/shard_map/ppermute | solution.py:181
  115.7 1.2 collective-permute-start.14
  116.9 3.6 %collective-permute-start.15 = (f32[32,4]{0,1:T(4,128)S(1)}, f32[32,4]{0,1:T(4,128)S(1)}, u32[]{:S(2)}, u32[]{:S(2)}) collective-permute-start(f32[32,4]{0,1:T(4,128)S(1)} %add.83), channel_id=1, source_target_pairs={{0,2},{1,3},{2,0},{3,1},{4,6},{5,7},{6,4},{7,5},{8,10},{9,11},{10,... | collective-permute-start | bytes 1544 | tf_op jit(solution)/shard_map/ppermute | solution.py:181
  118.6 4.7 %collective-permute-start.13 = (f32[2,1024]{1,0:T(2,128)S(1)}, f32[2,1024]{1,0:T(2,128)S(1)}, u32[]{:S(2)}, u32[]{:S(2)}) collective-permute-start(f32[2,1024]{1,0:T(2,128)S(1)} %add.77), channel_id=1, source_target_pairs={{0,8},{4,12},{8,0},{12,4},{1,9},{5,13},{9,1},{13,5},{2,10},{6,14},... | collective-permute-start | bytes 24584 | tf_op jit(solution)/shard_map/ppermute | solution.py:181
  (10 other events, 58.4 us)

commit v2 on v1

v2 whole, which is shorter than its diff:
```python
import functools

import jax
import jax.numpy as jnp
from jax import lax
from jax.experimental import pallas as pl
from jax.experimental.pallas import tpu as pltpu
from jax.sharding import PartitionSpec as P

NS_ITERS = 3

beta_first = 0.9
beta_second = 0.95
beta_stat = 0.95
adam_eps = 1e-08
norm_eps = 1e-06
step_count = 10.0

f32 = jnp.float32
bf16 = jnp.bfloat16
MIB = 1024 * 1024

NN = (((1,), (0,)), ((), ()))
NT = (((1,), (1,)), ((), ()))
TN = (((0,), (0,)), ((), ()))


def product(left, right, dims=NN):
    return lax.dot_general(left, right, dims, preferred_element_type=f32)


def adam_direction(first, second):
    first_hat = first / (1.0 - beta_first**step_count)
    second_hat = second / (1.0 - beta_second**step_count)
    return first_hat / (jnp.sqrt(second_hat) + adam_eps)


def tiles(extent, most=256):
    size = min(extent, most)
    return [slice(start, start + size) for start in range(0, extent, size)]


def join(whole, offsets, pieces):
    for place, piece in enumerate(pieces):
        count = piece.shape[0]
        whole[pl.ds(pl.multiple_of(offsets[place], count), count), :] = piece[...]


def call(kernel, outs, scratch, *operands):
    return pl.pallas_call(
        kernel,
        out_shape=outs,
        in_specs=[pl.BlockSpec(memory_space=pltpu.SMEM)]
        + [pl.BlockSpec(memory_space=pltpu.VMEM)] * (len(operands) - 1),
        out_specs=[pl.BlockSpec(memory_space=pltpu.VMEM)] * len(outs),
        scratch_shapes=scratch,
        compiler_params=pltpu.CompilerParams(vmem_limit_bytes=40 * MIB),
    )(*operands)


def shape(rows, columns, dtype):
    return jax.ShapeDtypeStruct((rows, columns), dtype)


def assemble_kernel(width, places, *refs):
    *blocks, out = refs
    for place, block in enumerate(blocks):
        out[:, pl.ds(pl.multiple_of(places[place], width), width)] = block[...]


def place_kernel(start, side, part, left_in, right_in, left, right, wide, sem):
    del left_in, right_in
    wide[...] = part[...].astype(f32)
    here = pl.ds(start, part.shape[0])

    @pl.when(side[0] == 1)
    def _():
        copy = pltpu.make_async_copy(wide, right.at[here], sem)
        copy.start()
        copy.wait()

    @pl.when(side[0] != 1)
    def _():
        copy = pltpu.make_async_copy(wide, left.at[here], sem)
        copy.start()
        copy.wait()


def place(side, part, start, left, right):
    anywhere = pl.BlockSpec(memory_space=pl.ANY)
    return pl.pallas_call(
        functools.partial(place_kernel, start),
        out_shape=[shape(*left.shape, f32)] * 2,
        in_specs=[
            pl.BlockSpec(memory_space=pltpu.SMEM),
            pl.BlockSpec(memory_space=pltpu.VMEM),
            anywhere,
            anywhere,
        ],
        out_specs=[anywhere, anywhere],
        scratch_shapes=[pltpu.VMEM(part.shape, f32), pltpu.SemaphoreType.DMA],
        input_output_aliases={2: 0, 3: 1},
    )(side, part, left, right)


def basis_kernel(n_left, n_right, offsets, *refs):
    left_pieces, right_pieces = refs[:n_left], refs[n_left : n_left + n_right]
    out = refs[-1]
    left_side = offsets[n_left + n_right] == 1

    @pl.when(left_side)
    def _():
        join(out, [offsets[i] for i in range(n_left)], left_pieces)

    @pl.when(jnp.logical_not(left_side))
    def _():
        join(out, [offsets[n_left + i] for i in range(n_right)], right_pieces)


def stats_kernel(n, offsets, *refs):
    pieces, column_pieces = refs[:n], refs[n : 2 * n]
    rows_ref, left_stat, right_stat = refs[2 * n : 2 * n + 3]
    left_next, right_next, keep, send, grad, columns = refs[2 * n + 3 :]
    join(grad, offsets, pieces)
    join(columns, offsets, column_pieces)
    for at in tiles(rows_ref.shape[0]):
        left_next[at] = beta_stat * left_stat[at] + product(rows_ref[at], grad[...], NT)
    for at in tiles(rows_ref.shape[0]):
        right_next[at] = beta_stat * right_stat[at] + product(columns[:, at], grad[...], TN)
    left_side = offsets[n] == 1

    @pl.when(left_side)
    def _():
        keep[...] = left_next[...].astype(bf16)
        send[...] = right_next[...].astype(bf16)

    @pl.when(jnp.logical_not(left_side))
    def _():
        keep[...] = right_next[...].astype(bf16)
        send[...] = left_next[...].astype(bf16)


def moments_kernel(n, offsets, *refs):
    pieces, column_pieces, right_pieces = refs[:n], refs[n : 2 * n], refs[2 * n : 3 * n]
    first, second = refs[3 * n : 3 * n + 2]
    first_next, second_next, direction, grad, columns, right, rotated_half = refs[3 * n + 2 :]
    join(grad, offsets, pieces)
    join(columns, offsets, column_pieces)
    join(right, offsets, right_pieces)
    for at in tiles(grad.shape[0]):
        rotated_half[at] = product(grad[at], right[...]).astype(bf16)
    for at in tiles(first.shape[0]):
        rotated = product(columns[:, at], rotated_half[...], TN)
        first_new = beta_first * first[at] + (1.0 - beta_first) * rotated
        second_new = beta_second * second[at] + (1.0 - beta_second) * rotated * rotated
        first_next[at] = first_new
        second_next[at] = second_new
        direction[at] = adam_direction(first_new, second_new).astype(bf16)


def update_kernel(n, offsets, *refs):
    pieces, right_pieces, rows_ref = refs[:n], refs[n : 2 * n], refs[2 * n]
    update, direction, right = refs[2 * n + 1 :]
    join(direction, offsets, pieces)
    join(right, offsets, right_pieces)
    for at in tiles(rows_ref.shape[0]):
        back_half = product(rows_ref[at], direction[...]).astype(bf16)
        update[at] = product(back_half, right[...], NT)


def rotation_kernel(ns, n_out, offsets, *refs):
    stat_pieces, basis, outs = refs[:ns], refs[ns], refs[ns + 1 : ns + 1 + n_out]
    stat, iterate, half_a, half_b = refs[ns + 1 + n_out :]
    join(stat, offsets, stat_pieces)
    squares = jnp.zeros((), f32)
    for at in tiles(stat.shape[0]):
        power = product(stat[at], basis[...])
        iterate[at] = power
        squares += jnp.sum(power * power)
    scale = 1.0 / jnp.sqrt(squares + norm_eps)
    for at in tiles(stat.shape[0]):
        value = iterate[at] * scale
        iterate[at] = value
        half_a[at] = value.astype(bf16)

    def step(source, at):
        gram = product(source[at], source[...], NT).astype(bf16)
        return 1.5 * iterate[at] - 0.5 * product(gram, source[...])

    source, target = half_a, half_b
    for sweep in range(NS_ITERS - 1):
        for at in tiles(stat.shape[0]):
            value = step(source, at)
            iterate[at] = value
            target[at] = value.astype(bf16)
        source, target = target, source
    for place, out in enumerate(outs):
        for at in tiles(out.shape[0]):
            size = at.stop - at.start
            here = pl.ds(pl.multiple_of(offsets[ns + place] + at.start, size), size)
            out[at] = step(source, here).astype(out.dtype)


def build(mesh):
    n_dp, n_tensor, n_section = mesh.shape["dp"], mesh.shape["tensor"], mesh.shape["section"]
    pair = n_dp == 2

    def swap(value):
        return lax.ppermute(value, "dp", [(0, 1), (1, 0)])

    def total(value, axis, count):
        if count & (count - 1):
            return lax.psum(value, axis)
        step = 1
        while step < count:
            value = value + lax.ppermute(value, axis, [(i, i ^ step) for i in range(count)])
            step *= 2
        return value

    def after(value, *others):
        return lax.optimization_barrier((value,) + others)[0]

    def local(
        grad_parts,
        first_moment,
        second_moment,
        left_stat,
        right_stat,
        left_basis,
        right_basis,
        gain_grads,
        gain_first,
        gain_second,
        table_grads,
        table_first,
        table_second,
    ):
        partial_value = grad_parts[0, 0]
        mats, extent, width = partial_value.shape
        rows = left_basis.shape[2]
        dp = lax.axis_index("dp")
        rank = lax.axis_index("tensor")
        own = dp * rows
        other = (n_dp - 1 - dp) * rows

        def columns_of(pieces):
            return [lax.dynamic_slice_in_dim(piece, own, rows, 1) for piece in pieces]

        gain_part = gain_grads[0, 0, 0]
        table_part = table_grads[0, 0]
        both = jnp.concatenate([gain_part.reshape(-1), table_part.reshape(-1)])
        both = total(both, "dp", n_dp)

        if pair:
            section = lax.axis_index("section")
            left_side = (dp == section % 2).astype(jnp.int32)
            left_local = left_basis[0, 0].astype(bf16)
            right_local = right_basis[0, 0].astype(bf16)
            last = None
            blocks = [None] * n_tensor
            for step in reversed(range(n_tensor)):
                mine = lax.dynamic_index_in_dim(partial_value, rank ^ step, 0, keepdims=False)
                sent = lax.dynamic_slice_in_dim(mine, other, rows, 0)
                got = swap(sent)
                if last is None:
                    left_local_out = after(left_local, got)
                else:
                    got = after(got, last)
                block = lax.dynamic_slice_in_dim(mine, own, rows, 0).astype(f32) + got.astype(f32)
                last = block = block.astype(bf16)
                if step:
                    block = lax.ppermute(
                        block, "tensor", [(i, i ^ step) for i in range(n_tensor)]
                    )
                blocks[step] = block
            left_cross_out = lax.dynamic_slice_in_dim(left_local_out, other, rows, 1)
            left_cross = swap(left_cross_out)
            left_rest = lax.ppermute(
                lax.dynamic_slice_in_dim(left_local_out, own, rows, 1),
                ("dp", "section"),
                [
                    ((1 - s % 2) * n_section + s, (s % 2) * n_section + s)
                    for s in range(n_section)
                ],
            )
            head = rows // 4
            right_head = swap(after(right_local[:head], last))
            places = jnp.stack([(rank ^ step) * width for step in range(n_tensor)])
            *blocks, both, left_cross, left_rest = lax.optimization_barrier(
                (*blocks, both, left_cross, left_rest)
            )
            (grad_rows,) = call(
                functools.partial(assemble_kernel, width),
                [shape(rows, extent, bf16)],
                [],
                places,
                *blocks,
            )
            grad_other, right_head = lax.optimization_barrier((swap(grad_rows), right_head))
            right_other = jnp.concatenate(
                [right_head, swap(after(right_local[head:], grad_rows))], axis=0
            )
            grad_pieces = [grad_rows, grad_other]
            right_pieces = [right_local, right_other]
            offsets = jnp.stack([own, other])
            left_columns = [lax.dynamic_slice_in_dim(left_local, own, rows, 1), left_cross]
        else:
            columns = lax.all_to_all(partial_value, "tensor", split_axis=0, concat_axis=2, tiled=True)
            summed = lax.psum_scatter(columns, "dp", scatter_dimension=1, tiled=True)
            grad_rows = summed[0]
            left_local = left_basis[0, 0].astype(bf16)
            right_local = right_basis[0, 0].astype(bf16)

            def gather(value):
                return [lax.all_gather(value, "dp", axis=0, tiled=True)]

            grad_pieces, left_pieces, right_pieces = (
                gather(grad_rows),
                gather(left_local),
                gather(right_local),
            )
            offsets = jnp.zeros((1,), jnp.int32)
            left_columns = columns_of(left_pieces)
            left_side = jnp.int32(1)
        gain_sum = total(both[: gain_part.size].reshape(gain_part.shape), "tensor", n_tensor)
        table_sum = total(both[gain_part.size :].reshape(table_part.shape), "section", n_section)
        grad_pieces[-1], gain_sum, table_sum = lax.optimization_barrier(
            (grad_pieces[-1], gain_sum, table_sum)
        )
        n = len(grad_pieces)
        square = pltpu.VMEM((extent, extent), bf16)
        strip = pltpu.VMEM((extent, rows), bf16)

        left_new, right_new, stat_keep, stat_send = call(
            functools.partial(stats_kernel, n),
            [shape(rows, extent, f32)] * 2 + [shape(rows, extent, bf16)] * 2,
            [square, strip],
            jnp.concatenate([offsets, left_side[None]]),
            *grad_pieces,
            *columns_of(grad_pieces),
            grad_rows,
            left_stat[0, 0],
            right_stat[0, 0],
        )
        stat_other = swap(stat_send) if pair else None
        first_new, second_new, direction = call(
            functools.partial(moments_kernel, n),
            [shape(rows, extent, f32)] * 2 + [shape(rows, extent, bf16)],
            [square, strip, square, square],
            offsets,
            *grad_pieces,
            *left_columns,
            *right_pieces,
            first_moment[0, 0],
            second_moment[0, 0],
        )
        direction_pieces = [direction, swap(direction)] if pair else gather(direction)

        def rotation(stat_pieces, basis, outs, bases):
            return call(
                functools.partial(rotation_kernel, len(stat_pieces), len(outs)),
                outs,
                [square, pltpu.VMEM((extent, extent), f32), square, square],
                jnp.concatenate([offsets, jnp.stack(bases)]),
                *stat_pieces,
                basis,
            )

        own_rows = shape(rows, extent, f32)
        if pair:
            left_other = jnp.where(
                own < rows,
                jnp.concatenate([left_cross, left_rest], axis=1),
                jnp.concatenate([left_rest, left_cross], axis=1),
            )
            (basis,) = call(
                functools.partial(basis_kernel, n, n),
                [shape(extent, extent, bf16)],
                [],
                jnp.concatenate([offsets, offsets, left_side[None]]),
                left_local,
                left_other,
                *right_pieces,
            )
            basis = after(basis, direction)
            rotation_own, rotation_send = rotation(
                [stat_keep, stat_other],
                basis,
                [own_rows, shape(rows, extent, bf16)],
                [own, other],
            )
            direction_pieces[1] = after(direction_pieces[1], rotation_send)
            cut = rows * 3 // 4
            rotation_parts = [swap(rotation_send[:cut])]
            rotation_parts.append(swap(rotation_send[cut:]))
            left_rotation, right_rotation = rotation_own, rotation_own
        else:
            (left_rotation,) = rotation(gather(stat_keep), left_pieces[0], [own_rows], [own])
            (right_rotation,) = rotation(gather(stat_send), right_pieces[0], [own_rows], [own])
        (update,) = call(
            functools.partial(update_kernel, n),
            [own_rows],
            [square, square],
            offsets,
            *direction_pieces,
            *right_pieces,
            left_local,
        )
        if pair:
            rotation_parts[0] = after(rotation_parts[0], update)
            for start, part in zip((0, cut), rotation_parts):
                left_rotation, right_rotation = place(
                    left_side[None], part, start, left_rotation, right_rotation
                )

        gain_moment = beta_first * gain_first[0] + (1.0 - beta_first) * gain_sum
        gain_squares = beta_second * gain_second[0] + (1.0 - beta_second) * gain_sum * gain_sum
        gain_update = adam_direction(gain_moment, gain_squares)
        table_moment = beta_first * table_first + (1.0 - beta_first) * table_sum
        table_squares = beta_second * table_second + (1.0 - beta_second) * table_sum * table_sum
        table_update = adam_direction(table_moment, table_squares)
        return (
            update[None, None],
            first_new[None, None],
            second_new[None, None],
            left_new[None, None],
            right_new[None, None],
            left_rotation[None, None],
            right_rotation[None, None],
            gain_update[None],
            gain_moment[None],
            gain_squares[None],
            table_update,
            table_moment,
            table_squares,
        )

    return local


def solution(mesh):
    state = P("section", "tensor", "dp", None)
    gains = P("section", None, None)
    table = P(None, "tensor")
    return jax.shard_map(
        build(mesh),
        mesh=mesh,
        in_specs=(P("section", "dp", None, None, "tensor"),)
        + (state,) * 6
        + (P("section", "dp", "tensor", None, None), gains, gains)
        + (P("section", "dp", None, "tensor"), table, table),
        out_specs=(state,) * 7 + (gains,) * 3 + (table,) * 3,
        check_vma=False,
    )
```

time: 176 us -> 165 us (0.938)
  Pallas kernels: 60.1 us -> 42.7 us
  starting transfers between devices: 21 us -> 30.4 us
  waiting for transfers between devices: 77.6 us -> 71.6 us
  other arithmetic: 7.96 us -> 10.3 us
    ppermute x5, waiting for transfers between devices: 26.8 us -> 3.19 us  [total(): lax.ppermute(value, axis, [(i, i ^ step) for i in range(count)])]
    ppermute x8 -> x12, waiting for transfers between devices: 35.2 us -> 58.4 us  [swap(): return lax.ppermute(value, 'dp', [(0, 1), (1, 0)])]
    pallas_call x6, Pallas kernels: 60.1 us -> 38.5 us  [call(): pl.pallas_call(kernel, out_shape=outs, in_specs=[pl.BlockSpec(memory_spac...]
    ppermute x3, waiting for transfers between devices: 15.6 us -> 9.36 us  [local(): lax.ppermute(block, 'tensor', [(i, i ^ step) for i in range(n_tensor)])]
    pallas_call x0 -> x2, Pallas kernels: none -> 4.17 us  [place(): pl.pallas_call(functools.partial(place_kernel, start), out_shape=[shape(*...]
    ppermute x8 -> x12, starting transfers between devices: 10.2 us -> 13.6 us  [swap(): return lax.ppermute(value, 'dp', [(0, 1), (1, 0)])]
    ppermute x3, starting transfers between devices: 4.39 us -> 7.39 us  [local(): lax.ppermute(block, 'tensor', [(i, i ^ step) for i in range(n_tensor)])]
    convert_element_type x1 -> x4, other arithmetic: 1.78 us -> 4.44 us  [local(): last = block = block.astype(bf16)]
  transfers between devices with their start and end apart: 16 -> 21, of which waited for: 10 -> 12; matrix products, arithmetic and copies ran while one was open for 6% -> 9% of each run, Pallas kernels for 31% -> 24%
where the time goes in v2:
time: 165 us
  waiting for transfers between devices  71.6 us (43%)
  Pallas kernels  42.7 us (26%)
  starting transfers between devices  30.4 us (18%)
  other arithmetic  10.3 us (6%)
  local copies, waits for them, and re-layouts  8.64 us (5%)
    ppermute x12, waiting for transfers between devices, swap(): return lax.ppermute(value, 'dp', [(0, 1), (1, 0)])  58.4 us
    pallas_call x6, Pallas kernels, call(): pl.pallas_call(kernel, out_shape=outs, in_specs=[pl.BlockSpec(memory_spac...  38.5 us
    ppermute x12, starting transfers between devices, swap(): return lax.ppermute(value, 'dp', [(0, 1), (1, 0)])  13.6 us
    ppermute x3, waiting for transfers between devices, local(): lax.ppermute(block, 'tensor', [(i, i ^ step) for i in range(n_tensor)])  9.36 us
    ppermute x5, starting transfers between devices, total(): lax.ppermute(value, axis, [(i, i ^ step) for i in range(count)])  8.11 us
    ppermute x3, starting transfers between devices, local(): lax.ppermute(block, 'tensor', [(i, i ^ step) for i in range(n_tensor)])  7.39 us
    convert_element_type x4, other arithmetic, local(): last = block = block.astype(bf16)  4.44 us
    pallas_call x2, Pallas kernels, place(): pl.pallas_call(functools.partial(place_kernel, start), out_shape=[shape(*...  4.17 us
  transfers between devices with their start and end apart: 21, of which 12 were waited for; matrix products, arithmetic and copies ran while one was open for 9% of the time, Pallas kernels for 24%

profile of v2, /device:TPU:0, one launch (start us, length us, event | category | flops | bytes accessed | tf_op | source)
XLA Modules:
  0.0 164.9 jit_solution(14454372415014672662)
XLA Ops:
  0.7 2.5 %dynamic-slice_bitcast_fusion.1 = (bf16[512,256]{1,0:T(8,128)(2,1)}, bf16[512,256]{1,0:T(8,128)(2,1)}, bf16[512,256]{1,0:T(8,128)(2,1)}, bf16[512,256]{1,0:T(8,128)(2,1)}) fusion(bf16[1,1,4,1024,256]{4,3,2,1,0:T(8,128)(2,1)} %param.13, s32[]{:T(128)S(6)} %select_n.68, s32[]{:T(128)S(6)} %select_n.62, s32[]{:T(128)S(6)} %select_n.66, s32[]{:T(128)S(6)} %select_n.64, ...), kind=kLoop, calls=%fused_computation.12 | loop fusion | bytes 2097172 | tf_op jit(solution)/shard_map/dynamic_slice | solution.py:263
  3.2 2.9 %collective-permute-start.3 = (bf16[512,256]{1,0:T(8,128)(2,1)}, bf16[512,256]{1,0:T(8,128)(2,1)}, u32[]{:S(2)}, u32[]{:S(2)}) collective-permute-start(bf16[512,256]{1,0:T(8,128)(2,1)} %get-tuple-element.110), channel_id=1, source_target_pairs={{0,16},{16,0},{1,17},{17,1},{2,18},{18,2},{3,19},{19,3},{4,20},{20... | collective-permute-start | bytes 786440 | tf_op jit(solution)/shard_map/ppermute | solution.py:209
  6.2 2.0 %collective-permute-start.1 = (bf16[512,256]{1,0:T(8,128)(2,1)}, bf16[512,256]{1,0:T(8,128)(2,1)}, u32[]{:S(2)}, u32[]{:S(2)}) collective-permute-start(bf16[512,256]{1,0:T(8,128)(2,1)} %get-tuple-element.112), channel_id=1, source_target_pairs={{0,16},{16,0},{1,17},{17,1},{2,18},{18,2},{3,19},{19,3},{4,20},{20... | collective-permute-start | bytes 786440 | tf_op jit(solution)/shard_map/ppermute | solution.py:209
  8.4 2.0 %collective-permute-start.7 = (f32[2176]{0:T(1024)S(1)}, f32[2176]{0:T(1024)S(1)}, u32[]{:S(2)}, u32[]{:S(2)}) collective-permute-start(f32[2176]{0:T(1024)S(1)} %constant_dynamic-update-slice_fusion.2), channel_id=1, source_target_pairs={{0,16},{16,0},{1,17},{17,1},{2,18},{18,2},{3,19},{19,3},{4,20},{20... | collective-permute-start | bytes 26120 | tf_op jit(solution)/shard_map/ppermute | solution.py:216
  10.6 2.9 %collective-permute-done.3 = bf16[512,256]{1,0:T(8,128)(2,1)} collective-permute-done((bf16[512,256]{1,0:T(8,128)(2,1)}, bf16[512,256]{1,0:T(8,128)(2,1)}, u32[]{:S(2)}, u32[]{:S(2)}) %collective-permute-start.3) | collective-permute-done | bytes 262176 | tf_op jit(solution)/shard_map/ppermute | solution.py:209
  14.7 4.5 %collective-permute-done.2 = bf16[512,256]{1,0:T(8,128)(2,1)} collective-permute-done((bf16[512,256]{1,0:T(8,128)(2,1)}, bf16[512,256]{1,0:T(8,128)(2,1)}, u32[]{:S(2)}, u32[]{:S(2)}) %collective-permute-start.2) | collective-permute-done | bytes 262176 | tf_op jit(solution)/shard_map/ppermute | solution.py:209
  20.3 3.2 %collective-permute-start.5 = (bf16[512,256]{1,0:T(8,128)(2,1)S(1)}, bf16[512,256]{1,0:T(8,128)(2,1)S(1)}, u32[]{:S(2)}, u32[]{:S(2)}) collective-permute-start(bf16[512,256]{1,0:T(8,128)(2,1)S(1)} %fusion.1), channel_id=1, source_target_pairs={{0,8},{4,12},{8,0},{12,4},{1,9},{5,13},{9,1},{13,5},{2,10},{6,14},... | collective-permute-start | bytes 786440 | tf_op jit(solution)/shard_map/ppermute | solution.py:272
  24.8 2.1 %collective-permute-start.8 = (bf16[512,512]{1,0:T(8,128)(2,1)S(1)}, bf16[512,512]{1,0:T(8,128)(2,1)S(1)}, u32[]{:S(2)}, u32[]{:S(2)}) collective-permute-start(bf16[512,512]{1,0:T(8,128)(2,1)S(1)} %get-tuple-element.115), channel_id=1, source_target_pairs={{0,16},{16,0},{1,17},{17,1},{2,18},{18,2},{3,19},{19,3},{4,20},{20... | collective-permute-start | bytes 1572872 | tf_op jit(solution)/shard_map/ppermute | solution.py:209
  30.6 4.2 %collective-permute-start.6 = (bf16[512,256]{1,0:T(8,128)(2,1)S(1)}, bf16[512,256]{1,0:T(8,128)(2,1)S(1)}, u32[]{:S(2)}, u32[]{:S(2)}) collective-permute-start(bf16[512,256]{1,0:T(8,128)(2,1)S(1)} %fusion), channel_id=1, source_target_pairs={{0,12},{4,8},{8,4},{12,0},{1,13},{5,9},{9,5},{13,1},{2,14},{6,10},... | collective-permute-start | bytes 786440 | tf_op jit(solution)/shard_map/ppermute | solution.py:272
  35.9 9.4 %collective-permute-done.4.refs_1_ = bf16[512,256]{1,0:T(8,128)(2,1)S(1)} collective-permute-done((bf16[512,256]{1,0:T(8,128)(2,1)S(1)}, bf16[512,256]{1,0:T(8,128)(2,1)S(1)}, u32[]{:S(2)}, u32[]{:S(2)}) %collective-permute-start.4) | collective-permute-done | bytes 262176 | tf_op jit(solution)/shard_map/ppermute | solution.py:272
  53.5 1.9 %convert_element_type.75 = bf16[1,1,512,1024]{3,2,1,0:T(8,128)(2,1)S(1)} convert(f32[1,1,512,1024]{3,2,1,0:T(8,128)} %param.18) | non-fusion elementwise | flops 524288 | bytes 3145728 | tf_op jit(solution)/shard_map/convert_element_type | solution.py:257
  57.7 2.7 %collective-permute-start.13 = (f32[2,1024]{1,0:T(2,128)S(1)}, f32[2,1024]{1,0:T(2,128)S(1)}, u32[]{:S(2)}, u32[]{:S(2)}) collective-permute-start(f32[2,1024]{1,0:T(2,128)S(1)} %add.136), channel_id=1, source_target_pairs={{0,8},{4,12},{8,0},{12,4},{1,9},{5,13},{9,1},{13,5},{2,10},{6,14},... | collective-permute-start | bytes 24584 | tf_op jit(solution)/shard_map/ppermute | solution.py:216
  60.5 1.9 %collective-permute-done.13 = f32[2,1024]{1,0:T(2,128)S(1)} collective-permute-done((f32[2,1024]{1,0:T(2,128)S(1)}, f32[2,1024]{1,0:T(2,128)S(1)}, u32[]{:S(2)}, u32[]{:S(2)}) %collective-permute-start.13) | collective-permute-done | bytes 8224 | tf_op jit(solution)/shard_map/ppermute | solution.py:216
  62.4 16.7 %collective-permute-done.11 = bf16[128,1024]{1,0:T(8,128)(2,1)S(1)} collective-permute-done((bf16[128,1024]{1,0:T(8,128)(2,1)}, bf16[128,1024]{1,0:T(8,128)(2,1)S(1)}, u32[]{:S(2)}, u32[]{:S(2)}) %collective-permute-start.11) | collective-permute-done | bytes 262176 | tf_op jit(solution)/shard_map/ppermute | solution.py:209
  79.2 5.7 %shard_map.230 = (f32[512,1024]{1,0:T(8,128)}, f32[512,1024]{1,0:T(8,128)}, bf16[512,1024]{1,0:T(8,128)(2,1)S(1)}, bf16[512,1024]{1,0:T(8,128)(2,1)}) custom-call(s32[3]{0:T(128)S(1)} %pad_add_fusion.3.offsets, bf16[512,1024]{1,0:T(8,128)(2,1)S(1)} %shard_map.228.refs_0_.refs_4_, bf16[512,1024]{1,0:T(8,128)(2,1)S(1)} %collective-permute-done.10.refs_1_, ...), custom_call_target="tpu_custom_call" | custom-call | tf_op jit(solution)/shard_map/pallas_call | solution.py:50
  86.1 9.9 %collective-permute-done.16 = bf16[384,1024]{1,0:T(8,128)(2,1)S(1)} collective-permute-done((bf16[384,1024]{1,0:T(8,128)(2,1)S(1)}, bf16[384,1024]{1,0:T(8,128)(2,1)S(1)}, u32[]{:S(2)}, u32[]{:S(2)}) %collective-permute-start.16) | collective-permute-done | bytes 786464 | tf_op jit(solution)/shard_map/ppermute | solution.py:209
  96.1 7.4 %shard_map.229 = (f32[512,1024]{1,0:T(8,128)}, f32[512,1024]{1,0:T(8,128)}, bf16[512,1024]{1,0:T(8,128)(2,1)}) custom-call(s32[2]{0:T(128)S(1)} %pad_add_fusion.offsets, bf16[512,1024]{1,0:T(8,128)(2,1)S(1)} %shard_map.228.refs_0_.refs_4_, bf16[512,1024]{1,0:T(8,128)(2,1)S(1)} %copy-done.3, bf16[512,512]{1,0:T(8,128)(2,1)S(1)} %dynamic-slice_bitcast_fusion.refs_2_, ...), custom_call_target="tpu_custom_call" | custom-call | tf_op jit(solution)/shard_map/pallas_call | solution.py:50
  104.4 1.9 %maximum_select_fusion.refs_1_ = bf16[512,1024]{1,0:T(8,128)(2,1)S(1)} fusion(bf16[512,512]{1,0:T(8,128)(2,1)} %collective-permute-done.9, bf16[512,512]{1,0:T(8,128)(2,1)} %copy-done.6, pred[]{:T(512)S(6)} %lt.46), kind=kLoop, calls=%fused_computation | loop fusion | flops 4718592 | bytes 2097153 | tf_op jit(solution)/shard_map/jit(_where)/select_n | solution.py:371
  107.2 11.4 %collective-permute-done.18.refs_1_ = bf16[512,1024]{1,0:T(8,128)(2,1)} collective-permute-done((bf16[512,1024]{1,0:T(8,128)(2,1)}, bf16[512,1024]{1,0:T(8,128)(2,1)}, u32[]{:S(2)}, u32[]{:S(2)}) %collective-permute-start.18) | collective-permute-done | bytes 1048608 | tf_op jit(solution)/shard_map/ppermute | solution.py:209
  118.6 18.3 %shard_map.232 = (f32[512,1024]{1,0:T(8,128)}, bf16[512,1024]{1,0:T(8,128)(2,1)S(1)}) custom-call(s32[4]{0:T(128)S(1)} %pad_add_fusion.2.offsets, bf16[512,1024]{1,0:T(8,128)(2,1)S(1)} %copy-done.11, bf16[512,1024]{1,0:T(8,128)(2,1)} %collective-permute-done.18.refs_1_, bf16[1024,1024]{1,0:T(8,128)(2,1)S(1)} %shard_map.231.refs_2_), custom_call_target="tpu_custom_call" | custom-call | tf_op jit(solution)/shard_map/pallas_call | solution.py:50
  141.0 5.6 %shard_map.233 = f32[512,1024]{1,0:T(8,128)} custom-call(s32[2]{0:T(128)S(1)} %pad_add_fusion.offsets, bf16[512,1024]{1,0:T(8,128)(2,1)} %get-tuple-element.62.refs_0_, bf16[512,1024]{1,0:T(8,128)(2,1)} %collective-permute-done.17.refs_1_, bf16[512,1024]{1,0:T(8,128)(2,1)S(1)} %convert_bitcast_fusion.refs_4_.refs_2_, bf16[512,1024]{1,0:T(8,128)(2,1)S(1)} %copy-done.1, ...), custom_call_target="tpu_custom_call" | custom-call | tf_op jit(solution)/shard_map/pallas_call | solution.py:50
  148.0 9.9 %collective-permute-done.20.part = bf16[384,1024]{1,0:T(8,128)(2,1)} collective-permute-done((bf16[384,1024]{1,0:T(8,128)(2,1)S(1)}, bf16[384,1024]{1,0:T(8,128)(2,1)}, u32[]{:S(2)}, u32[]{:S(2)}) %collective-permute-start.20) | collective-permute-done | bytes 786464 | tf_op jit(solution)/shard_map/ppermute | solution.py:209
  157.9 2.4 %shard_map.234 = (f32[512,1024]{1,0:T(8,128)}, f32[512,1024]{1,0:T(8,128)}) custom-call(s32[1]{0:T(128)} %bitcast.21.side, bf16[384,1024]{1,0:T(8,128)(2,1)} %collective-permute-done.20.part, f32[512,1024]{1,0:T(8,128)} %get-tuple-element.74.left_in, f32[512,1024]{1,0:T(8,128)} %copy.54.right_in), custom_call_target="tpu_custom_call", output_to_operand_aliasing={{0}: (2, {}), {1}: (3, {})} | custom-call | tf_op jit(solution)/shard_map/pallas_call | solution.py:91
  160.3 2.0 %collective-permute-done.19.part = bf16[128,1024]{1,0:T(8,128)(2,1)S(1)} collective-permute-done((bf16[128,1024]{1,0:T(8,128)(2,1)}, bf16[128,1024]{1,0:T(8,128)(2,1)S(1)}, u32[]{:S(2)}, u32[]{:S(2)}) %collective-permute-start.19) | collective-permute-done | bytes 262176 | tf_op jit(solution)/shard_map/ppermute | solution.py:209
  (116 shorter events, 30.4 us)
Async XLA Ops:
  3.2 10.4 %collective-permute-start.3 = (bf16[512,256]{1,0:T(8,128)(2,1)}, bf16[512,256]{1,0:T(8,128)(2,1)}, u32[]{:S(2)}, u32[]{:S(2)}) collective-permute-start(bf16[512,256]{1,0:T(8,128)(2,1)} %get-tuple-element.110), channel_id=1, source_target_pairs={{0,16},{16,0},{1,17},{17,1},{2,18},{18,2},{3,19},{19,3},{4,20},{20... | collective-permute-start | bytes 786440 | tf_op jit(solution)/shard_map/ppermute | solution.py:209
  6.1 13.1 %collective-permute-start.2 = (bf16[512,256]{1,0:T(8,128)(2,1)}, bf16[512,256]{1,0:T(8,128)(2,1)}, u32[]{:S(2)}, u32[]{:S(2)}) collective-permute-start(bf16[512,256]{1,0:T(8,128)(2,1)} %get-tuple-element.111), channel_id=1, source_target_pairs={{0,16},{16,0},{1,17},{17,1},{2,18},{18,2},{3,19},{19,3},{4,20},{20... | collective-permute-start | bytes 786440 | tf_op jit(solution)/shard_map/ppermute | solution.py:209
  6.2 18.6 %collective-permute-start.1 = (bf16[512,256]{1,0:T(8,128)(2,1)}, bf16[512,256]{1,0:T(8,128)(2,1)}, u32[]{:S(2)}, u32[]{:S(2)}) collective-permute-start(bf16[512,256]{1,0:T(8,128)(2,1)} %get-tuple-element.112), channel_id=1, source_target_pairs={{0,16},{16,0},{1,17},{17,1},{2,18},{18,2},{3,19},{19,3},{4,20},{20... | collective-permute-start | bytes 786440 | tf_op jit(solution)/shard_map/ppermute | solution.py:209
  8.2 26.6 %collective-permute-start = (bf16[512,256]{1,0:T(8,128)(2,1)}, bf16[512,256]{1,0:T(8,128)(2,1)S(1)}, u32[]{:S(2)}, u32[]{:S(2)}) collective-permute-start(bf16[512,256]{1,0:T(8,128)(2,1)} %get-tuple-element.113), channel_id=1, source_target_pairs={{0,16},{16,0},{1,17},{17,1},{2,18},{18,2},{3,19},{19,3},{4,20},{20... | collective-permute-start | bytes 786440 | tf_op jit(solution)/shard_map/ppermute | solution.py:209
  8.4 22.2 %collective-permute-start.7 = (f32[2176]{0:T(1024)S(1)}, f32[2176]{0:T(1024)S(1)}, u32[]{:S(2)}, u32[]{:S(2)}) collective-permute-start(f32[2176]{0:T(1024)S(1)} %constant_dynamic-update-slice_fusion.2), channel_id=1, source_target_pairs={{0,16},{16,0},{1,17},{17,1},{2,18},{18,2},{3,19},{19,3},{4,20},{20... | collective-permute-start | bytes 26120 | tf_op jit(solution)/shard_map/ppermute | solution.py:216
  20.3 24.9 %collective-permute-start.5 = (bf16[512,256]{1,0:T(8,128)(2,1)S(1)}, bf16[512,256]{1,0:T(8,128)(2,1)S(1)}, u32[]{:S(2)}, u32[]{:S(2)}) collective-permute-start(bf16[512,256]{1,0:T(8,128)(2,1)S(1)} %fusion.1), channel_id=1, source_target_pairs={{0,8},{4,12},{8,0},{12,4},{1,9},{5,13},{9,1},{13,5},{2,10},{6,14},... | collective-permute-start | bytes 786440 | tf_op jit(solution)/shard_map/ppermute | solution.py:272
  23.6 24.6 %copy-start.14 = (f32[1,1,512,1024]{3,2,1,0:T(8,128)S(1)}, f32[1,1,512,1024]{3,2,1,0:T(8,128)}, u32[]{:S(2)}) copy-start(f32[1,1,512,1024]{3,2,1,0:T(8,128)} %param.19) | copy-start | bytes 6291460
  24.8 20.4 %collective-permute-start.8 = (bf16[512,512]{1,0:T(8,128)(2,1)S(1)}, bf16[512,512]{1,0:T(8,128)(2,1)S(1)}, u32[]{:S(2)}, u32[]{:S(2)}) collective-permute-start(bf16[512,512]{1,0:T(8,128)(2,1)S(1)} %get-tuple-element.115), channel_id=1, source_target_pairs={{0,16},{16,0},{1,17},{17,1},{2,18},{18,2},{3,19},{19,3},{4,20},{20... | collective-permute-start | bytes 1572872 | tf_op jit(solution)/shard_map/ppermute | solution.py:209
  26.9 19.8 %collective-permute-start.9 = (bf16[512,512]{1,0:T(8,128)(2,1)S(1)}, bf16[512,512]{1,0:T(8,128)(2,1)}, u32[]{:S(2)}, u32[]{:S(2)}) collective-permute-start(bf16[512,512]{1,0:T(8,128)(2,1)S(1)} %get-tuple-element.114), channel_id=1, source_target_pairs={{16,0},{1,17},{18,2},{3,19},{20,4},{5,21},{22,6},{7,23},{24,8},{9,... | collective-permute-start | bytes 1572872 | tf_op jit(solution)/shard_map/ppermute | solution.py:278
  30.6 14.7 %collective-permute-start.6 = (bf16[512,256]{1,0:T(8,128)(2,1)S(1)}, bf16[512,256]{1,0:T(8,128)(2,1)S(1)}, u32[]{:S(2)}, u32[]{:S(2)}) collective-permute-start(bf16[512,256]{1,0:T(8,128)(2,1)S(1)} %fusion), channel_id=1, source_target_pairs={{0,12},{4,8},{8,4},{12,0},{1,13},{5,9},{9,5},{13,1},{2,14},{6,10},... | collective-permute-start | bytes 786440 | tf_op jit(solution)/shard_map/ppermute | solution.py:272
  34.8 10.5 %collective-permute-start.4 = (bf16[512,256]{1,0:T(8,128)(2,1)S(1)}, bf16[512,256]{1,0:T(8,128)(2,1)S(1)}, u32[]{:S(2)}, u32[]{:S(2)}) collective-permute-start(bf16[512,256]{1,0:T(8,128)(2,1)S(1)} %fusion.2), channel_id=1, source_target_pairs={{0,4},{4,0},{8,12},{12,8},{1,5},{5,1},{9,13},{13,9},{2,6},{6,2},{1... | collective-permute-start | bytes 786440 | tf_op jit(solution)/shard_map/ppermute | solution.py:272
  47.4 31.7 %collective-permute-start.10 = (bf16[512,1024]{1,0:T(8,128)(2,1)S(1)}, bf16[512,1024]{1,0:T(8,128)(2,1)S(1)}, u32[]{:S(2)}, u32[]{:S(2)}) collective-permute-start(bf16[512,1024]{1,0:T(8,128)(2,1)S(1)} %shard_map.228.refs_0_.refs_4_), channel_id=1, source_target_pairs={{0,16},{16,0},{1,17},{17,1},{2,18},{18,2},{3,19},{19,3},{4,20},{20... | collective-permute-start | bytes 3145736 | tf_op jit(solution)/shard_map/ppermute | solution.py:209
  49.1 30.0 %collective-permute-start.11 = (bf16[128,1024]{1,0:T(8,128)(2,1)}, bf16[128,1024]{1,0:T(8,128)(2,1)S(1)}, u32[]{:S(2)}, u32[]{:S(2)}) collective-permute-start(bf16[128,1024]{1,0:T(8,128)(2,1)} %slice_bitcast_fusion.1), channel_id=1, source_target_pairs={{0,16},{16,0},{1,17},{17,1},{2,18},{18,2},{3,19},{19,3},{4,20},{20... | collective-permute-start | bytes 786440 | tf_op jit(solution)/shard_map/ppermute | solution.py:209
  51.5 4.7 %collective-permute-start.14 = (f32[32,4]{0,1:T(4,128)S(1)}, f32[32,4]{0,1:T(4,128)S(1)}, u32[]{:S(2)}, u32[]{:S(2)}) collective-permute-start(f32[32,4]{0,1:T(4,128)S(1)} %copy.48), channel_id=1, source_target_pairs={{0,1},{1,0},{2,3},{3,2},{4,5},{5,4},{6,7},{7,6},{8,9},{9,8},{10,11... | collective-permute-start | bytes 1544 | tf_op jit(solution)/shard_map/ppermute | solution.py:216
  51.5 6.2 %collective-permute-start.12 = (f32[2,1024]{1,0:T(2,128)S(1)}, f32[2,1024]{1,0:T(2,128)S(1)}, u32[]{:S(2)}, u32[]{:S(2)}) collective-permute-start(f32[2,1024]{1,0:T(2,128)S(1)} %reshape.73), channel_id=1, source_target_pairs={{0,4},{4,0},{8,12},{12,8},{1,5},{5,1},{9,13},{13,9},{2,6},{6,2},{1... | collective-permute-start | bytes 24584 | tf_op jit(solution)/shard_map/ppermute | solution.py:216
  53.5 25.7 %copy-start.8 = (f32[1,1,512,1024]{3,2,1,0:T(8,128)S(1)}, f32[1,1,512,1024]{3,2,1,0:T(8,128)}, u32[]{:S(2)}) copy-start(f32[1,1,512,1024]{3,2,1,0:T(8,128)} %param.16) | copy-start | bytes 6291460
  53.5 25.7 %copy-start.9 = (f32[1,1,512,1024]{3,2,1,0:T(8,128)S(1)}, f32[1,1,512,1024]{3,2,1,0:T(8,128)}, u32[]{:S(2)}) copy-start(f32[1,1,512,1024]{3,2,1,0:T(8,128)} %param.17) | copy-start | bytes 6291460
  55.4 40.6 %collective-permute-start.16 = (bf16[384,1024]{1,0:T(8,128)(2,1)S(1)}, bf16[384,1024]{1,0:T(8,128)(2,1)S(1)}, u32[]{:S(2)}, u32[]{:S(2)}) collective-permute-start(bf16[384,1024]{1,0:T(8,128)(2,1)S(1)} %copy-done.16), channel_id=1, source_target_pairs={{0,16},{16,0},{1,17},{17,1},{2,18},{18,2},{3,19},{19,3},{4,20},{20... | collective-permute-start | bytes 2359304 | tf_op jit(solution)/shard_map/ppermute | solution.py:209
  56.2 4.2 %collective-permute-start.15 = (f32[32,4]{0,1:T(4,128)S(1)}, f32[32,4]{0,1:T(4,128)S(1)}, u32[]{:S(2)}, u32[]{:S(2)}) collective-permute-start(f32[32,4]{0,1:T(4,128)S(1)} %add.138), channel_id=1, source_target_pairs={{0,2},{1,3},{2,0},{3,1},{4,6},{5,7},{6,4},{7,5},{8,10},{9,11},{10,... | collective-permute-start | bytes 1544 | tf_op jit(solution)/shard_map/ppermute | solution.py:216
  57.7 4.6 %collective-permute-start.13 = (f32[2,1024]{1,0:T(2,128)S(1)}, f32[2,1024]{1,0:T(2,128)S(1)}, u32[]{:S(2)}, u32[]{:S(2)}) collective-permute-start(f32[2,1024]{1,0:T(2,128)S(1)} %add.136), channel_id=1, source_target_pairs={{0,8},{4,12},{8,0},{12,4},{1,9},{5,13},{9,1},{13,5},{2,10},{6,14},... | collective-permute-start | bytes 24584 | tf_op jit(solution)/shard_map/ppermute | solution.py:216
  84.9 33.6 %collective-permute-start.18 = (bf16[512,1024]{1,0:T(8,128)(2,1)}, bf16[512,1024]{1,0:T(8,128)(2,1)}, u32[]{:S(2)}, u32[]{:S(2)}) collective-permute-start(bf16[512,1024]{1,0:T(8,128)(2,1)} %get-tuple-element.64), channel_id=1, source_target_pairs={{0,16},{16,0},{1,17},{17,1},{2,18},{18,2},{3,19},{19,3},{4,20},{20... | collective-permute-start | bytes 3145736 | tf_op jit(solution)/shard_map/ppermute | solution.py:209
  103.5 37.6 %collective-permute-start.17 = (bf16[512,1024]{1,0:T(8,128)(2,1)}, bf16[512,1024]{1,0:T(8,128)(2,1)}, u32[]{:S(2)}, u32[]{:S(2)}) collective-permute-start(bf16[512,1024]{1,0:T(8,128)(2,1)} %get-tuple-element.62.refs_0_), channel_id=1, source_target_pairs={{0,16},{16,0},{1,17},{17,1},{2,18},{18,2},{3,19},{19,3},{4,20},{20... | collective-permute-start | bytes 3145736 | tf_op jit(solution)/shard_map/ppermute | solution.py:209
  137.0 20.9 %collective-permute-start.20 = (bf16[384,1024]{1,0:T(8,128)(2,1)S(1)}, bf16[384,1024]{1,0:T(8,128)(2,1)}, u32[]{:S(2)}, u32[]{:S(2)}) collective-permute-start(bf16[384,1024]{1,0:T(8,128)(2,1)S(1)} %slice.39), channel_id=1, source_target_pairs={{0,16},{16,0},{1,17},{17,1},{2,18},{18,2},{3,19},{19,3},{4,20},{20... | collective-permute-start | bytes 2359304 | tf_op jit(solution)/shard_map/ppermute | solution.py:209
  138.5 23.7 %collective-permute-start.19 = (bf16[128,1024]{1,0:T(8,128)(2,1)}, bf16[128,1024]{1,0:T(8,128)(2,1)S(1)}, u32[]{:S(2)}, u32[]{:S(2)}) collective-permute-start(bf16[128,1024]{1,0:T(8,128)(2,1)} %slice.38), channel_id=1, source_target_pairs={{0,16},{16,0},{1,17},{17,1},{2,18},{18,2},{3,19},{19,3},{4,20},{20... | collective-permute-start | bytes 786440 | tf_op jit(solution)/shard_map/ppermute | solution.py:209
  (21 other events, 125.7 us)

commit v3 on v2

--- a/solution.py
+++ b/solution.py
@@ -103,50 +103,72 @@
     )(side, part, left, right)
 
 
-def basis_kernel(n_left, n_right, offsets, *refs):
-    left_pieces, right_pieces = refs[:n_left], refs[n_left : n_left + n_right]
-    out = refs[-1]
-    left_side = offsets[n_left + n_right] == 1
+def join_kernel(offsets, *refs):
+    *pieces, out = refs
+    join(out, offsets, pieces)
+
+
+def basis_kernel(n, scalars, *refs):
+    *left_pieces, right, out = refs
+    left_side = scalars[n] == 1
 
     @pl.when(left_side)
     def _():
-        join(out, [offsets[i] for i in range(n_left)], left_pieces)
+        join(out, scalars, left_pieces)
 
     @pl.when(jnp.logical_not(left_side))
     def _():
-        join(out, [offsets[n_left + i] for i in range(n_right)], right_pieces)
+        out[...] = right[...]
 
 
 def stats_kernel(n, offsets, *refs):
     pieces, column_pieces = refs[:n], refs[n : 2 * n]
     rows_ref, left_stat, right_stat = refs[2 * n : 2 * n + 3]
-    left_next, right_next, keep, send, grad, columns = refs[2 * n + 3 :]
+    left_next, right_next, left_half, right_half, grad, columns = refs[2 * n + 3 :]
     join(grad, offsets, pieces)
     join(columns, offsets, column_pieces)
     for at in tiles(rows_ref.shape[0]):
-        left_next[at] = beta_stat * left_stat[at] + product(rows_ref[at], grad[...], NT)
-    for at in tiles(rows_ref.shape[0]):
-        right_next[at] = beta_stat * right_stat[at] + product(columns[:, at], grad[...], TN)
-    left_side = offsets[n] == 1
+        left_new = beta_stat * left_stat[at] + product(rows_ref[at], grad[...], NT)
+        right_new = beta_stat * right_stat[at] + product(columns[:, at], grad[...], TN)
+        left_next[at] = left_new
+        right_next[at] = right_new
+        left_half[at] = left_new.astype(bf16)
+        right_half[at] = right_new.astype(bf16)
+
+
+def pair_stats_kernel(offsets, *refs):
+    (own_rows, other_rows), left_stat, right_stat = refs[:2], refs[2], refs[3]
+    left_next, right_next, keep, added, grad = refs[4:]
+    join(grad, offsets, (own_rows, other_rows))
+    count = own_rows.shape[0]
+    own = pl.multiple_of(offsets[0], count)
+    other = pl.multiple_of(offsets[1], count)
+    for at in tiles(count):
+        columns = grad[:, pl.ds(own + at.start, at.stop - at.start)]
+        left_next[at] = beta_stat * left_stat[at] + product(own_rows[at], grad[...], NT)
+        right_next[at] = beta_stat * right_stat[at] + product(columns, grad[...], TN)
+    left_side = offsets[2] == 1
 
     @pl.when(left_side)
     def _():
         keep[...] = left_next[...].astype(bf16)
-        send[...] = right_next[...].astype(bf16)
+        for at in tiles(count):
+            added[at] = product(other_rows[at], grad[...], NT)
 
     @pl.when(jnp.logical_not(left_side))
     def _():
         keep[...] = right_next[...].astype(bf16)
-        send[...] = left_next[...].astype(bf16)
+        for at in tiles(count):
+            columns = grad[:, pl.ds(other + at.start, at.stop - at.start)]
+            added[at] = product(columns, grad[...], TN)
 
 
 def moments_kernel(n, offsets, *refs):
-    pieces, column_pieces, right_pieces = refs[:n], refs[n : 2 * n], refs[2 * n : 3 * n]
-    first, second = refs[3 * n : 3 * n + 2]
-    first_next, second_next, direction, grad, columns, right, rotated_half = refs[3 * n + 2 :]
+    pieces, column_pieces, right = refs[:n], refs[n : 2 * n], refs[2 * n]
+    first, second = refs[2 * n + 1 : 2 * n + 3]
+    first_next, second_next, direction, grad, columns, rotated_half = refs[2 * n + 3 :]
     join(grad, offsets, pieces)
     join(columns, offsets, column_pieces)
-    join(right, offsets, right_pieces)
     for at in tiles(grad.shape[0]):
         rotated_half[at] = product(grad[at], right[...]).astype(bf16)
     for at in tiles(first.shape[0]):
@@ -159,19 +181,23 @@
 
 
 def update_kernel(n, offsets, *refs):
-    pieces, right_pieces, rows_ref = refs[:n], refs[n : 2 * n], refs[2 * n]
-    update, direction, right = refs[2 * n + 1 :]
+    pieces, right, rows_ref, update, direction = refs[:n], *refs[n:]
     join(direction, offsets, pieces)
-    join(right, offsets, right_pieces)
     for at in tiles(rows_ref.shape[0]):
         back_half = product(rows_ref[at], direction[...]).astype(bf16)
         update[at] = product(back_half, right[...], NT)
 
 
 def rotation_kernel(ns, n_out, offsets, *refs):
-    stat_pieces, basis, outs = refs[:ns], refs[ns], refs[ns + 1 : ns + 1 + n_out]
-    stat, iterate, half_a, half_b = refs[ns + 1 + n_out :]
-    join(stat, offsets, stat_pieces)
+    stat_pieces, basis, outs = refs[:ns], refs[ns], refs[-4 - n_out : -4]
+    stat, iterate, half_a, half_b = refs[-4:]
+    join(stat, offsets, stat_pieces[:1])
+    if ns > 1:
+        before, added = stat_pieces[1], refs[ns + 1]
+        count = before.shape[0]
+        for at in tiles(count):
+            here = pl.ds(pl.multiple_of(offsets[1] + at.start, at.stop - at.start), at.stop - at.start)
+            stat[here, :] = (beta_stat * before[at].astype(f32) + added[at]).astype(bf16)
     squares = jnp.zeros((), f32)
     for at in tiles(stat.shape[0]):
         power = product(stat[at], basis[...])
@@ -283,8 +309,7 @@
                     for s in range(n_section)
                 ],
             )
-            head = rows // 4
-            right_head = swap(after(right_local[:head], last))
+            right_other = swap(after(right_local, last))
             places = jnp.stack([(rank ^ step) * width for step in range(n_tensor)])
             *blocks, both, left_cross, left_rest = lax.optimization_barrier(
                 (*blocks, both, left_cross, left_rest)
@@ -296,12 +321,18 @@
                 places,
                 *blocks,
             )
-            grad_other, right_head = lax.optimization_barrier((swap(grad_rows), right_head))
-            right_other = jnp.concatenate(
-                [right_head, swap(after(right_local[head:], grad_rows))], axis=0
-            )
+            right_pieces = [right_local, right_other]
+            (right_full,) = call(
+                join_kernel,
+                [shape(extent, extent, bf16)],
+                [],
+                jnp.stack([own, other]),
+                *right_pieces,
+            )
+            grad_other, right_full = lax.optimization_barrier((swap(grad_rows), right_full))
             grad_pieces = [grad_rows, grad_other]
-            right_pieces = [right_local, right_other]
+            stat_send = jnp.where(left_side == 1, right_stat[0, 0], left_stat[0, 0]).astype(bf16)
+            stat_other = swap(after(stat_send, grad_rows))
             offsets = jnp.stack([own, other])
             left_columns = [lax.dynamic_slice_in_dim(left_local, own, rows, 1), left_cross]
         else:
@@ -314,14 +345,13 @@
             def gather(value):
                 return [lax.all_gather(value, "dp", axis=0, tiled=True)]
 
-            grad_pieces, left_pieces, right_pieces = (
+            grad_pieces, left_pieces, (right_full,) = (
                 gather(grad_rows),
                 gather(left_local),
                 gather(right_local),
             )
             offsets = jnp.zeros((1,), jnp.int32)
             left_columns = columns_of(left_pieces)
-            left_side = jnp.int32(1)
         gain_sum = total(both[: gain_part.size].reshape(gain_part.shape), "tensor", n_tensor)
         table_sum = total(both[gain_part.size :].reshape(table_part.shape), "section", n_section)
         grad_pieces[-1], gain_sum, table_sum = lax.optimization_barrier(
@@ -331,32 +361,45 @@
         square = pltpu.VMEM((extent, extent), bf16)
         strip = pltpu.VMEM((extent, rows), bf16)
 
-        left_new, right_new, stat_keep, stat_send = call(
-            functools.partial(stats_kernel, n),
-            [shape(rows, extent, f32)] * 2 + [shape(rows, extent, bf16)] * 2,
-            [square, strip],
-            jnp.concatenate([offsets, left_side[None]]),
-            *grad_pieces,
-            *columns_of(grad_pieces),
-            grad_rows,
-            left_stat[0, 0],
-            right_stat[0, 0],
-        )
-        stat_other = swap(stat_send) if pair else None
         first_new, second_new, direction = call(
             functools.partial(moments_kernel, n),
             [shape(rows, extent, f32)] * 2 + [shape(rows, extent, bf16)],
-            [square, strip, square, square],
+            [square, strip, square],
             offsets,
             *grad_pieces,
             *left_columns,
-            *right_pieces,
+            right_full,
             first_moment[0, 0],
             second_moment[0, 0],
         )
         direction_pieces = [direction, swap(direction)] if pair else gather(direction)
-
-        def rotation(stat_pieces, basis, outs, bases):
+        grad_rows = after(grad_rows, direction)
+        if pair:
+            left_new, right_new, stat_keep, stat_added = call(
+                pair_stats_kernel,
+                [shape(rows, extent, f32)] * 2
+                + [shape(rows, extent, bf16), shape(rows, extent, f32)],
+                [square],
+                jnp.concatenate([offsets, left_side[None]]),
+                grad_rows,
+                grad_pieces[1],
+                left_stat[0, 0],
+                right_stat[0, 0],
+            )
+        else:
+            left_new, right_new, left_new_half, right_new_half = call(
+                functools.partial(stats_kernel, n),
+                [shape(rows, extent, f32)] * 2 + [shape(rows, extent, bf16)] * 2,
+                [square, strip],
+                offsets,
+                *grad_pieces,
+                *columns_of(grad_pieces),
+                grad_rows,
+                left_stat[0, 0],
+                right_stat[0, 0],
+            )
+
+        def rotation(stat_pieces, basis, outs, bases, *more):
             return call(
                 functools.partial(rotation_kernel, len(stat_pieces), len(outs)),
                 outs,
@@ -364,6 +407,7 @@
                 jnp.concatenate([offsets, jnp.stack(bases)]),
                 *stat_pieces,
                 basis,
+                *more,
             )
 
         own_rows = shape(rows, extent, f32)
@@ -374,13 +418,13 @@
                 jnp.concatenate([left_rest, left_cross], axis=1),
             )
             (basis,) = call(
-                functools.partial(basis_kernel, n, n),
+                functools.partial(basis_kernel, n),
                 [shape(extent, extent, bf16)],
                 [],
-                jnp.concatenate([offsets, offsets, left_side[None]]),
+                jnp.concatenate([offsets, left_side[None]]),
                 left_local,
                 left_other,
-                *right_pieces,
+                right_full,
             )
             basis = after(basis, direction)
             rotation_own, rotation_send = rotation(
@@ -388,30 +432,37 @@
                 basis,
                 [own_rows, shape(rows, extent, bf16)],
                 [own, other],
+                stat_added,
             )
             direction_pieces[1] = after(direction_pieces[1], rotation_send)
             cut = rows * 3 // 4
             rotation_parts = [swap(rotation_send[:cut])]
             rotation_parts.append(swap(rotation_send[cut:]))
-            left_rotation, right_rotation = rotation_own, rotation_own
         else:
-            (left_rotation,) = rotation(gather(stat_keep), left_pieces[0], [own_rows], [own])
-            (right_rotation,) = rotation(gather(stat_send), right_pieces[0], [own_rows], [own])
+            (left_rotation,) = rotation(gather(left_new_half), left_pieces[0], [own_rows], [own])
+            (right_rotation,) = rotation(gather(right_new_half), right_full, [own_rows], [own])
         (update,) = call(
             functools.partial(update_kernel, n),
             [own_rows],
-            [square, square],
+            [square],
             offsets,
             *direction_pieces,
-            *right_pieces,
+            right_full,
             left_local,
         )
         if pair:
             rotation_parts[0] = after(rotation_parts[0], update)
-            for start, part in zip((0, cut), rotation_parts):
-                left_rotation, right_rotation = place(
-                    left_side[None], part, start, left_rotation, right_rotation
-                )
+            left_rotation, right_rotation = place(
+                left_side[None], rotation_parts[0], 0, rotation_own, rotation_own
+            )
+            tail = rotation_parts[1].astype(f32)
+            tail_own = rotation_own[cut:]
+            left_rotation = left_rotation.at[cut:].set(
+                jnp.where(left_side == 1, tail_own, tail)
+            )
+            right_rotation = right_rotation.at[cut:].set(
+                jnp.where(left_side == 1, tail, tail_own)
+            )
 
         gain_moment = beta_first * gain_first[0] + (1.0 - beta_first) * gain_sum
         gain_squares = beta_second * gain_second[0] + (1.0 - beta_second) * gain_sum * gain_sum

time: 165 us -> 163 us (0.988)
  waiting for transfers between devices: 71.6 us -> 61.4 us
  other arithmetic: 10.3 us -> 14.6 us
  Pallas kernels: 42.7 us -> 46.4 us
    ppermute x12 -> x11, waiting for transfers between devices: 58.4 us -> 48.1 us  [swap(): return lax.ppermute(value, 'dp', [(0, 1), (1, 0)])]
    pallas_call x6 -> x7, Pallas kernels: 38.5 us -> 44 us  [call(): pl.pallas_call(kernel, out_shape=outs, in_specs=[pl.BlockSpec(memory_spac...]
    convert_element_type x0 -> x1, other arithmetic: none -> 3 us  [local(): jnp.where(left_side == 1, right_stat[0, 0], left_stat[0, 0]).astype(bf16)]
    scatter x0 -> x1, other arithmetic: none -> 2.22 us  [local(): right_rotation.at[cut:].set(jnp.where(left_side == 1, tail, tail_own))]
    unnamed x52 -> x38, local copies, waits for them, and re-layouts: 3.12 us -> 5.1 us
    pallas_call x2 -> x1, Pallas kernels: 4.17 us -> 2.38 us  [place(): pl.pallas_call(functools.partial(place_kernel, start), out_shape=[shape(*...]
    convert_element_type x2, other arithmetic: 2.06 us -> 0.31 us  [local(): left_local = left_basis[0, 0].astype(bf16)]
    slice x2 -> x0, local copies, waits for them, and re-layouts: 1.65 us -> none  [the longest x1 0.93 us: local(): right_local[head:]]
  transfers between devices with their start and end apart: 21 -> 20, of which waited for: 12 -> 11; matrix products, arithmetic and copies ran while one was open for 9% -> 10% of each run, Pallas kernels for 24% -> 29%
where the time goes in v3:
time: 163 us; the launch traced here: 162 us
  waiting for transfers between devices  61.4 us (38%)
  Pallas kernels  46.4 us (28%)
  starting transfers between devices  31 us (19%)
  other arithmetic  14.6 us (9%)
  local copies, waits for them, and re-layouts  8.06 us (5%)
    ppermute x11, waiting for transfers between devices, swap(): return lax.ppermute(value, 'dp', [(0, 1), (1, 0)])  48.1 us
    pallas_call x7, Pallas kernels, call(): pl.pallas_call(kernel, out_shape=outs, in_specs=[pl.BlockSpec(memory_spac...  44 us
    ppermute x11, starting transfers between devices, swap(): return lax.ppermute(value, 'dp', [(0, 1), (1, 0)])  14.1 us
    ppermute x3, waiting for transfers between devices, local(): lax.ppermute(block, 'tensor', [(i, i ^ step) for i in range(n_tensor)])  9.36 us
    ppermute x5, starting transfers between devices, total(): lax.ppermute(value, axis, [(i, i ^ step) for i in range(count)])  8.19 us
    ppermute x3, starting transfers between devices, local(): lax.ppermute(block, 'tensor', [(i, i ^ step) for i in range(n_tensor)])  7.39 us
    unnamed x38, local copies, waits for them, and re-layouts  5.1 us
    convert_element_type x4, other arithmetic, local(): last = block = block.astype(bf16)  4.44 us
  transfers between devices with their start and end apart: 20, of which 11 were waited for; matrix products, arithmetic and copies ran while one was open for 10% of the time, Pallas kernels for 29%

profile of v3, /device:TPU:0, one launch (start us, length us, event | category | flops | bytes accessed | tf_op | source)
XLA Modules:
  0.0 162.4 jit_solution(17645862970638977767)
XLA Ops:
  0.7 2.5 %dynamic-slice_bitcast_fusion.1 = (bf16[512,256]{1,0:T(8,128)(2,1)}, bf16[512,256]{1,0:T(8,128)(2,1)}, bf16[512,256]{1,0:T(8,128)(2,1)}, bf16[512,256]{1,0:T(8,128)(2,1)}) fusion(bf16[1,1,4,1024,256]{4,3,2,1,0:T(8,128)(2,1)} %param.17, s32[]{:T(128)S(6)} %select_n.86, s32[]{:T(128)S(6)} %select_n.80, s32[]{:T(128)S(6)} %select_n.84, s32[]{:T(128)S(6)} %select_n.82, ...), kind=kLoop, calls=%fused_computation.18 | loop fusion | bytes 2097172 | tf_op jit(solution)/shard_map/dynamic_slice | solution.py:289
  3.2 2.9 %collective-permute-start.3 = (bf16[512,256]{1,0:T(8,128)(2,1)}, bf16[512,256]{1,0:T(8,128)(2,1)}, u32[]{:S(2)}, u32[]{:S(2)}) collective-permute-start(bf16[512,256]{1,0:T(8,128)(2,1)} %get-tuple-element.134), channel_id=1, source_target_pairs={{0,16},{16,0},{1,17},{17,1},{2,18},{18,2},{3,19},{19,3},{4,20},{20... | collective-permute-start | bytes 786440 | tf_op jit(solution)/shard_map/ppermute | solution.py:235
  6.2 2.0 %collective-permute-start.1 = (bf16[512,256]{1,0:T(8,128)(2,1)}, bf16[512,256]{1,0:T(8,128)(2,1)}, u32[]{:S(2)}, u32[]{:S(2)}) collective-permute-start(bf16[512,256]{1,0:T(8,128)(2,1)} %get-tuple-element.136), channel_id=1, source_target_pairs={{0,16},{16,0},{1,17},{17,1},{2,18},{18,2},{3,19},{19,3},{4,20},{20... | collective-permute-start | bytes 786440 | tf_op jit(solution)/shard_map/ppermute | solution.py:235
  8.4 2.0 %collective-permute-start.7 = (f32[2176]{0:T(1024)S(1)}, f32[2176]{0:T(1024)S(1)}, u32[]{:S(2)}, u32[]{:S(2)}) collective-permute-start(f32[2176]{0:T(1024)S(1)} %constant_dynamic-update-slice_fusion), channel_id=1, source_target_pairs={{0,16},{16,0},{1,17},{17,1},{2,18},{18,2},{3,19},{19,3},{4,20},{20... | collective-permute-start | bytes 26120 | tf_op jit(solution)/shard_map/ppermute | solution.py:242
  14.7 4.5 %collective-permute-done.2 = bf16[512,256]{1,0:T(8,128)(2,1)} collective-permute-done((bf16[512,256]{1,0:T(8,128)(2,1)}, bf16[512,256]{1,0:T(8,128)(2,1)}, u32[]{:S(2)}, u32[]{:S(2)}) %collective-permute-start.2) | collective-permute-done | bytes 262176 | tf_op jit(solution)/shard_map/ppermute | solution.py:235
  20.3 3.2 %collective-permute-start.5 = (bf16[512,256]{1,0:T(8,128)(2,1)S(1)}, bf16[512,256]{1,0:T(8,128)(2,1)S(1)}, u32[]{:S(2)}, u32[]{:S(2)}) collective-permute-start(bf16[512,256]{1,0:T(8,128)(2,1)S(1)} %fusion.5), channel_id=1, source_target_pairs={{0,8},{4,12},{8,0},{12,4},{1,9},{5,13},{9,1},{13,5},{2,10},{6,14},... | collective-permute-start | bytes 786440 | tf_op jit(solution)/shard_map/ppermute | solution.py:298
  24.8 2.1 %collective-permute-start.8 = (bf16[512,512]{1,0:T(8,128)(2,1)S(1)}, bf16[512,512]{1,0:T(8,128)(2,1)S(1)}, u32[]{:S(2)}, u32[]{:S(2)}) collective-permute-start(bf16[512,512]{1,0:T(8,128)(2,1)S(1)} %get-tuple-element.139), channel_id=1, source_target_pairs={{0,16},{16,0},{1,17},{17,1},{2,18},{18,2},{3,19},{19,3},{4,20},{20... | collective-permute-start | bytes 1572872 | tf_op jit(solution)/shard_map/ppermute | solution.py:235
  30.6 4.2 %collective-permute-start.6 = (bf16[512,256]{1,0:T(8,128)(2,1)S(1)}, bf16[512,256]{1,0:T(8,128)(2,1)S(1)}, u32[]{:S(2)}, u32[]{:S(2)}) collective-permute-start(bf16[512,256]{1,0:T(8,128)(2,1)S(1)} %fusion.4), channel_id=1, source_target_pairs={{0,12},{4,8},{8,4},{12,0},{1,13},{5,9},{9,5},{13,1},{2,14},{6,10},... | collective-permute-start | bytes 786440 | tf_op jit(solution)/shard_map/ppermute | solution.py:298
  35.9 9.4 %collective-permute-done.4.refs_1_ = bf16[512,256]{1,0:T(8,128)(2,1)S(1)} collective-permute-done((bf16[512,256]{1,0:T(8,128)(2,1)S(1)}, bf16[512,256]{1,0:T(8,128)(2,1)S(1)}, u32[]{:S(2)}, u32[]{:S(2)}) %collective-permute-start.4) | collective-permute-done | bytes 262176 | tf_op jit(solution)/shard_map/ppermute | solution.py:298
  49.7 3.0 %select_convert_fusion = bf16[512,1024]{1,0:T(8,128)(2,1)} fusion(pred[]{:T(512)S(6)} %eq.11, f32[1,1,512,1024]{3,2,1,0:T(8,128)} %param.21, f32[1,1,512,1024]{3,2,1,0:T(8,128)S(1)} %copy-done.1), kind=kLoop, calls=%fused_computation | loop fusion | flops 524288 | bytes 5242881 | tf_op jit(solution)/shard_map/convert_element_type | solution.py:334
  54.6 2.4 %collective-permute-start.12 = (f32[2,1024]{1,0:T(2,128)S(1)}, f32[2,1024]{1,0:T(2,128)S(1)}, u32[]{:S(2)}, u32[]{:S(2)}) collective-permute-start(f32[2,1024]{1,0:T(2,128)S(1)} %reshape.124), channel_id=1, source_target_pairs={{0,4},{4,0},{8,12},{12,8},{1,5},{5,1},{9,13},{13,9},{2,6},{6,2},{1... | collective-permute-start | bytes 24584 | tf_op jit(solution)/shard_map/ppermute | solution.py:242
  58.8 1.9 %collective-permute-start.13 = (f32[2,1024]{1,0:T(2,128)S(1)}, f32[2,1024]{1,0:T(2,128)S(1)}, u32[]{:S(2)}, u32[]{:S(2)}) collective-permute-start(f32[2,1024]{1,0:T(2,128)S(1)} %add.138), channel_id=1, source_target_pairs={{0,8},{4,12},{8,0},{12,4},{1,9},{5,13},{9,1},{13,5},{2,10},{6,14},... | collective-permute-start | bytes 24584 | tf_op jit(solution)/shard_map/ppermute | solution.py:242
  60.8 2.6 %collective-permute-done.13 = f32[2,1024]{1,0:T(2,128)S(1)} collective-permute-done((f32[2,1024]{1,0:T(2,128)S(1)}, f32[2,1024]{1,0:T(2,128)S(1)}, u32[]{:S(2)}, u32[]{:S(2)}) %collective-permute-start.13) | collective-permute-done | bytes 8224 | tf_op jit(solution)/shard_map/ppermute | solution.py:242
  63.5 8.2 %collective-permute-done.11.refs_1_ = bf16[512,1024]{1,0:T(8,128)(2,1)} collective-permute-done((bf16[512,1024]{1,0:T(8,128)(2,1)}, bf16[512,1024]{1,0:T(8,128)(2,1)}, u32[]{:S(2)}, u32[]{:S(2)}) %collective-permute-start.11) | collective-permute-done | bytes 1048608 | tf_op jit(solution)/shard_map/ppermute | solution.py:235
  73.3 20.8 %collective-permute-done.10.refs_1_ = bf16[512,1024]{1,0:T(8,128)(2,1)} collective-permute-done((bf16[512,1024]{1,0:T(8,128)(2,1)}, bf16[512,1024]{1,0:T(8,128)(2,1)}, u32[]{:S(2)}, u32[]{:S(2)}) %collective-permute-start.10) | collective-permute-done | bytes 1048608 | tf_op jit(solution)/shard_map/ppermute | solution.py:235
  94.1 8.3 %shard_map.230 = (f32[512,1024]{1,0:T(8,128)}, f32[512,1024]{1,0:T(8,128)}, bf16[512,1024]{1,0:T(8,128)(2,1)}) custom-call(s32[2]{0:T(128)S(1)} %pad_add_fusion.offsets, bf16[512,1024]{1,0:T(8,128)(2,1)} %shard_map.228.refs_0_, bf16[512,1024]{1,0:T(8,128)(2,1)} %collective-permute-done.10.refs_1_, bf16[512,512]{1,0:T(8,128)(2,1)S(1)} %dynamic-slice_bitcast_fusion.refs_2_, ...), custom_call_target="tpu_custom_call" | custom-call | tf_op jit(solution)/shard_map/pallas_call | solution.py:50
  104.1 1.9 %maximum_select_fusion.refs_1_ = bf16[512,1024]{1,0:T(8,128)(2,1)S(1)} fusion(bf16[512,512]{1,0:T(8,128)(2,1)} %collective-permute-done.9, bf16[512,512]{1,0:T(8,128)(2,1)} %copy-done.6, pred[]{:T(512)S(6)} %lt.44), kind=kLoop, calls=%fused_computation.1 | loop fusion | flops 4718592 | bytes 2097153 | tf_op jit(solution)/shard_map/jit(_where)/select_n | solution.py:415
  108.2 7.7 %shard_map.231 = (f32[512,1024]{1,0:T(8,128)}, f32[512,1024]{1,0:T(8,128)}, bf16[512,1024]{1,0:T(8,128)(2,1)S(1)}, f32[512,1024]{1,0:T(8,128)S(1)}) custom-call(s32[3]{0:T(128)S(1)} %pad_add_fusion.3.offsets.scalars, bf16[512,1024]{1,0:T(8,128)(2,1)} %shard_map.228.refs_0_, bf16[512,1024]{1,0:T(8,128)(2,1)} %collective-permute-done.10.refs_1_, ...), custom_call_target="tpu_custom_call" | custom-call | tf_op jit(solution)/shard_map/pallas_call | solution.py:50
  116.6 18.6 %shard_map.233 = (f32[512,1024]{1,0:T(8,128)S(1)}, bf16[512,1024]{1,0:T(8,128)(2,1)S(1)}) custom-call(s32[4]{0:T(128)S(1)} %pad_add_fusion.2.offsets, bf16[512,1024]{1,0:T(8,128)(2,1)S(1)} %get-tuple-element.86.refs_0_, bf16[512,1024]{1,0:T(8,128)(2,1)} %collective-permute-done.17.refs_1_, bf16[1024,1024]{1,0:T(8,128)(2,1)S(1)} %shard_map.232.refs_2_, ...), custom_call_target="tpu_custom_call" | custom-call | tf_op jit(solution)/shard_map/pallas_call | solution.py:50
  141.3 5.4 %shard_map.234 = f32[512,1024]{1,0:T(8,128)} custom-call(s32[2]{0:T(128)S(1)} %pad_add_fusion.offsets, bf16[512,1024]{1,0:T(8,128)(2,1)} %get-tuple-element.84.refs_0_, bf16[512,1024]{1,0:T(8,128)(2,1)} %collective-permute-done.16.refs_1_, bf16[1024,1024]{1,0:T(8,128)(2,1)S(1)} %shard_map.229.refs_4_.refs_2_, ...), custom_call_target="tpu_custom_call" | custom-call | tf_op jit(solution)/shard_map/pallas_call | solution.py:50
  146.7 9.2 %collective-permute-done.18.part = bf16[384,1024]{1,0:T(8,128)(2,1)} collective-permute-done((bf16[384,1024]{1,0:T(8,128)(2,1)S(1)}, bf16[384,1024]{1,0:T(8,128)(2,1)}, u32[]{:S(2)}, u32[]{:S(2)}) %collective-permute-start.18) | collective-permute-done | bytes 786464 | tf_op jit(solution)/shard_map/ppermute | solution.py:235
  155.9 2.4 %shard_map.235 = (f32[512,1024]{1,0:T(8,128)}, f32[512,1024]{1,0:T(8,128)}) custom-call(s32[1]{0:T(128)} %bitcast.19.side, bf16[384,1024]{1,0:T(8,128)(2,1)} %collective-permute-done.18.part, f32[512,1024]{1,0:T(8,128)} %copy.50.left_in, f32[512,1024]{1,0:T(8,128)} %copy.51.right_in), custom_call_target="tpu_custom_call", output_to_operand_aliasing={{0}: (2, {}), {1}: (3, {})} | custom-call | tf_op jit(solution)/shard_map/pallas_call | solution.py:91
  158.3 1.9 %collective-permute-done.19 = bf16[128,1024]{1,0:T(8,128)(2,1)} collective-permute-done((bf16[128,1024]{1,0:T(8,128)(2,1)S(1)}, bf16[128,1024]{1,0:T(8,128)(2,1)}, u32[]{:S(2)}, u32[]{:S(2)}) %collective-permute-start.19) | collective-permute-done | bytes 262176 | tf_op jit(solution)/shard_map/ppermute | solution.py:235
  160.1 2.2 %fusion.3 = (f32[1,1,512,1024]{3,2,1,0:T(8,128)}, f32[1,1,512,1024]{3,2,1,0:T(8,128)}) fusion(f32[1,1,512,1024]{3,2,1,0:T(8,128)} %bitcast.82, bf16[128,1024]{1,0:T(8,128)(2,1)} %collective-permute-done.19, f32[512,1024]{1,0:T(8,128)} %copy-done, pred[]{:T(512)S(6)} %eq.11, f32[1,1,512,1024]{3,2,1,0:T(8,128)} %bitcast.81), kind=kLoop, calls=%fused_computation.8 | loop fusion | flops 393216 | bytes 1835009 | tf_op jit(solution)/shard_map/scatter | solution.py:463
  (95 shorter events, 32.3 us)
Async XLA Ops:
  3.2 10.4 %collective-permute-start.3 = (bf16[512,256]{1,0:T(8,128)(2,1)}, bf16[512,256]{1,0:T(8,128)(2,1)}, u32[]{:S(2)}, u32[]{:S(2)}) collective-permute-start(bf16[512,256]{1,0:T(8,128)(2,1)} %get-tuple-element.134), channel_id=1, source_target_pairs={{0,16},{16,0},{1,17},{17,1},{2,18},{18,2},{3,19},{19,3},{4,20},{20... | collective-permute-start | bytes 786440 | tf_op jit(solution)/shard_map/ppermute | solution.py:235
  6.1 13.1 %collective-permute-start.2 = (bf16[512,256]{1,0:T(8,128)(2,1)}, bf16[512,256]{1,0:T(8,128)(2,1)}, u32[]{:S(2)}, u32[]{:S(2)}) collective-permute-start(bf16[512,256]{1,0:T(8,128)(2,1)} %get-tuple-element.135), channel_id=1, source_target_pairs={{0,16},{16,0},{1,17},{17,1},{2,18},{18,2},{3,19},{19,3},{4,20},{20... | collective-permute-start | bytes 786440 | tf_op jit(solution)/shard_map/ppermute | solution.py:235
  6.2 18.6 %collective-permute-start.1 = (bf16[512,256]{1,0:T(8,128)(2,1)}, bf16[512,256]{1,0:T(8,128)(2,1)}, u32[]{:S(2)}, u32[]{:S(2)}) collective-permute-start(bf16[512,256]{1,0:T(8,128)(2,1)} %get-tuple-element.136), channel_id=1, source_target_pairs={{0,16},{16,0},{1,17},{17,1},{2,18},{18,2},{3,19},{19,3},{4,20},{20... | collective-permute-start | bytes 786440 | tf_op jit(solution)/shard_map/ppermute | solution.py:235
  8.2 26.6 %collective-permute-start = (bf16[512,256]{1,0:T(8,128)(2,1)}, bf16[512,256]{1,0:T(8,128)(2,1)S(1)}, u32[]{:S(2)}, u32[]{:S(2)}) collective-permute-start(bf16[512,256]{1,0:T(8,128)(2,1)} %get-tuple-element.137), channel_id=1, source_target_pairs={{0,16},{16,0},{1,17},{17,1},{2,18},{18,2},{3,19},{19,3},{4,20},{20... | collective-permute-start | bytes 786440 | tf_op jit(solution)/shard_map/ppermute | solution.py:235
  8.4 22.1 %collective-permute-start.7 = (f32[2176]{0:T(1024)S(1)}, f32[2176]{0:T(1024)S(1)}, u32[]{:S(2)}, u32[]{:S(2)}) collective-permute-start(f32[2176]{0:T(1024)S(1)} %constant_dynamic-update-slice_fusion), channel_id=1, source_target_pairs={{0,16},{16,0},{1,17},{17,1},{2,18},{18,2},{3,19},{19,3},{4,20},{20... | collective-permute-start | bytes 26120 | tf_op jit(solution)/shard_map/ppermute | solution.py:242
  20.3 26.3 %collective-permute-start.5 = (bf16[512,256]{1,0:T(8,128)(2,1)S(1)}, bf16[512,256]{1,0:T(8,128)(2,1)S(1)}, u32[]{:S(2)}, u32[]{:S(2)}) collective-permute-start(bf16[512,256]{1,0:T(8,128)(2,1)S(1)} %fusion.5), channel_id=1, source_target_pairs={{0,8},{4,12},{8,0},{12,4},{1,9},{5,13},{9,1},{13,5},{2,10},{6,14},... | collective-permute-start | bytes 786440 | tf_op jit(solution)/shard_map/ppermute | solution.py:298
  23.6 26.1 %copy-start.1 = (f32[1,1,512,1024]{3,2,1,0:T(8,128)S(1)}, f32[1,1,512,1024]{3,2,1,0:T(8,128)}, u32[]{:S(2)}) copy-start(f32[1,1,512,1024]{3,2,1,0:T(8,128)} %param.20) | copy-start | bytes 6291460
  24.8 21.9 %collective-permute-start.8 = (bf16[512,512]{1,0:T(8,128)(2,1)S(1)}, bf16[512,512]{1,0:T(8,128)(2,1)S(1)}, u32[]{:S(2)}, u32[]{:S(2)}) collective-permute-start(bf16[512,512]{1,0:T(8,128)(2,1)S(1)} %get-tuple-element.139), channel_id=1, source_target_pairs={{0,16},{16,0},{1,17},{17,1},{2,18},{18,2},{3,19},{19,3},{4,20},{20... | collective-permute-start | bytes 1572872 | tf_op jit(solution)/shard_map/ppermute | solution.py:235
  26.9 20.6 %collective-permute-start.9 = (bf16[512,512]{1,0:T(8,128)(2,1)S(1)}, bf16[512,512]{1,0:T(8,128)(2,1)}, u32[]{:S(2)}, u32[]{:S(2)}) collective-permute-start(bf16[512,512]{1,0:T(8,128)(2,1)S(1)} %get-tuple-element.138), channel_id=1, source_target_pairs={{16,0},{1,17},{18,2},{3,19},{20,4},{5,21},{22,6},{7,23},{24,8},{9,... | collective-permute-start | bytes 1572872 | tf_op jit(solution)/shard_map/ppermute | solution.py:304
  30.6 16.1 %collective-permute-start.6 = (bf16[512,256]{1,0:T(8,128)(2,1)S(1)}, bf16[512,256]{1,0:T(8,128)(2,1)S(1)}, u32[]{:S(2)}, u32[]{:S(2)}) collective-permute-start(bf16[512,256]{1,0:T(8,128)(2,1)S(1)} %fusion.4), channel_id=1, source_target_pairs={{0,12},{4,8},{8,4},{12,0},{1,13},{5,9},{9,5},{13,1},{2,14},{6,10},... | collective-permute-start | bytes 786440 | tf_op jit(solution)/shard_map/ppermute | solution.py:298
  34.8 10.5 %collective-permute-start.4 = (bf16[512,256]{1,0:T(8,128)(2,1)S(1)}, bf16[512,256]{1,0:T(8,128)(2,1)S(1)}, u32[]{:S(2)}, u32[]{:S(2)}) collective-permute-start(bf16[512,256]{1,0:T(8,128)(2,1)S(1)} %fusion.6), channel_id=1, source_target_pairs={{0,4},{4,0},{8,12},{12,8},{1,5},{5,1},{9,13},{13,9},{2,6},{6,2},{1... | collective-permute-start | bytes 786440 | tf_op jit(solution)/shard_map/ppermute | solution.py:298
  45.2 26.4 %collective-permute-start.11 = (bf16[512,1024]{1,0:T(8,128)(2,1)}, bf16[512,1024]{1,0:T(8,128)(2,1)}, u32[]{:S(2)}, u32[]{:S(2)}) collective-permute-start(bf16[512,1024]{1,0:T(8,128)(2,1)} %convert_bitcast_fusion.refs_0_), channel_id=1, source_target_pairs={{0,16},{16,0},{1,17},{17,1},{2,18},{18,2},{3,19},{19,3},{4,20},{20... | collective-permute-start | bytes 3145736 | tf_op jit(solution)/shard_map/ppermute | solution.py:235
  49.1 45.0 %collective-permute-start.10 = (bf16[512,1024]{1,0:T(8,128)(2,1)}, bf16[512,1024]{1,0:T(8,128)(2,1)}, u32[]{:S(2)}, u32[]{:S(2)}) collective-permute-start(bf16[512,1024]{1,0:T(8,128)(2,1)} %shard_map.228.refs_0_), channel_id=1, source_target_pairs={{0,16},{16,0},{1,17},{17,1},{2,18},{18,2},{3,19},{19,3},{4,20},{20... | collective-permute-start | bytes 3145736 | tf_op jit(solution)/shard_map/ppermute | solution.py:235
  52.7 63.8 %collective-permute-start.17 = (bf16[512,1024]{1,0:T(8,128)(2,1)}, bf16[512,1024]{1,0:T(8,128)(2,1)}, u32[]{:S(2)}, u32[]{:S(2)}) collective-permute-start(bf16[512,1024]{1,0:T(8,128)(2,1)} %select_convert_fusion), channel_id=1, source_target_pairs={{0,16},{16,0},{1,17},{17,1},{2,18},{18,2},{3,19},{19,3},{4,20},{20... | collective-permute-start | bytes 3145736 | tf_op jit(solution)/shard_map/ppermute | solution.py:235
  54.5 2.4 %collective-permute-start.14 = (f32[32,4]{0,1:T(4,128)S(1)}, f32[32,4]{0,1:T(4,128)S(1)}, u32[]{:S(2)}, u32[]{:S(2)}) collective-permute-start(f32[32,4]{0,1:T(4,128)S(1)} %copy.46), channel_id=1, source_target_pairs={{0,1},{1,0},{2,3},{3,2},{4,5},{5,4},{6,7},{7,6},{8,9},{9,8},{10,11... | collective-permute-start | bytes 1544 | tf_op jit(solution)/shard_map/ppermute | solution.py:242
  54.6 4.3 %collective-permute-start.12 = (f32[2,1024]{1,0:T(2,128)S(1)}, f32[2,1024]{1,0:T(2,128)S(1)}, u32[]{:S(2)}, u32[]{:S(2)}) collective-permute-start(f32[2,1024]{1,0:T(2,128)S(1)} %reshape.124), channel_id=1, source_target_pairs={{0,4},{4,0},{8,12},{12,8},{1,5},{5,1},{9,13},{13,9},{2,6},{6,2},{1... | collective-permute-start | bytes 24584 | tf_op jit(solution)/shard_map/ppermute | solution.py:242
  56.9 37.2 %copy-start.7 = (bf16[512,512]{1,0:T(8,128)(2,1)S(1)}, bf16[512,512]{1,0:T(8,128)(2,1)}, u32[]{:S(2)}) copy-start(bf16[512,512]{1,0:T(8,128)(2,1)} %copy-done.6) | copy-start | bytes 1572868
  57.0 3.9 %collective-permute-start.15 = (f32[32,4]{0,1:T(4,128)S(1)}, f32[32,4]{0,1:T(4,128)S(1)}, u32[]{:S(2)}, u32[]{:S(2)}) collective-permute-start(f32[32,4]{0,1:T(4,128)S(1)} %add.140), channel_id=1, source_target_pairs={{0,2},{1,3},{2,0},{3,1},{4,6},{5,7},{6,4},{7,5},{8,10},{9,11},{10,... | collective-permute-start | bytes 1544 | tf_op jit(solution)/shard_map/ppermute | solution.py:242
  58.8 4.6 %collective-permute-start.13 = (f32[2,1024]{1,0:T(2,128)S(1)}, f32[2,1024]{1,0:T(2,128)S(1)}, u32[]{:S(2)}, u32[]{:S(2)}) collective-permute-start(f32[2,1024]{1,0:T(2,128)S(1)} %add.138), channel_id=1, source_target_pairs={{0,8},{4,12},{8,0},{12,4},{1,9},{5,13},{9,1},{13,5},{2,10},{6,14},... | collective-permute-start | bytes 24584 | tf_op jit(solution)/shard_map/ppermute | solution.py:242
  63.4 30.7 %copy-start.4 = (f32[1,1,512,1024]{3,2,1,0:T(8,128)S(1)}, f32[1,1,512,1024]{3,2,1,0:T(8,128)}, u32[]{:S(2)}) copy-start(f32[1,1,512,1024]{3,2,1,0:T(8,128)} %param.18) | copy-start | bytes 6291460
  63.5 30.7 %copy-start.5 = (f32[1,1,512,1024]{3,2,1,0:T(8,128)S(1)}, f32[1,1,512,1024]{3,2,1,0:T(8,128)}, u32[]{:S(2)}) copy-start(f32[1,1,512,1024]{3,2,1,0:T(8,128)} %param.19) | copy-start | bytes 6291460
  102.5 38.9 %collective-permute-start.16 = (bf16[512,1024]{1,0:T(8,128)(2,1)}, bf16[512,1024]{1,0:T(8,128)(2,1)}, u32[]{:S(2)}, u32[]{:S(2)}) collective-permute-start(bf16[512,1024]{1,0:T(8,128)(2,1)} %get-tuple-element.84.refs_0_), channel_id=1, source_target_pairs={{0,16},{16,0},{1,17},{17,1},{2,18},{18,2},{3,19},{19,3},{4,20},{20... | collective-permute-start | bytes 3145736 | tf_op jit(solution)/shard_map/ppermute | solution.py:235
  135.3 20.6 %collective-permute-start.18 = (bf16[384,1024]{1,0:T(8,128)(2,1)S(1)}, bf16[384,1024]{1,0:T(8,128)(2,1)}, u32[]{:S(2)}, u32[]{:S(2)}) collective-permute-start(bf16[384,1024]{1,0:T(8,128)(2,1)S(1)} %slice.59), channel_id=1, source_target_pairs={{0,16},{16,0},{1,17},{17,1},{2,18},{18,2},{3,19},{19,3},{4,20},{20... | collective-permute-start | bytes 2359304 | tf_op jit(solution)/shard_map/ppermute | solution.py:235
  136.8 23.4 %collective-permute-start.19 = (bf16[128,1024]{1,0:T(8,128)(2,1)S(1)}, bf16[128,1024]{1,0:T(8,128)(2,1)}, u32[]{:S(2)}, u32[]{:S(2)}) collective-permute-start(bf16[128,1024]{1,0:T(8,128)(2,1)S(1)} %slice.61), channel_id=1, source_target_pairs={{0,16},{16,0},{1,17},{17,1},{2,18},{18,2},{3,19},{19,3},{4,20},{20... | collective-permute-start | bytes 786440 | tf_op jit(solution)/shard_map/ppermute | solution.py:235
  (13 other events, 47.8 us)

commit v4 on v3

--- a/solution.py
+++ b/solution.py
@@ -283,12 +283,19 @@
             left_local = left_basis[0, 0].astype(bf16)
             right_local = right_basis[0, 0].astype(bf16)
             last = None
+            to_send = partial_value
             blocks = [None] * n_tensor
             for step in reversed(range(n_tensor)):
                 mine = lax.dynamic_index_in_dim(partial_value, rank ^ step, 0, keepdims=False)
-                sent = lax.dynamic_slice_in_dim(mine, other, rows, 0)
+                sent = lax.dynamic_slice_in_dim(
+                    lax.dynamic_index_in_dim(to_send, rank ^ step, 0, keepdims=False),
+                    other,
+                    rows,
+                    0,
+                )
                 got = swap(sent)
                 if last is None:
+                    to_send = after(to_send, sent)
                     left_local_out = after(left_local, got)
                 else:
                     got = after(got, last)

time: 163 us -> 162 us (level)
  waiting for transfers between devices: 61.4 us -> 59.3 us
    ppermute x11, waiting for transfers between devices: 48.1 us -> 46 us  [swap(): return lax.ppermute(value, 'dp', [(0, 1), (1, 0)])]
    dynamic_slice x1 -> x2, local copies, waits for them, and re-layouts: 2.46 us -> 3.95 us  [local(): lax.dynamic_slice_in_dim(lax.dynamic_index_in_dim(to_send, rank ^ step, 0...]
  transfers between devices with their start and end apart: 20 -> 20, of which waited for: 11 -> 10; matrix products, arithmetic and copies ran while one was open for 10% -> 11% of each run, Pallas kernels for 29% -> 29%
where the time goes in v4:
time: 162 us
  waiting for transfers between devices  59.3 us (37%)
  Pallas kernels  46.4 us (29%)
  starting transfers between devices  31 us (19%)
  other arithmetic  14.6 us (9%)
  local copies, waits for them, and re-layouts  9.55 us (6%)
    ppermute x11, waiting for transfers between devices, swap(): return lax.ppermute(value, 'dp', [(0, 1), (1, 0)])  46 us
    pallas_call x7, Pallas kernels, call(): pl.pallas_call(kernel, out_shape=outs, in_specs=[pl.BlockSpec(memory_spac...  44 us
    ppermute x11, starting transfers between devices, swap(): return lax.ppermute(value, 'dp', [(0, 1), (1, 0)])  14.1 us
    ppermute x3, waiting for transfers between devices, local(): lax.ppermute(block, 'tensor', [(i, i ^ step) for i in range(n_tensor)])  9.36 us
    ppermute x5, starting transfers between devices, total(): lax.ppermute(value, axis, [(i, i ^ step) for i in range(count)])  8.19 us
    ppermute x3, starting transfers between devices, local(): lax.ppermute(block, 'tensor', [(i, i ^ step) for i in range(n_tensor)])  7.4 us
    unnamed x38, local copies, waits for them, and re-layouts  5.1 us
    convert_element_type x4, other arithmetic, local(): last = block = block.astype(bf16)  4.44 us
  transfers between devices with their start and end apart: 20, of which 10 were waited for; matrix products, arithmetic and copies ran while one was open for 11% of the time, Pallas kernels for 29%

profile of v4, /device:TPU:0, one launch (start us, length us, event | category | flops | bytes accessed | tf_op | source)
XLA Modules:
  0.0 161.7 jit_solution(140041003077156874)
XLA Ops:
  0.7 1.9 %dynamic-slice_bitcast_fusion.4 = bf16[512,256]{1,0:T(8,128)(2,1)} fusion(bf16[1,1,4,1024,256]{4,3,2,1,0:T(8,128)(2,1)} %param.17, s32[]{:T(128)S(6)} %select_n.84, s32[]{:T(128)S(6)} %select_n.86), kind=kLoop, calls=%fused_computation.21 | loop fusion | bytes 524296 | tf_op jit(solution)/shard_map/dynamic_slice | solution.py:290
  2.6 2.9 %collective-permute-start.3 = (bf16[512,256]{1,0:T(8,128)(2,1)}, bf16[512,256]{1,0:T(8,128)(2,1)}, u32[]{:S(2)}, u32[]{:S(2)}) collective-permute-start(bf16[512,256]{1,0:T(8,128)(2,1)} %dynamic-slice_bitcast_fusion.4), channel_id=1, source_target_pairs={{0,16},{16,0},{1,17},{17,1},{2,18},{18,2},{3,19},{19,3},{4,20},{20... | collective-permute-start | bytes 786440 | tf_op jit(solution)/shard_map/ppermute | solution.py:235
  5.5 2.1 %dynamic-slice_bitcast_fusion.1 = (bf16[512,256]{1,0:T(8,128)(2,1)}, bf16[512,256]{1,0:T(8,128)(2,1)}, bf16[512,256]{1,0:T(8,128)(2,1)}) fusion(bf16[4,1024,256]{2,1,0:T(8,128)(2,1)} %bitcast.84, s32[]{:T(128)S(6)} %select_n.90, s32[]{:T(128)S(6)} %select_n.86, s32[]{:T(128)S(6)} %select_n.88, s32[]{:T(128)S(6)} %select_n.80), kind=kLoop, calls=%fused_computation.18 | loop fusion | bytes 1572880 | tf_op jit(solution)/shard_map/dynamic_slice | solution.py:290
  7.6 2.0 %collective-permute-start.1 = (bf16[512,256]{1,0:T(8,128)(2,1)}, bf16[512,256]{1,0:T(8,128)(2,1)}, u32[]{:S(2)}, u32[]{:S(2)}) collective-permute-start(bf16[512,256]{1,0:T(8,128)(2,1)} %get-tuple-element.137), channel_id=1, source_target_pairs={{0,16},{16,0},{1,17},{17,1},{2,18},{18,2},{3,19},{19,3},{4,20},{20... | collective-permute-start | bytes 786440 | tf_op jit(solution)/shard_map/ppermute | solution.py:235
  9.9 2.0 %collective-permute-start.7 = (f32[2176]{0:T(1024)S(1)}, f32[2176]{0:T(1024)S(1)}, u32[]{:S(2)}, u32[]{:S(2)}) collective-permute-start(f32[2176]{0:T(1024)S(1)} %constant_dynamic-update-slice_fusion), channel_id=1, source_target_pairs={{0,16},{16,0},{1,17},{17,1},{2,18},{18,2},{3,19},{19,3},{4,20},{20... | collective-permute-start | bytes 26120 | tf_op jit(solution)/shard_map/ppermute | solution.py:242
  14.4 4.2 %collective-permute-done.2 = bf16[512,256]{1,0:T(8,128)(2,1)} collective-permute-done((bf16[512,256]{1,0:T(8,128)(2,1)}, bf16[512,256]{1,0:T(8,128)(2,1)}, u32[]{:S(2)}, u32[]{:S(2)}) %collective-permute-start.2) | collective-permute-done | bytes 262176 | tf_op jit(solution)/shard_map/ppermute | solution.py:235
  19.7 3.2 %collective-permute-start.5 = (bf16[512,256]{1,0:T(8,128)(2,1)S(1)}, bf16[512,256]{1,0:T(8,128)(2,1)S(1)}, u32[]{:S(2)}, u32[]{:S(2)}) collective-permute-start(bf16[512,256]{1,0:T(8,128)(2,1)S(1)} %fusion.5), channel_id=1, source_target_pairs={{0,8},{4,12},{8,0},{12,4},{1,9},{5,13},{9,1},{13,5},{2,10},{6,14},... | collective-permute-start | bytes 786440 | tf_op jit(solution)/shard_map/ppermute | solution.py:305
  24.2 2.1 %collective-permute-start.8 = (bf16[512,512]{1,0:T(8,128)(2,1)S(1)}, bf16[512,512]{1,0:T(8,128)(2,1)S(1)}, u32[]{:S(2)}, u32[]{:S(2)}) collective-permute-start(bf16[512,512]{1,0:T(8,128)(2,1)S(1)} %get-tuple-element.140), channel_id=1, source_target_pairs={{0,16},{16,0},{1,17},{17,1},{2,18},{18,2},{3,19},{19,3},{4,20},{20... | collective-permute-start | bytes 1572872 | tf_op jit(solution)/shard_map/ppermute | solution.py:235
  30.0 4.2 %collective-permute-start.6 = (bf16[512,256]{1,0:T(8,128)(2,1)S(1)}, bf16[512,256]{1,0:T(8,128)(2,1)S(1)}, u32[]{:S(2)}, u32[]{:S(2)}) collective-permute-start(bf16[512,256]{1,0:T(8,128)(2,1)S(1)} %fusion.4), channel_id=1, source_target_pairs={{0,12},{4,8},{8,4},{12,0},{1,13},{5,9},{9,5},{13,1},{2,14},{6,10},... | collective-permute-start | bytes 786440 | tf_op jit(solution)/shard_map/ppermute | solution.py:305
  35.3 9.3 %collective-permute-done.4.refs_1_ = bf16[512,256]{1,0:T(8,128)(2,1)S(1)} collective-permute-done((bf16[512,256]{1,0:T(8,128)(2,1)S(1)}, bf16[512,256]{1,0:T(8,128)(2,1)S(1)}, u32[]{:S(2)}, u32[]{:S(2)}) %collective-permute-start.4) | collective-permute-done | bytes 262176 | tf_op jit(solution)/shard_map/ppermute | solution.py:305
  49.1 3.0 %select_convert_fusion = bf16[512,1024]{1,0:T(8,128)(2,1)} fusion(pred[]{:T(512)S(6)} %eq.11, f32[1,1,512,1024]{3,2,1,0:T(8,128)} %param.21, f32[1,1,512,1024]{3,2,1,0:T(8,128)S(1)} %copy-done.1), kind=kLoop, calls=%fused_computation | loop fusion | flops 524288 | bytes 5242881 | tf_op jit(solution)/shard_map/convert_element_type | solution.py:341
  53.9 2.4 %collective-permute-start.12 = (f32[2,1024]{1,0:T(2,128)S(1)}, f32[2,1024]{1,0:T(2,128)S(1)}, u32[]{:S(2)}, u32[]{:S(2)}) collective-permute-start(f32[2,1024]{1,0:T(2,128)S(1)} %reshape.124), channel_id=1, source_target_pairs={{0,4},{4,0},{8,12},{12,8},{1,5},{5,1},{9,13},{13,9},{2,6},{6,2},{1... | collective-permute-start | bytes 24584 | tf_op jit(solution)/shard_map/ppermute | solution.py:242
  58.2 1.9 %collective-permute-start.13 = (f32[2,1024]{1,0:T(2,128)S(1)}, f32[2,1024]{1,0:T(2,128)S(1)}, u32[]{:S(2)}, u32[]{:S(2)}) collective-permute-start(f32[2,1024]{1,0:T(2,128)S(1)} %add.136), channel_id=1, source_target_pairs={{0,8},{4,12},{8,0},{12,4},{1,9},{5,13},{9,1},{13,5},{2,10},{6,14},... | collective-permute-start | bytes 24584 | tf_op jit(solution)/shard_map/ppermute | solution.py:242
  60.2 2.6 %collective-permute-done.13 = f32[2,1024]{1,0:T(2,128)S(1)} collective-permute-done((f32[2,1024]{1,0:T(2,128)S(1)}, f32[2,1024]{1,0:T(2,128)S(1)}, u32[]{:S(2)}, u32[]{:S(2)}) %collective-permute-start.13) | collective-permute-done | bytes 8224 | tf_op jit(solution)/shard_map/ppermute | solution.py:242
  62.9 8.2 %collective-permute-done.11.refs_1_ = bf16[512,1024]{1,0:T(8,128)(2,1)} collective-permute-done((bf16[512,1024]{1,0:T(8,128)(2,1)}, bf16[512,1024]{1,0:T(8,128)(2,1)}, u32[]{:S(2)}, u32[]{:S(2)}) %collective-permute-start.11) | collective-permute-done | bytes 1048608 | tf_op jit(solution)/shard_map/ppermute | solution.py:235
  72.7 20.8 %collective-permute-done.10.refs_1_ = bf16[512,1024]{1,0:T(8,128)(2,1)} collective-permute-done((bf16[512,1024]{1,0:T(8,128)(2,1)}, bf16[512,1024]{1,0:T(8,128)(2,1)}, u32[]{:S(2)}, u32[]{:S(2)}) %collective-permute-start.10) | collective-permute-done | bytes 1048608 | tf_op jit(solution)/shard_map/ppermute | solution.py:235
  93.5 8.3 %shard_map.230 = (f32[512,1024]{1,0:T(8,128)}, f32[512,1024]{1,0:T(8,128)}, bf16[512,1024]{1,0:T(8,128)(2,1)}) custom-call(s32[2]{0:T(128)S(1)} %pad_add_fusion.offsets, bf16[512,1024]{1,0:T(8,128)(2,1)} %shard_map.228.refs_0_, bf16[512,1024]{1,0:T(8,128)(2,1)} %collective-permute-done.10.refs_1_, bf16[512,512]{1,0:T(8,128)(2,1)S(1)} %dynamic-slice_bitcast_fusion.refs_2_, ...), custom_call_target="tpu_custom_call" | custom-call | tf_op jit(solution)/shard_map/pallas_call | solution.py:50
  103.4 1.9 %maximum_select_fusion.refs_1_ = bf16[512,1024]{1,0:T(8,128)(2,1)S(1)} fusion(bf16[512,512]{1,0:T(8,128)(2,1)} %collective-permute-done.9, bf16[512,512]{1,0:T(8,128)(2,1)} %copy-done.6, pred[]{:T(512)S(6)} %lt.48), kind=kLoop, calls=%fused_computation.1 | loop fusion | flops 4718592 | bytes 2097153 | tf_op jit(solution)/shard_map/jit(_where)/select_n | solution.py:422
  107.6 7.7 %shard_map.231 = (f32[512,1024]{1,0:T(8,128)}, f32[512,1024]{1,0:T(8,128)}, bf16[512,1024]{1,0:T(8,128)(2,1)S(1)}, f32[512,1024]{1,0:T(8,128)S(1)}) custom-call(s32[3]{0:T(128)S(1)} %pad_add_fusion.3.offsets.scalars, bf16[512,1024]{1,0:T(8,128)(2,1)} %shard_map.228.refs_0_, bf16[512,1024]{1,0:T(8,128)(2,1)} %collective-permute-done.10.refs_1_, ...), custom_call_target="tpu_custom_call" | custom-call | tf_op jit(solution)/shard_map/pallas_call | solution.py:50
  116.0 18.6 %shard_map.233 = (f32[512,1024]{1,0:T(8,128)S(1)}, bf16[512,1024]{1,0:T(8,128)(2,1)S(1)}) custom-call(s32[4]{0:T(128)S(1)} %pad_add_fusion.2.offsets, bf16[512,1024]{1,0:T(8,128)(2,1)S(1)} %get-tuple-element.88.refs_0_, bf16[512,1024]{1,0:T(8,128)(2,1)} %collective-permute-done.17.refs_1_, bf16[1024,1024]{1,0:T(8,128)(2,1)S(1)} %shard_map.232.refs_2_, ...), custom_call_target="tpu_custom_call" | custom-call | tf_op jit(solution)/shard_map/pallas_call | solution.py:50
  140.7 5.4 %shard_map.234 = f32[512,1024]{1,0:T(8,128)} custom-call(s32[2]{0:T(128)S(1)} %pad_add_fusion.offsets, bf16[512,1024]{1,0:T(8,128)(2,1)} %get-tuple-element.86.refs_0_, bf16[512,1024]{1,0:T(8,128)(2,1)} %collective-permute-done.16.refs_1_, bf16[1024,1024]{1,0:T(8,128)(2,1)S(1)} %shard_map.229.refs_4_.refs_2_, ...), custom_call_target="tpu_custom_call" | custom-call | tf_op jit(solution)/shard_map/pallas_call | solution.py:50
  146.1 9.2 %collective-permute-done.18.part = bf16[384,1024]{1,0:T(8,128)(2,1)} collective-permute-done((bf16[384,1024]{1,0:T(8,128)(2,1)S(1)}, bf16[384,1024]{1,0:T(8,128)(2,1)}, u32[]{:S(2)}, u32[]{:S(2)}) %collective-permute-start.18) | collective-permute-done | bytes 786464 | tf_op jit(solution)/shard_map/ppermute | solution.py:235
  155.3 2.4 %shard_map.235 = (f32[512,1024]{1,0:T(8,128)}, f32[512,1024]{1,0:T(8,128)}) custom-call(s32[1]{0:T(128)} %bitcast.20.side, bf16[384,1024]{1,0:T(8,128)(2,1)} %collective-permute-done.18.part, f32[512,1024]{1,0:T(8,128)} %copy.50.left_in, f32[512,1024]{1,0:T(8,128)} %copy.51.right_in), custom_call_target="tpu_custom_call", output_to_operand_aliasing={{0}: (2, {}), {1}: (3, {})} | custom-call | tf_op jit(solution)/shard_map/pallas_call | solution.py:91
  159.5 2.2 %fusion.3 = (f32[1,1,512,1024]{3,2,1,0:T(8,128)}, f32[1,1,512,1024]{3,2,1,0:T(8,128)}) fusion(f32[1,1,512,1024]{3,2,1,0:T(8,128)} %bitcast.83, bf16[128,1024]{1,0:T(8,128)(2,1)} %collective-permute-done.19, f32[512,1024]{1,0:T(8,128)} %copy-done, pred[]{:T(512)S(6)} %eq.11, f32[1,1,512,1024]{3,2,1,0:T(8,128)} %bitcast.82), kind=kLoop, calls=%fused_computation.8 | loop fusion | flops 393216 | bytes 1835009 | tf_op jit(solution)/shard_map/scatter | solution.py:470
  (96 shorter events, 32.3 us)
Async XLA Ops:
  2.6 10.7 %collective-permute-start.3 = (bf16[512,256]{1,0:T(8,128)(2,1)}, bf16[512,256]{1,0:T(8,128)(2,1)}, u32[]{:S(2)}, u32[]{:S(2)}) collective-permute-start(bf16[512,256]{1,0:T(8,128)(2,1)} %dynamic-slice_bitcast_fusion.4), channel_id=1, source_target_pairs={{0,16},{16,0},{1,17},{17,1},{2,18},{18,2},{3,19},{19,3},{4,20},{20... | collective-permute-start | bytes 786440 | tf_op jit(solution)/shard_map/ppermute | solution.py:235
  7.6 11.0 %collective-permute-start.2 = (bf16[512,256]{1,0:T(8,128)(2,1)}, bf16[512,256]{1,0:T(8,128)(2,1)}, u32[]{:S(2)}, u32[]{:S(2)}) collective-permute-start(bf16[512,256]{1,0:T(8,128)(2,1)} %get-tuple-element.136), channel_id=1, source_target_pairs={{0,16},{16,0},{1,17},{17,1},{2,18},{18,2},{3,19},{19,3},{4,20},{20... | collective-permute-start | bytes 786440 | tf_op jit(solution)/shard_map/ppermute | solution.py:235
  7.6 16.6 %collective-permute-start.1 = (bf16[512,256]{1,0:T(8,128)(2,1)}, bf16[512,256]{1,0:T(8,128)(2,1)}, u32[]{:S(2)}, u32[]{:S(2)}) collective-permute-start(bf16[512,256]{1,0:T(8,128)(2,1)} %get-tuple-element.137), channel_id=1, source_target_pairs={{0,16},{16,0},{1,17},{17,1},{2,18},{18,2},{3,19},{19,3},{4,20},{20... | collective-permute-start | bytes 786440 | tf_op jit(solution)/shard_map/ppermute | solution.py:235
  9.6 24.5 %collective-permute-start = (bf16[512,256]{1,0:T(8,128)(2,1)}, bf16[512,256]{1,0:T(8,128)(2,1)S(1)}, u32[]{:S(2)}, u32[]{:S(2)}) collective-permute-start(bf16[512,256]{1,0:T(8,128)(2,1)} %get-tuple-element.138), channel_id=1, source_target_pairs={{0,16},{16,0},{1,17},{17,1},{2,18},{18,2},{3,19},{19,3},{4,20},{20... | collective-permute-start | bytes 786440 | tf_op jit(solution)/shard_map/ppermute | solution.py:235
  9.9 20.1 %collective-permute-start.7 = (f32[2176]{0:T(1024)S(1)}, f32[2176]{0:T(1024)S(1)}, u32[]{:S(2)}, u32[]{:S(2)}) collective-permute-start(f32[2176]{0:T(1024)S(1)} %constant_dynamic-update-slice_fusion), channel_id=1, source_target_pairs={{0,16},{16,0},{1,17},{17,1},{2,18},{18,2},{3,19},{19,3},{4,20},{20... | collective-permute-start | bytes 26120 | tf_op jit(solution)/shard_map/ppermute | solution.py:242
  19.7 26.3 %collective-permute-start.5 = (bf16[512,256]{1,0:T(8,128)(2,1)S(1)}, bf16[512,256]{1,0:T(8,128)(2,1)S(1)}, u32[]{:S(2)}, u32[]{:S(2)}) collective-permute-start(bf16[512,256]{1,0:T(8,128)(2,1)S(1)} %fusion.5), channel_id=1, source_target_pairs={{0,8},{4,12},{8,0},{12,4},{1,9},{5,13},{9,1},{13,5},{2,10},{6,14},... | collective-permute-start | bytes 786440 | tf_op jit(solution)/shard_map/ppermute | solution.py:305
  23.0 26.1 %copy-start.1 = (f32[1,1,512,1024]{3,2,1,0:T(8,128)S(1)}, f32[1,1,512,1024]{3,2,1,0:T(8,128)}, u32[]{:S(2)}) copy-start(f32[1,1,512,1024]{3,2,1,0:T(8,128)} %param.20) | copy-start | bytes 6291460
  24.2 21.9 %collective-permute-start.8 = (bf16[512,512]{1,0:T(8,128)(2,1)S(1)}, bf16[512,512]{1,0:T(8,128)(2,1)S(1)}, u32[]{:S(2)}, u32[]{:S(2)}) collective-permute-start(bf16[512,512]{1,0:T(8,128)(2,1)S(1)} %get-tuple-element.140), channel_id=1, source_target_pairs={{0,16},{16,0},{1,17},{17,1},{2,18},{18,2},{3,19},{19,3},{4,20},{20... | collective-permute-start | bytes 1572872 | tf_op jit(solution)/shard_map/ppermute | solution.py:235
  26.3 20.6 %collective-permute-start.9 = (bf16[512,512]{1,0:T(8,128)(2,1)S(1)}, bf16[512,512]{1,0:T(8,128)(2,1)}, u32[]{:S(2)}, u32[]{:S(2)}) collective-permute-start(bf16[512,512]{1,0:T(8,128)(2,1)S(1)} %get-tuple-element.139), channel_id=1, source_target_pairs={{16,0},{1,17},{18,2},{3,19},{20,4},{5,21},{22,6},{7,23},{24,8},{9,... | collective-permute-start | bytes 1572872 | tf_op jit(solution)/shard_map/ppermute | solution.py:311
  30.0 16.1 %collective-permute-start.6 = (bf16[512,256]{1,0:T(8,128)(2,1)S(1)}, bf16[512,256]{1,0:T(8,128)(2,1)S(1)}, u32[]{:S(2)}, u32[]{:S(2)}) collective-permute-start(bf16[512,256]{1,0:T(8,128)(2,1)S(1)} %fusion.4), channel_id=1, source_target_pairs={{0,12},{4,8},{8,4},{12,0},{1,13},{5,9},{9,5},{13,1},{2,14},{6,10},... | collective-permute-start | bytes 786440 | tf_op jit(solution)/shard_map/ppermute | solution.py:305
  34.1 10.5 %collective-permute-start.4 = (bf16[512,256]{1,0:T(8,128)(2,1)S(1)}, bf16[512,256]{1,0:T(8,128)(2,1)S(1)}, u32[]{:S(2)}, u32[]{:S(2)}) collective-permute-start(bf16[512,256]{1,0:T(8,128)(2,1)S(1)} %fusion.6), channel_id=1, source_target_pairs={{0,4},{4,0},{8,12},{12,8},{1,5},{5,1},{9,13},{13,9},{2,6},{6,2},{1... | collective-permute-start | bytes 786440 | tf_op jit(solution)/shard_map/ppermute | solution.py:305
  44.6 26.4 %collective-permute-start.11 = (bf16[512,1024]{1,0:T(8,128)(2,1)}, bf16[512,1024]{1,0:T(8,128)(2,1)}, u32[]{:S(2)}, u32[]{:S(2)}) collective-permute-start(bf16[512,1024]{1,0:T(8,128)(2,1)} %convert_bitcast_fusion.refs_0_), channel_id=1, source_target_pairs={{0,16},{16,0},{1,17},{17,1},{2,18},{18,2},{3,19},{19,3},{4,20},{20... | collective-permute-start | bytes 3145736 | tf_op jit(solution)/shard_map/ppermute | solution.py:235
  48.5 45.0 %collective-permute-start.10 = (bf16[512,1024]{1,0:T(8,128)(2,1)}, bf16[512,1024]{1,0:T(8,128)(2,1)}, u32[]{:S(2)}, u32[]{:S(2)}) collective-permute-start(bf16[512,1024]{1,0:T(8,128)(2,1)} %shard_map.228.refs_0_), channel_id=1, source_target_pairs={{0,16},{16,0},{1,17},{17,1},{2,18},{18,2},{3,19},{19,3},{4,20},{20... | collective-permute-start | bytes 3145736 | tf_op jit(solution)/shard_map/ppermute | solution.py:235
  52.1 63.8 %collective-permute-start.17 = (bf16[512,1024]{1,0:T(8,128)(2,1)}, bf16[512,1024]{1,0:T(8,128)(2,1)}, u32[]{:S(2)}, u32[]{:S(2)}) collective-permute-start(bf16[512,1024]{1,0:T(8,128)(2,1)} %select_convert_fusion), channel_id=1, source_target_pairs={{0,16},{16,0},{1,17},{17,1},{2,18},{18,2},{3,19},{19,3},{4,20},{20... | collective-permute-start | bytes 3145736 | tf_op jit(solution)/shard_map/ppermute | solution.py:235
  53.9 2.4 %collective-permute-start.14 = (f32[32,4]{0,1:T(4,128)S(1)}, f32[32,4]{0,1:T(4,128)S(1)}, u32[]{:S(2)}, u32[]{:S(2)}) collective-permute-start(f32[32,4]{0,1:T(4,128)S(1)} %copy.46), channel_id=1, source_target_pairs={{0,1},{1,0},{2,3},{3,2},{4,5},{5,4},{6,7},{7,6},{8,9},{9,8},{10,11... | collective-permute-start | bytes 1544 | tf_op jit(solution)/shard_map/ppermute | solution.py:242
  53.9 4.3 %collective-permute-start.12 = (f32[2,1024]{1,0:T(2,128)S(1)}, f32[2,1024]{1,0:T(2,128)S(1)}, u32[]{:S(2)}, u32[]{:S(2)}) collective-permute-start(f32[2,1024]{1,0:T(2,128)S(1)} %reshape.124), channel_id=1, source_target_pairs={{0,4},{4,0},{8,12},{12,8},{1,5},{5,1},{9,13},{13,9},{2,6},{6,2},{1... | collective-permute-start | bytes 24584 | tf_op jit(solution)/shard_map/ppermute | solution.py:242
  56.3 37.2 %copy-start.7 = (bf16[512,512]{1,0:T(8,128)(2,1)S(1)}, bf16[512,512]{1,0:T(8,128)(2,1)}, u32[]{:S(2)}) copy-start(bf16[512,512]{1,0:T(8,128)(2,1)} %copy-done.6) | copy-start | bytes 1572868
  56.4 3.9 %collective-permute-start.15 = (f32[32,4]{0,1:T(4,128)S(1)}, f32[32,4]{0,1:T(4,128)S(1)}, u32[]{:S(2)}, u32[]{:S(2)}) collective-permute-start(f32[32,4]{0,1:T(4,128)S(1)} %add.138), channel_id=1, source_target_pairs={{0,2},{1,3},{2,0},{3,1},{4,6},{5,7},{6,4},{7,5},{8,10},{9,11},{10,... | collective-permute-start | bytes 1544 | tf_op jit(solution)/shard_map/ppermute | solution.py:242
  58.2 4.6 %collective-permute-start.13 = (f32[2,1024]{1,0:T(2,128)S(1)}, f32[2,1024]{1,0:T(2,128)S(1)}, u32[]{:S(2)}, u32[]{:S(2)}) collective-permute-start(f32[2,1024]{1,0:T(2,128)S(1)} %add.136), channel_id=1, source_target_pairs={{0,8},{4,12},{8,0},{12,4},{1,9},{5,13},{9,1},{13,5},{2,10},{6,14},... | collective-permute-start | bytes 24584 | tf_op jit(solution)/shard_map/ppermute | solution.py:242
  62.8 30.7 %copy-start.4 = (f32[1,1,512,1024]{3,2,1,0:T(8,128)S(1)}, f32[1,1,512,1024]{3,2,1,0:T(8,128)}, u32[]{:S(2)}) copy-start(f32[1,1,512,1024]{3,2,1,0:T(8,128)} %param.18) | copy-start | bytes 6291460
  62.8 30.7 %copy-start.5 = (f32[1,1,512,1024]{3,2,1,0:T(8,128)S(1)}, f32[1,1,512,1024]{3,2,1,0:T(8,128)}, u32[]{:S(2)}) copy-start(f32[1,1,512,1024]{3,2,1,0:T(8,128)} %param.19) | copy-start | bytes 6291460
  101.8 38.9 %collective-permute-start.16 = (bf16[512,1024]{1,0:T(8,128)(2,1)}, bf16[512,1024]{1,0:T(8,128)(2,1)}, u32[]{:S(2)}, u32[]{:S(2)}) collective-permute-start(bf16[512,1024]{1,0:T(8,128)(2,1)} %get-tuple-element.86.refs_0_), channel_id=1, source_target_pairs={{0,16},{16,0},{1,17},{17,1},{2,18},{18,2},{3,19},{19,3},{4,20},{20... | collective-permute-start | bytes 3145736 | tf_op jit(solution)/shard_map/ppermute | solution.py:235
  134.7 20.6 %collective-permute-start.18 = (bf16[384,1024]{1,0:T(8,128)(2,1)S(1)}, bf16[384,1024]{1,0:T(8,128)(2,1)}, u32[]{:S(2)}, u32[]{:S(2)}) collective-permute-start(bf16[384,1024]{1,0:T(8,128)(2,1)S(1)} %slice.59), channel_id=1, source_target_pairs={{0,16},{16,0},{1,17},{17,1},{2,18},{18,2},{3,19},{19,3},{4,20},{20... | collective-permute-start | bytes 2359304 | tf_op jit(solution)/shard_map/ppermute | solution.py:235
  136.2 23.3 %collective-permute-start.19 = (bf16[128,1024]{1,0:T(8,128)(2,1)S(1)}, bf16[128,1024]{1,0:T(8,128)(2,1)}, u32[]{:S(2)}, u32[]{:S(2)}) collective-permute-start(bf16[128,1024]{1,0:T(8,128)(2,1)S(1)} %slice.61), channel_id=1, source_target_pairs={{0,16},{16,0},{1,17},{17,1},{2,18},{18,2},{3,19},{19,3},{4,20},{20... | collective-permute-start | bytes 786440 | tf_op jit(solution)/shard_map/ppermute | solution.py:235
  (13 other events, 52.2 us)

commit v5 on v4

--- a/solution.py
+++ b/solution.py
@@ -442,7 +442,7 @@
                 stat_added,
             )
             direction_pieces[1] = after(direction_pieces[1], rotation_send)
-            cut = rows * 3 // 4
+            cut = rows * 13 // 16
             rotation_parts = [swap(rotation_send[:cut])]
             rotation_parts.append(swap(rotation_send[cut:]))
         else:

time: 162 us -> 162 us (level)
  local copies, waits for them, and re-layouts: 9.55 us -> 16.7 us
  Pallas kernels: 46.4 us -> 43.2 us
  starting transfers between devices: 31 us -> 28.7 us
    unnamed x38 -> x44, local copies, waits for them, and re-layouts: 5.1 us -> 10.5 us
    pallas_call x7, Pallas kernels: 44 us -> 40.7 us  [call(): pl.pallas_call(kernel, out_shape=outs, in_specs=[pl.BlockSpec(memory_spac...]
    ppermute x11, waiting for transfers between devices: 46 us -> 43.2 us  [swap(): return lax.ppermute(value, 'dp', [(0, 1), (1, 0)])]
    convert_element_type x4, other arithmetic: 4.44 us -> 6.55 us  [local(): last = block = block.astype(bf16)]
    ppermute x5, starting transfers between devices: 8.19 us -> 6.31 us  [total(): lax.ppermute(value, axis, [(i, i ^ step) for i in range(count)])]
  transfers between devices with their start and end apart: 20 -> 20, of which waited for: 10 -> 12; matrix products, arithmetic and copies ran while one was open for 11% -> 13% of each run, Pallas kernels for 29% -> 27%
where the time goes in v5:
time: 162 us
  waiting for transfers between devices  57.7 us (36%)
  Pallas kernels  43.2 us (27%)
  starting transfers between devices  28.7 us (18%)
  local copies, waits for them, and re-layouts  16.7 us (10%)
  other arithmetic  14.6 us (9%)
    ppermute x11, waiting for transfers between devices, swap(): return lax.ppermute(value, 'dp', [(0, 1), (1, 0)])  43.2 us
    pallas_call x7, Pallas kernels, call(): pl.pallas_call(kernel, out_shape=outs, in_specs=[pl.BlockSpec(memory_spac...  40.7 us
    ppermute x11, starting transfers between devices, swap(): return lax.ppermute(value, 'dp', [(0, 1), (1, 0)])  13.8 us
    unnamed x44, local copies, waits for them, and re-layouts  10.5 us
    ppermute x3, waiting for transfers between devices, local(): lax.ppermute(block, 'tensor', [(i, i ^ step) for i in range(n_tensor)])  10 us
    ppermute x3, starting transfers between devices, local(): lax.ppermute(block, 'tensor', [(i, i ^ step) for i in range(n_tensor)])  7.33 us
    convert_element_type x4, other arithmetic, local(): last = block = block.astype(bf16)  6.55 us
    ppermute x5, starting transfers between devices, total(): lax.ppermute(value, axis, [(i, i ^ step) for i in range(count)])  6.31 us
  transfers between devices with their start and end apart: 20, of which 12 were waited for; matrix products, arithmetic and copies ran while one was open for 13% of the time, Pallas kernels for 27%

profile of v5, /device:TPU:0, one launch (start us, length us, event | category | flops | bytes accessed | tf_op | source)
XLA Modules:
  0.0 161.7 jit_solution(11234380085339665908)
XLA Ops:
  0.7 1.9 %dynamic-slice_bitcast_fusion.4 = bf16[512,256]{1,0:T(8,128)(2,1)} fusion(bf16[1,1,4,1024,256]{4,3,2,1,0:T(8,128)(2,1)} %param.17, s32[]{:T(128)S(6)} %select_n.84, s32[]{:T(128)S(6)} %select_n.86), kind=kLoop, calls=%fused_computation.21 | loop fusion | bytes 524296 | tf_op jit(solution)/shard_map/dynamic_slice | solution.py:290
  2.6 2.9 %collective-permute-start.3 = (bf16[512,256]{1,0:T(8,128)(2,1)}, bf16[512,256]{1,0:T(8,128)(2,1)S(1)}, u32[]{:S(2)}, u32[]{:S(2)}) collective-permute-start(bf16[512,256]{1,0:T(8,128)(2,1)} %dynamic-slice_bitcast_fusion.4), channel_id=1, source_target_pairs={{0,16},{16,0},{1,17},{17,1},{2,18},{18,2},{3,19},{19,3},{4,20},{20... | collective-permute-start | bytes 786440 | tf_op jit(solution)/shard_map/ppermute | solution.py:235
  5.5 2.1 %dynamic-slice_bitcast_fusion.1 = (bf16[512,256]{1,0:T(8,128)(2,1)}, bf16[512,256]{1,0:T(8,128)(2,1)}, bf16[512,256]{1,0:T(8,128)(2,1)}) fusion(bf16[4,1024,256]{2,1,0:T(8,128)(2,1)} %bitcast.84, s32[]{:T(128)S(6)} %select_n.90, s32[]{:T(128)S(6)} %select_n.86, s32[]{:T(128)S(6)} %select_n.88, s32[]{:T(128)S(6)} %select_n.80), kind=kLoop, calls=%fused_computation.18 | loop fusion | bytes 1572880 | tf_op jit(solution)/shard_map/dynamic_slice | solution.py:290
  7.6 2.0 %collective-permute-start.1 = (bf16[512,256]{1,0:T(8,128)(2,1)}, bf16[512,256]{1,0:T(8,128)(2,1)}, u32[]{:S(2)}, u32[]{:S(2)}) collective-permute-start(bf16[512,256]{1,0:T(8,128)(2,1)} %get-tuple-element.137), channel_id=1, source_target_pairs={{0,16},{16,0},{1,17},{17,1},{2,18},{18,2},{3,19},{19,3},{4,20},{20... | collective-permute-start | bytes 786440 | tf_op jit(solution)/shard_map/ppermute | solution.py:235
  9.9 2.0 %collective-permute-start.7 = (f32[2176]{0:T(1024)S(1)}, f32[2176]{0:T(1024)S(1)}, u32[]{:S(2)}, u32[]{:S(2)}) collective-permute-start(f32[2176]{0:T(1024)S(1)} %constant_dynamic-update-slice_fusion), channel_id=1, source_target_pairs={{0,16},{16,0},{1,17},{17,1},{2,18},{18,2},{3,19},{19,3},{4,20},{20... | collective-permute-start | bytes 26120 | tf_op jit(solution)/shard_map/ppermute | solution.py:242
  12.9 1.8 %fusion = bf16[512,256]{1,0:T(8,128)(2,1)} fusion(bf16[512,256]{1,0:T(8,128)(2,1)S(1)} %collective-permute-done.3, bf16[1,1,4,1024,256]{4,3,2,1,0:T(8,128)(2,1)} %param.17, s32[]{:T(128)S(6)} %select_n.84, s32[]{:T(128)S(6)} %select_n.82), kind=kLoop, calls=%fused_computation.4 | loop fusion | flops 524288 | bytes 786440 | tf_op jit(solution)/shard_map/convert_element_type | solution.py:303
  14.6 4.0 %collective-permute-done.2 = bf16[512,256]{1,0:T(8,128)(2,1)} collective-permute-done((bf16[512,256]{1,0:T(8,128)(2,1)}, bf16[512,256]{1,0:T(8,128)(2,1)}, u32[]{:S(2)}, u32[]{:S(2)}) %collective-permute-start.2) | collective-permute-done | bytes 262176 | tf_op jit(solution)/shard_map/ppermute | solution.py:235
  18.6 1.8 %fusion.1 = bf16[512,256]{1,0:T(8,128)(2,1)} fusion(bf16[512,256]{1,0:T(8,128)(2,1)} %collective-permute-done.2, bf16[1,1,4,1024,256]{4,3,2,1,0:T(8,128)(2,1)} %param.17, s32[]{:T(128)S(6)} %select_n.90, s32[]{:T(128)S(6)} %select_n.82), kind=kLoop, calls=%fused_computation.6 | loop fusion | flops 524288 | bytes 786440 | tf_op jit(solution)/shard_map/convert_element_type | solution.py:303
  20.4 3.2 %collective-permute-start.5 = (bf16[512,256]{1,0:T(8,128)(2,1)}, bf16[512,256]{1,0:T(8,128)(2,1)S(1)}, u32[]{:S(2)}, u32[]{:S(2)}) collective-permute-start(bf16[512,256]{1,0:T(8,128)(2,1)} %fusion.1), channel_id=1, source_target_pairs={{0,8},{4,12},{8,0},{12,4},{1,9},{5,13},{9,1},{13,5},{2,10},{6,14},... | collective-permute-start | bytes 786440 | tf_op jit(solution)/shard_map/ppermute | solution.py:305
  24.6 1.6 %collective-permute-start.8 = (bf16[512,512]{1,0:T(8,128)(2,1)}, bf16[512,512]{1,0:T(8,128)(2,1)S(1)}, u32[]{:S(2)}, u32[]{:S(2)}) collective-permute-start(bf16[512,512]{1,0:T(8,128)(2,1)} %get-tuple-element.140), channel_id=1, source_target_pairs={{0,16},{16,0},{1,17},{17,1},{2,18},{18,2},{3,19},{19,3},{4,20},{20... | collective-permute-start | bytes 1572872 | tf_op jit(solution)/shard_map/ppermute | solution.py:235
  27.5 1.8 %fusion.2 = bf16[512,256]{1,0:T(8,128)(2,1)} fusion(bf16[512,256]{1,0:T(8,128)(2,1)} %collective-permute-done.1, bf16[1,1,4,1024,256]{4,3,2,1,0:T(8,128)(2,1)} %param.17, s32[]{:T(128)S(6)} %select_n.88, s32[]{:T(128)S(6)} %select_n.82), kind=kLoop, calls=%fused_computation.8 | loop fusion | flops 524288 | bytes 786440 | tf_op jit(solution)/shard_map/convert_element_type | solution.py:303
  30.0 4.2 %collective-permute-start.6 = (bf16[512,256]{1,0:T(8,128)(2,1)}, bf16[512,256]{1,0:T(8,128)(2,1)S(1)}, u32[]{:S(2)}, u32[]{:S(2)}) collective-permute-start(bf16[512,256]{1,0:T(8,128)(2,1)} %fusion), channel_id=1, source_target_pairs={{0,12},{4,8},{8,4},{12,0},{1,13},{5,9},{9,5},{13,1},{2,14},{6,10},... | collective-permute-start | bytes 786440 | tf_op jit(solution)/shard_map/ppermute | solution.py:305
  35.4 10.0 %collective-permute-done.4.refs_1_ = bf16[512,256]{1,0:T(8,128)(2,1)S(1)} collective-permute-done((bf16[512,256]{1,0:T(8,128)(2,1)}, bf16[512,256]{1,0:T(8,128)(2,1)S(1)}, u32[]{:S(2)}, u32[]{:S(2)}) %collective-permute-start.4) | collective-permute-done | bytes 262176 | tf_op jit(solution)/shard_map/ppermute | solution.py:305
  52.3 3.5 %select_convert_fusion = bf16[512,1024]{1,0:T(8,128)(2,1)} fusion(pred[]{:T(512)S(6)} %eq.11, f32[1,1,512,1024]{3,2,1,0:T(8,128)} %param.21, f32[1,1,512,1024]{3,2,1,0:T(8,128)} %param.20), kind=kLoop, calls=%fused_computation | loop fusion | flops 524288 | bytes 5242881 | tf_op jit(solution)/shard_map/convert_element_type | solution.py:341
  62.1 1.8 %collective-permute-start.13 = (f32[2,1024]{1,0:T(2,128)S(1)}, f32[2,1024]{1,0:T(2,128)S(1)}, u32[]{:S(2)}, u32[]{:S(2)}) collective-permute-start(f32[2,1024]{1,0:T(2,128)S(1)} %add.136), channel_id=1, source_target_pairs={{0,8},{4,12},{8,0},{12,4},{1,9},{5,13},{9,1},{13,5},{2,10},{6,14},... | collective-permute-start | bytes 24584 | tf_op jit(solution)/shard_map/ppermute | solution.py:242
  64.0 2.7 %collective-permute-done.13 = f32[2,1024]{1,0:T(2,128)S(1)} collective-permute-done((f32[2,1024]{1,0:T(2,128)S(1)}, f32[2,1024]{1,0:T(2,128)S(1)}, u32[]{:S(2)}, u32[]{:S(2)}) %collective-permute-start.13) | collective-permute-done | bytes 8224 | tf_op jit(solution)/shard_map/ppermute | solution.py:242
  66.7 5.5 %collective-permute-done.11.refs_1_ = bf16[512,1024]{1,0:T(8,128)(2,1)} collective-permute-done((bf16[512,1024]{1,0:T(8,128)(2,1)S(1)}, bf16[512,1024]{1,0:T(8,128)(2,1)}, u32[]{:S(2)}, u32[]{:S(2)}) %collective-permute-start.11) | collective-permute-done | bytes 1048608 | tf_op jit(solution)/shard_map/ppermute | solution.py:235
  73.6 21.1 %collective-permute-done.10.refs_1_ = bf16[512,1024]{1,0:T(8,128)(2,1)} collective-permute-done((bf16[512,1024]{1,0:T(8,128)(2,1)S(1)}, bf16[512,1024]{1,0:T(8,128)(2,1)}, u32[]{:S(2)}, u32[]{:S(2)}) %collective-permute-start.10) | collective-permute-done | bytes 1048608 | tf_op jit(solution)/shard_map/ppermute | solution.py:235
  96.8 7.6 %shard_map.230 = (f32[512,1024]{1,0:T(8,128)}, f32[512,1024]{1,0:T(8,128)}, bf16[512,1024]{1,0:T(8,128)(2,1)S(1)}) custom-call(s32[2]{0:T(128)S(1)} %pad_add_fusion.offsets, bf16[512,1024]{1,0:T(8,128)(2,1)S(1)} %shard_map.228.refs_0_, bf16[512,1024]{1,0:T(8,128)(2,1)} %collective-permute-done.10.refs_1_, bf16[512,512]{1,0:T(8,128)(2,1)S(1)} %copy-done.6, ...), custom_call_target="tpu_custom_call" | custom-call | tf_op jit(solution)/shard_map/pallas_call | solution.py:50
  109.7 7.3 %shard_map.231 = (f32[512,1024]{1,0:T(8,128)}, f32[512,1024]{1,0:T(8,128)}, bf16[512,1024]{1,0:T(8,128)(2,1)S(1)}, f32[512,1024]{1,0:T(8,128)S(1)}) custom-call(s32[3]{0:T(128)S(1)} %pad_add_fusion.3.offsets.scalars, bf16[512,1024]{1,0:T(8,128)(2,1)S(1)} %shard_map.228.refs_0_, bf16[512,1024]{1,0:T(8,128)(2,1)} %collective-permute-done.10.refs_1_, ...), custom_call_target="tpu_custom_call" | custom-call | tf_op jit(solution)/shard_map/pallas_call | solution.py:50
  117.2 18.7 %shard_map.233 = (f32[512,1024]{1,0:T(8,128)S(1)}, bf16[512,1024]{1,0:T(8,128)(2,1)S(1)}) custom-call(s32[4]{0:T(128)S(1)} %pad_add_fusion.2.offsets, bf16[512,1024]{1,0:T(8,128)(2,1)S(1)} %get-tuple-element.88.refs_0_, bf16[512,1024]{1,0:T(8,128)(2,1)} %collective-permute-done.17.refs_1_, bf16[1024,1024]{1,0:T(8,128)(2,1)S(1)} %shard_map.232.refs_2_, ...), custom_call_target="tpu_custom_call" | custom-call | tf_op jit(solution)/shard_map/pallas_call | solution.py:50
  142.0 4.3 %shard_map.234 = f32[512,1024]{1,0:T(8,128)} custom-call(s32[2]{0:T(128)S(1)} %pad_add_fusion.offsets, bf16[512,1024]{1,0:T(8,128)(2,1)S(1)} %get-tuple-element.86.refs_0_, bf16[512,1024]{1,0:T(8,128)(2,1)S(1)} %collective-permute-done.16.refs_1_, bf16[1024,1024]{1,0:T(8,128)(2,1)S(1)} %shard_map.229.refs_4_.refs_2_, ...), custom_call_target="tpu_custom_call" | custom-call | tf_op jit(solution)/shard_map/pallas_call | solution.py:50
  146.4 11.6 %collective-permute-done.18.part = bf16[416,1024]{1,0:T(8,128)(2,1)} collective-permute-done((bf16[416,1024]{1,0:T(8,128)(2,1)S(1)}, bf16[416,1024]{1,0:T(8,128)(2,1)}, u32[]{:S(2)}, u32[]{:S(2)}) %collective-permute-start.18) | collective-permute-done | bytes 852000 | tf_op jit(solution)/shard_map/ppermute | solution.py:235
  158.0 2.5 %shard_map.235 = (f32[512,1024]{1,0:T(8,128)}, f32[512,1024]{1,0:T(8,128)}) custom-call(s32[1]{0:T(128)} %bitcast.20.side, bf16[416,1024]{1,0:T(8,128)(2,1)} %collective-permute-done.18.part, f32[512,1024]{1,0:T(8,128)} %copy.50.left_in, f32[512,1024]{1,0:T(8,128)} %copy.51.right_in), custom_call_target="tpu_custom_call", output_to_operand_aliasing={{0}: (2, {}), {1}: (3, {})} | custom-call | tf_op jit(solution)/shard_map/pallas_call | solution.py:91
  (102 shorter events, 34.9 us)
Async XLA Ops:
  0.7 9.2 %copy-start.14 = (f32[1,1,1,2,1024]{4,3,2,1,0:T(2,128)S(1)}, f32[1,1,1,2,1024]{4,3,2,1,0:T(2,128)}, u32[]{:S(2)}) copy-start(f32[1,1,1,2,1024]{4,3,2,1,0:T(2,128)} %param.24) | copy-start | bytes 24580
  0.7 11.3 %copy-start.11 = (f32[1,1,512,1024]{3,2,1,0:T(8,128)S(1)}, f32[1,1,512,1024]{3,2,1,0:T(8,128)}, u32[]{:S(2)}) copy-start(f32[1,1,512,1024]{3,2,1,0:T(8,128)} %param.22) | copy-start | bytes 6291460
  2.6 10.3 %collective-permute-start.3 = (bf16[512,256]{1,0:T(8,128)(2,1)}, bf16[512,256]{1,0:T(8,128)(2,1)S(1)}, u32[]{:S(2)}, u32[]{:S(2)}) collective-permute-start(bf16[512,256]{1,0:T(8,128)(2,1)} %dynamic-slice_bitcast_fusion.4), channel_id=1, source_target_pairs={{0,16},{16,0},{1,17},{17,1},{2,18},{18,2},{3,19},{19,3},{4,20},{20... | collective-permute-start | bytes 786440 | tf_op jit(solution)/shard_map/ppermute | solution.py:235
  7.6 11.0 %collective-permute-start.2 = (bf16[512,256]{1,0:T(8,128)(2,1)}, bf16[512,256]{1,0:T(8,128)(2,1)}, u32[]{:S(2)}, u32[]{:S(2)}) collective-permute-start(bf16[512,256]{1,0:T(8,128)(2,1)} %get-tuple-element.136), channel_id=1, source_target_pairs={{0,16},{16,0},{1,17},{17,1},{2,18},{18,2},{3,19},{19,3},{4,20},{20... | collective-permute-start | bytes 786440 | tf_op jit(solution)/shard_map/ppermute | solution.py:235
  7.6 17.0 %collective-permute-start.1 = (bf16[512,256]{1,0:T(8,128)(2,1)}, bf16[512,256]{1,0:T(8,128)(2,1)}, u32[]{:S(2)}, u32[]{:S(2)}) collective-permute-start(bf16[512,256]{1,0:T(8,128)(2,1)} %get-tuple-element.137), channel_id=1, source_target_pairs={{0,16},{16,0},{1,17},{17,1},{2,18},{18,2},{3,19},{19,3},{4,20},{20... | collective-permute-start | bytes 786440 | tf_op jit(solution)/shard_map/ppermute | solution.py:235
  9.6 24.5 %collective-permute-start = (bf16[512,256]{1,0:T(8,128)(2,1)}, bf16[512,256]{1,0:T(8,128)(2,1)}, u32[]{:S(2)}, u32[]{:S(2)}) collective-permute-start(bf16[512,256]{1,0:T(8,128)(2,1)} %get-tuple-element.138), channel_id=1, source_target_pairs={{0,16},{16,0},{1,17},{17,1},{2,18},{18,2},{3,19},{19,3},{4,20},{20... | collective-permute-start | bytes 786440 | tf_op jit(solution)/shard_map/ppermute | solution.py:235
  9.9 20.1 %collective-permute-start.7 = (f32[2176]{0:T(1024)S(1)}, f32[2176]{0:T(1024)S(1)}, u32[]{:S(2)}, u32[]{:S(2)}) collective-permute-start(f32[2176]{0:T(1024)S(1)} %constant_dynamic-update-slice_fusion), channel_id=1, source_target_pairs={{0,16},{16,0},{1,17},{17,1},{2,18},{18,2},{3,19},{19,3},{4,20},{20... | collective-permute-start | bytes 26120 | tf_op jit(solution)/shard_map/ppermute | solution.py:242
  20.4 27.1 %collective-permute-start.5 = (bf16[512,256]{1,0:T(8,128)(2,1)}, bf16[512,256]{1,0:T(8,128)(2,1)S(1)}, u32[]{:S(2)}, u32[]{:S(2)}) collective-permute-start(bf16[512,256]{1,0:T(8,128)(2,1)} %fusion.1), channel_id=1, source_target_pairs={{0,8},{4,12},{8,0},{12,4},{1,9},{5,13},{9,1},{13,5},{2,10},{6,14},... | collective-permute-start | bytes 786440 | tf_op jit(solution)/shard_map/ppermute | solution.py:305
  24.6 23.6 %collective-permute-start.8 = (bf16[512,512]{1,0:T(8,128)(2,1)}, bf16[512,512]{1,0:T(8,128)(2,1)S(1)}, u32[]{:S(2)}, u32[]{:S(2)}) collective-permute-start(bf16[512,512]{1,0:T(8,128)(2,1)} %get-tuple-element.140), channel_id=1, source_target_pairs={{0,16},{16,0},{1,17},{17,1},{2,18},{18,2},{3,19},{19,3},{4,20},{20... | collective-permute-start | bytes 1572872 | tf_op jit(solution)/shard_map/ppermute | solution.py:235
  26.3 22.8 %collective-permute-start.9 = (bf16[512,512]{1,0:T(8,128)(2,1)}, bf16[512,512]{1,0:T(8,128)(2,1)}, u32[]{:S(2)}, u32[]{:S(2)}) collective-permute-start(bf16[512,512]{1,0:T(8,128)(2,1)} %get-tuple-element.139), channel_id=1, source_target_pairs={{16,0},{1,17},{18,2},{3,19},{20,4},{5,21},{22,6},{7,23},{24,8},{9,... | collective-permute-start | bytes 1572872 | tf_op jit(solution)/shard_map/ppermute | solution.py:311
  30.0 17.5 %collective-permute-start.6 = (bf16[512,256]{1,0:T(8,128)(2,1)}, bf16[512,256]{1,0:T(8,128)(2,1)S(1)}, u32[]{:S(2)}, u32[]{:S(2)}) collective-permute-start(bf16[512,256]{1,0:T(8,128)(2,1)} %fusion), channel_id=1, source_target_pairs={{0,12},{4,8},{8,4},{12,0},{1,13},{5,9},{9,5},{13,1},{2,14},{6,10},... | collective-permute-start | bytes 786440 | tf_op jit(solution)/shard_map/ppermute | solution.py:305
  34.1 11.2 %collective-permute-start.4 = (bf16[512,256]{1,0:T(8,128)(2,1)}, bf16[512,256]{1,0:T(8,128)(2,1)S(1)}, u32[]{:S(2)}, u32[]{:S(2)}) collective-permute-start(bf16[512,256]{1,0:T(8,128)(2,1)} %fusion.2), channel_id=1, source_target_pairs={{0,4},{4,0},{8,12},{12,8},{1,5},{5,1},{9,13},{13,9},{2,6},{6,2},{1... | collective-permute-start | bytes 786440 | tf_op jit(solution)/shard_map/ppermute | solution.py:305
  46.1 26.2 %collective-permute-start.11 = (bf16[512,1024]{1,0:T(8,128)(2,1)S(1)}, bf16[512,1024]{1,0:T(8,128)(2,1)}, u32[]{:S(2)}, u32[]{:S(2)}) collective-permute-start(bf16[512,1024]{1,0:T(8,128)(2,1)S(1)} %convert_bitcast_fusion.refs_0_), channel_id=1, source_target_pairs={{0,16},{16,0},{1,17},{17,1},{2,18},{18,2},{3,19},{19,3},{4,20},{20... | collective-permute-start | bytes 3145736 | tf_op jit(solution)/shard_map/ppermute | solution.py:235
  51.6 43.1 %collective-permute-start.10 = (bf16[512,1024]{1,0:T(8,128)(2,1)S(1)}, bf16[512,1024]{1,0:T(8,128)(2,1)}, u32[]{:S(2)}, u32[]{:S(2)}) collective-permute-start(bf16[512,1024]{1,0:T(8,128)(2,1)S(1)} %shard_map.228.refs_0_), channel_id=1, source_target_pairs={{0,16},{16,0},{1,17},{17,1},{2,18},{18,2},{3,19},{19,3},{4,20},{20... | collective-permute-start | bytes 3145736 | tf_op jit(solution)/shard_map/ppermute | solution.py:235
  55.8 61.4 %collective-permute-start.17 = (bf16[512,1024]{1,0:T(8,128)(2,1)}, bf16[512,1024]{1,0:T(8,128)(2,1)}, u32[]{:S(2)}, u32[]{:S(2)}) collective-permute-start(bf16[512,1024]{1,0:T(8,128)(2,1)} %select_convert_fusion), channel_id=1, source_target_pairs={{0,16},{16,0},{1,17},{17,1},{2,18},{18,2},{3,19},{19,3},{4,20},{20... | collective-permute-start | bytes 3145736 | tf_op jit(solution)/shard_map/ppermute | solution.py:235
  58.4 1.2 collective-permute-start.14
  58.4 3.7 %collective-permute-start.12 = (f32[2,1024]{1,0:T(2,128)S(1)}, f32[2,1024]{1,0:T(2,128)S(1)}, u32[]{:S(2)}, u32[]{:S(2)}) collective-permute-start(f32[2,1024]{1,0:T(2,128)S(1)} %reshape.124), channel_id=1, source_target_pairs={{0,4},{4,0},{8,12},{12,8},{1,5},{5,1},{9,13},{13,9},{2,6},{6,2},{1... | collective-permute-start | bytes 24584 | tf_op jit(solution)/shard_map/ppermute | solution.py:242
  59.6 4.4 %collective-permute-start.15 = (f32[32,4]{0,1:T(4,128)S(1)}, f32[32,4]{0,1:T(4,128)S(1)}, u32[]{:S(2)}, u32[]{:S(2)}) collective-permute-start(f32[32,4]{0,1:T(4,128)S(1)} %add.138), channel_id=1, source_target_pairs={{0,2},{1,3},{2,0},{3,1},{4,6},{5,7},{6,4},{7,5},{8,10},{9,11},{10,... | collective-permute-start | bytes 1544 | tf_op jit(solution)/shard_map/ppermute | solution.py:242
  62.1 4.5 %collective-permute-start.13 = (f32[2,1024]{1,0:T(2,128)S(1)}, f32[2,1024]{1,0:T(2,128)S(1)}, u32[]{:S(2)}, u32[]{:S(2)}) collective-permute-start(f32[2,1024]{1,0:T(2,128)S(1)} %add.136), channel_id=1, source_target_pairs={{0,8},{4,12},{8,0},{12,4},{1,9},{5,13},{9,1},{13,5},{2,10},{6,14},... | collective-permute-start | bytes 24584 | tf_op jit(solution)/shard_map/ppermute | solution.py:242
  66.7 28.0 %copy-start.2 = (f32[1,1,512,1024]{3,2,1,0:T(8,128)S(1)}, f32[1,1,512,1024]{3,2,1,0:T(8,128)}, u32[]{:S(2)}) copy-start(f32[1,1,512,1024]{3,2,1,0:T(8,128)} %param.18) | copy-start | bytes 6291460
  66.7 28.0 %copy-start.3 = (f32[1,1,512,1024]{3,2,1,0:T(8,128)S(1)}, f32[1,1,512,1024]{3,2,1,0:T(8,128)}, u32[]{:S(2)}) copy-start(f32[1,1,512,1024]{3,2,1,0:T(8,128)} %param.19) | copy-start | bytes 6291460
  104.4 37.6 %collective-permute-start.16 = (bf16[512,1024]{1,0:T(8,128)(2,1)S(1)}, bf16[512,1024]{1,0:T(8,128)(2,1)S(1)}, u32[]{:S(2)}, u32[]{:S(2)}) collective-permute-start(bf16[512,1024]{1,0:T(8,128)(2,1)S(1)} %get-tuple-element.86.refs_0_), channel_id=1, source_target_pairs={{0,16},{16,0},{1,17},{17,1},{2,18},{18,2},{3,19},{19,3},{4,20},{20... | collective-permute-start | bytes 3145736 | tf_op jit(solution)/shard_map/ppermute | solution.py:235
  135.9 22.1 %collective-permute-start.18 = (bf16[416,1024]{1,0:T(8,128)(2,1)S(1)}, bf16[416,1024]{1,0:T(8,128)(2,1)}, u32[]{:S(2)}, u32[]{:S(2)}) collective-permute-start(bf16[416,1024]{1,0:T(8,128)(2,1)S(1)} %slice.59), channel_id=1, source_target_pairs={{0,16},{16,0},{1,17},{17,1},{2,18},{18,2},{3,19},{19,3},{4,20},{20... | collective-permute-start | bytes 2555912 | tf_op jit(solution)/shard_map/ppermute | solution.py:235
  140.1 20.7 %collective-permute-start.19 = (bf16[96,1024]{1,0:T(8,128)(2,1)S(1)}, bf16[96,1024]{1,0:T(8,128)(2,1)S(1)}, u32[]{:S(2)}, u32[]{:S(2)}) collective-permute-start(bf16[96,1024]{1,0:T(8,128)(2,1)S(1)} %slice.61), channel_id=1, source_target_pairs={{0,16},{16,0},{1,17},{17,1},{2,18},{18,2},{3,19},{19,3},{4,20},{20... | collective-permute-start | bytes 589832 | tf_op jit(solution)/shard_map/ppermute | solution.py:235
  (16 other events, 36.2 us)
